TPU v7x, 512 devices: a whole 4x4x16 slice. The times are simulated.
512 devices in a mesh: prow: 32 (over y, x, z_hi), pcol: 16 (over z_lo, core).
Axes of the slice: x: 4, y: 4, z: 16 (z_hi: 2, z_lo: 8; z = z_hi * 8 + z_lo), core: 2. Of those that a mesh axis runs over, the one named last changes fastest.
Arguments:
- right_side: float32 [2, 1024, 2048], P(None, 'prow', 'pcol'), may hold values from -6 to 6
- diag_inverse: float32 [2, 1024, 1024], P(None, 'prow'), as said below
- coupling: float32 [1024, 1024], P('prow'), may hold values from -0.1875 to 0.1875
- panel: float32 [2, 1024, 8192], P(None, 'prow', 'pcol'), may hold values from -0.0625 to 0.0625
- solved: float32 [8192, 2048], P('pcol'), may hold values from -6 to 6
Outputs:
- solution: float32 [2, 1024, 2048], P(None, 'prow', 'pcol')
Inputs may be any that keep to these rules, and one draw needn't show every extreme that they name: `diag_inverse`: each of the 2 blocks is lower triangular, its diagonal entries between 0.6 and 1.4.
All inputs are finite; a program needn't handle non-finite values.
Results may differ from a plain program's by a relative error of at most 0.000062.
Values sent between devices are 32-bit elements; how exact they have to be, the bound alone decides.
No kernel may reach another device: no remote copies, remote signals or barrier semaphores. Data moves between devices by JAX's collectives and lax.ppermute only.
A program may use at most 64 MiB of HBM per device.

v0:
```python
import jax
import jax.numpy as jnp
from jax import lax
from jax.sharding import PartitionSpec as P


def multiplier_operand(factor_matrix, piece):
    return jnp.dot(
        factor_matrix, piece, precision=lax.Precision.HIGHEST, preferred_element_type=jnp.float32
    )


def on_device(right_side, diag_inverse, coupling, panel, solved):
    summand_list = jnp.einsum("ftq,qg->ftg", panel, solved, precision=lax.Precision.HIGHEST)
    sums = lax.psum_scatter(summand_list, "pcol", scatter_dimension=2, tiled=True)
    first_part = sums[0]
    second_part = sums[1]
    first_res = right_side[0] - first_part
    first_sol = multiplier_operand(
        diag_inverse[0], lax.all_gather(first_res, "prow", axis=0, tiled=True)
    )
    cross = multiplier_operand(coupling, lax.all_gather(first_sol, "prow", axis=0, tiled=True))
    second_res = right_side[1] - second_part - cross
    second_solution = multiplier_operand(
        diag_inverse[1], lax.all_gather(second_res, "prow", axis=0, tiled=True)
    )
    return jnp.stack([first_sol, second_solution])


def solution(mesh):
    return jax.shard_map(
        on_device,
        mesh=mesh,
        in_specs=(
            P(None, "prow", "pcol"),
            P(None, "prow", None),
            P("prow", None),
            P(None, "prow", "pcol"),
            P("pcol", None),
        ),
        out_specs=P(None, "prow", "pcol"),
        check_vma=False,
    )
```

profile of v0, /device:TPU:2, one launch (start us, length us, event | category | flops | bytes accessed | tf_op | source)
XLA Modules:
  0.0 600.6 jit_solution(5436476501328035409)
XLA Ops:
  6.5 0.0 copy-start
  6.5 0.0 copy-start.3
  6.5 0.0 copy-start.1
  6.5 0.0 copy-start.2
  6.5 0.0 reduce-scatter.2.cloned.1.call-start
  6.6 0.9 copy-done
  7.4 5.6 fusion
  13.1 0.0 reduce-scatter.2.cloned.1.call-update
  13.1 109.8 %reduce-scatter.2.cloned.1.call-done = f32[2,32,128]{2,1,0:T(8,128)} async-done(((f32[2,32,2048]{2,1,0:T(8,128)}), f32[2,32,128]{2,1,0:T(8,128)}) %reduce-scatter.2.cloned.1.call-update) | async-done | bytes 32784 | tf_op jit(solution)/shard_map/reduce_scatter | solution.py:15
  122.9 0.0 copy-done.3
  122.9 0.7 slice_subtract_fusion.1
  123.6 154.0 %all-gather = f32[1,1024,128]{2,1,0:T(8,128)S(1)} all-gather(f32[1,32,128]{2,1,0:T(8,128)S(1)} %slice_subtract_fusion.1), channel_id=2, replica_groups=mesh['prow'=32,'pcol'=16] {'prow'}, dimensions={1}, use_global_device_ids=true | all-gather | bytes 540672 | tf_op jit(solution)/shard_map/all_gather | solution.py:20
  277.6 0.0 copy-done.1
  277.6 0.4 fusion.3
  278.0 154.1 %all_gather.10 = f32[1024,128]{1,0:T(8,128)S(1)} all-gather(f32[32,128]{1,0:T(8,128)S(1)} %bitcast.31), channel_id=1, replica_groups=mesh['prow'=32,'pcol'=16] {'prow'}, dimensions={0}, use_global_device_ids=true | all-gather | bytes 540672 | tf_op jit(solution)/shard_map/all_gather | solution.py:22
  432.1 0.0 copy-done.2
  432.1 1.1 fusion.2
  433.2 159.4 %all_gather.11 = f32[1024,128]{1,0:T(8,128)S(1)} all-gather(f32[32,128]{1,0:T(8,128)S(1)} %fusion.2), channel_id=1, replica_groups=mesh['prow'=32,'pcol'=16] {'prow'}, dimensions={0}, use_global_device_ids=true | all-gather | bytes 540672 | tf_op jit(solution)/shard_map/all_gather | solution.py:25
  592.7 0.4 convolution_bitcast_fusion
  593.1 0.6 pad_maximum_fusion
Async XLA Ops:
  6.5 0.9 copy-start
  6.5 116.4 %copy-start.3 = (f32[2,32,128]{2,1,0:T(8,128)S(1)}, f32[2,32,128]{2,1,0:T(8,128)}, u32[]{:S(2)}) copy-start(f32[2,32,128]{2,1,0:T(8,128)} %param.5) | copy-start | bytes 98308
  6.5 271.1 %copy-start.1 = (f32[2,32,1024]{2,1,0:T(8,128)S(1)}, f32[2,32,1024]{2,1,0:T(8,128)}, u32[]{:S(2)}) copy-start(f32[2,32,1024]{2,1,0:T(8,128)} %param.6) | copy-start | bytes 786436
  6.5 425.6 %copy-start.2 = (f32[32,1024]{1,0:T(8,128)S(1)}, f32[32,1024]{1,0:T(8,128)}, u32[]{:S(2)}) copy-start(f32[32,1024]{1,0:T(8,128)} %param.7) | copy-start | bytes 393220
  6.5 116.3 %reduce-scatter.2.cloned.1.call-start = ((), (), s32[]{:S(2)}) async-start(), calls=%async_computation.1 | async-start | bytes 557056 | tf_op jit(solution)/shard_map/reduce_scatter | solution.py:15
Sparse Core Ops, SparseCore 0:
  13.2 109.6 reduce-scatter.1
where the time goes:
time: 601 us
  blocking collectives  468 us (78%)
  waiting for transfers between devices  110 us (18%)
  between operations  13.4 us (2%)
  matrix products  7.58 us (1%)
    all_gather x1, blocking collectives, on_device(): lax.all_gather(second_res, 'prow', axis=0, tiled=True)  159 us
    all_gather x1, blocking collectives, on_device(): lax.all_gather(first_sol, 'prow', axis=0, tiled=True)  154 us
    all_gather x1, blocking collectives, on_device(): lax.all_gather(first_res, 'prow', axis=0, tiled=True)  154 us
    reduce_scatter x1, waiting for transfers between devices, on_device(): lax.psum_scatter(summand_list, 'pcol', scatter_dimension=2, tiled=True)  110 us
  transfers between devices with their start and end apart: 1, of which 1 were waited for; matrix products, arithmetic and copies ran while one was open for 0% of the time, Pallas kernels for 0%

commit v1 on v0

v1 whole, which is shorter than its diff:
```python
import jax
import jax.numpy as jnp
from jax import lax
from jax.sharding import Mesh, PartitionSpec as P

ROWS = ("y", "x", "zh")
COLS = ("zl", "core")


def mul(a, b):
    return jnp.dot(a, b, precision=lax.Precision.HIGH, preferred_element_type=jnp.float32)


def gather_plane(block):
    copies = jnp.broadcast_to(block[None], (16,) + block.shape)
    got = lax.all_to_all(copies, ("y", "x"), 0, 0, tiled=True)
    return got.reshape(16 * block.shape[0], block.shape[1])


def reduce_line(blocks):
    copies = jnp.broadcast_to(blocks[None], (2,) + blocks.shape).reshape(16, 32, 128)
    got = lax.all_to_all(copies, ("zh", "zl"), 0, 0, tiled=True)
    return got.reshape(2, 8, 32, 128).sum(1).reshape(64, 128)


def on_device(right_side, diag_inverse, coupling, panel, solved):
    zh, zl, core = (lax.axis_index(a) for a in ("zh", "zl", "core"))

    factors = jnp.stack([diag_inverse[0], coupling])
    slots = jnp.where((jnp.arange(2) == 1 - zh)[:, None, None, None], factors[None], 0.0)
    other = lax.psum_scatter(slots, "zh", scatter_dimension=0, tiled=True)[0]

    total = mul(panel.reshape(64, 512), solved).reshape(64, 8, 2, 128)
    send = lax.dynamic_index_in_dim(total, 1 - core, 2, keepdims=False)
    keep = lax.dynamic_index_in_dim(total, core, 2, keepdims=False)
    total = keep + lax.ppermute(send, "core", [(0, 1), (1, 0)])
    total = total.reshape(2, 32, 8, 128).transpose(0, 2, 1, 3)
    mine = (jnp.arange(8) == zl)[None, :, None, None]
    reduced = jnp.where(mine, right_side[:, None], 0.0) - total

    first_res = reduce_line(reduced[0])
    second_part = reduce_line(reduced[1])

    def both(index, x):
        a, b = mul(factors[index], x), mul(other[index], x)
        return jnp.where(zh == 0, jnp.concatenate([a, b]), jnp.concatenate([b, a])), a

    first_sol, first_mine = both(0, gather_plane(first_res))
    cross, _ = both(1, gather_plane(first_sol))
    second_res = second_part - cross
    second_mine = mul(diag_inverse[1], gather_plane(second_res))
    return jnp.stack([first_mine, second_mine])


def solution(mesh):
    fine = Mesh(mesh.devices.reshape(4, 4, 2, 8, 2), ROWS + COLS)
    return jax.shard_map(
        on_device,
        mesh=fine,
        in_specs=(
            P(None, ROWS, COLS),
            P(None, ROWS, None),
            P(ROWS, None),
            P(None, ROWS, COLS),
            P(COLS, None),
        ),
        out_specs=P(None, ROWS, COLS),
        check_vma=False,
    )
```

time: 601 us -> 165 us (0.27)
  the two profiles are of different devices: /device:TPU:2 before, /device:TPU:32 now
where the time goes in v1:
time: 165 us; the launch traced here: 164 us
  waiting for transfers between devices  80.1 us (49%)
  starting transfers between devices  39 us (24%)
  blocking collectives  13.9 us (8%)
  between operations  13.6 us (8%)
  local copies, waits for them, and re-layouts  8.64 us (5%)
  matrix products  7.32 us (4%)
  other arithmetic  1.73 us (1%)
    reduce_scatter x1, waiting for transfers between devices, on_device(): other = lax.psum_scatter(slots, 'zh', scatter_dimension=0, tiled=True)[0]  38.6 us
    all_to_all x2, starting transfers between devices, reduce_line(): got = lax.all_to_all(copies, ('zh', 'zl'), 0, 0, tiled=True)  22 us
    all_to_all x2, waiting for transfers between devices, gather_plane(): got = lax.all_to_all(copies, ('y', 'x'), 0, 0, tiled=True)  21.6 us
    all_to_all x2, waiting for transfers between devices, reduce_line(): got = lax.all_to_all(copies, ('zh', 'zl'), 0, 0, tiled=True)  18.3 us
    all_to_all x2, starting transfers between devices, gather_plane(): got = lax.all_to_all(copies, ('y', 'x'), 0, 0, tiled=True)  14.9 us
    all_to_all x1, blocking collectives, gather_plane(): got = lax.all_to_all(copies, ('y', 'x'), 0, 0, tiled=True)  13.9 us
    dot_general x6, matrix products, mul(): jnp.dot(a, b, precision=lax.Precision.HIGH, preferred_element_type=jnp.fl...  7.32 us
    dot_general x1, local copies, waits for them, and re-layouts, mul(): jnp.dot(a, b, precision=lax.Precision.HIGH, preferred_element_type=jnp.fl...  5.39 us
  transfers between devices with their start and end apart: 6, of which 5 were waited for; matrix products, arithmetic and copies ran while one was open for 2% of the time, Pallas kernels for 0%

profile of v1, /device:TPU:32, one launch (start us, length us, event | category | flops | bytes accessed | tf_op | source)
XLA Modules:
  0.0 164.2 jit_solution(1495240620087095024)
XLA Ops:
  6.5 0.0 copy-start
  6.5 5.4 %copy.9 = f32[2048,512]{1,0:T(8,128)} copy(f32[2048,512]{0,1:T(8,128)} %bitcast.66) | data formatting | bytes 8388608 | tf_op jit(solution)/shard_map/dot_general | solution.py:11
  11.9 0.0 copy-done
  11.9 0.0 copy-start.2
  12.0 4.3 %fusion.8 = f32[64,8,2,128]{3,0,2,1:T(8,128)S(1)} fusion(f32[64,512,1,1]{1,0,3,2:T(8,128)S(1)} %bitcast.60, f32[8,2,128,512]{3,2,1,0:T(8,128)} %bitcast.61), kind=kOutput, calls=%fused_computation.26 | convolution fusion | flops 402653184 | bytes 4849664 | tf_op jit(solution)/shard_map/dot_general | solution.py:11
  16.3 2.1 %collective-permute-start = (f32[64,8,128]{2,0,1:T(8,128)S(1)}, f32[64,8,128]{2,0,1:T(8,128)S(1)}, u32[]{:S(2)}, u32[]{:S(2)}) collective-permute-start(f32[64,8,128]{2,0,1:T(8,128)S(1)} %dynamic-slice_bitcast_fusion), channel_id=1, source_target_pairs={{0,1},{1,0},{2,3},{3,2},{4,5},{5,4},{6,7},{7,6},{8,9},{9,8},{10,11... | collective-permute-start | bytes 786440 | tf_op jit(solution)/shard_map/ppermute | solution.py:36
  18.3 1.5 collective-permute-done
  19.9 0.0 copy-done.3
  19.9 0.1 select_subtract_fusion
  20.0 0.7 broadcast_in_dim.81
  20.7 15.2 %all-to-all-start = ((f32[16,32,128]{2,1,0:T(8,128)}), f32[16,32,128]{2,1,0:T(8,128)S(1)}, u32[]{:S(2)}, u32[]{:S(2)}) async-start(f32[16,32,128]{2,1,0:T(8,128)} %bitcast.10), calls=%async_computation | async-start | bytes 524288 | tf_op jit(solution)/shard_map/all_to_all | solution.py:22
  36.0 18.3 %all-to-all-done = f32[16,32,128]{2,1,0:T(8,128)S(1)} async-done(((f32[16,32,128]{2,1,0:T(8,128)}), f32[16,32,128]{2,1,0:T(8,128)S(1)}, u32[]{:S(2)}, u32[]{:S(2)}) %all-to-all-start) | async-done | bytes 262176 | tf_op jit(solution)/shard_map/all_to_all | solution.py:22
  54.3 0.8 broadcast_in_dim.83
  55.1 7.0 %all-to-all-start.1 = ((f32[16,64,128]{2,1,0:T(8,128)}), f32[16,64,128]{2,1,0:T(8,128)S(1)}, u32[]{:S(2)}, u32[]{:S(2)}) async-start(f32[16,64,128]{2,1,0:T(8,128)} %broadcast_in_dim.83), calls=%async_computation.1 | async-start | bytes 1048576 | tf_op jit(solution)/shard_map/all_to_all | solution.py:16
  62.2 0.0 reduce-scatter.2.cloned.1.call-start
  62.2 0.9 broadcast_select_fusion
  63.1 0.0 reduce-scatter.2.cloned.1.call-update
  63.2 9.9 %all-to-all-done.1 = f32[16,64,128]{2,1,0:T(8,128)S(1)} async-done(((f32[16,64,128]{2,1,0:T(8,128)}), f32[16,64,128]{2,1,0:T(8,128)S(1)}, u32[]{:S(2)}, u32[]{:S(2)}) %all-to-all-start.1) | async-done | bytes 524320 | tf_op jit(solution)/shard_map/all_to_all | solution.py:16
  73.1 0.7 broadcast_in_dim.85
  73.8 6.8 %all-to-all-start.2 = ((f32[16,32,128]{2,1,0:T(8,128)}), f32[16,32,128]{2,1,0:T(8,128)S(1)}, u32[]{:S(2)}, u32[]{:S(2)}) async-start(f32[16,32,128]{2,1,0:T(8,128)} %bitcast.18), calls=%async_computation.2 | async-start | bytes 524288 | tf_op jit(solution)/shard_map/all_to_all | solution.py:22
  80.6 0.3 fusion.3
  80.9 38.6 %reduce-scatter.2.cloned.1.call-done = f32[1,2,32,1024]{3,2,1,0:T(8,128)} async-done(((f32[2,2,32,1024]{3,2,1,0:T(8,128)}), f32[1,2,32,1024]{3,2,1,0:T(8,128)}) %reduce-scatter.2.cloned.1.call-update) | async-done | bytes 262160 | tf_op jit(solution)/shard_map/reduce_scatter | solution.py:31
  119.5 1.1 fusion.1
  120.7 0.0 all-to-all-done.2
  120.7 0.8 broadcast_in_dim.89
  121.5 7.8 %all-to-all-start.3 = ((f32[16,64,128]{2,1,0:T(8,128)}), f32[16,64,128]{2,1,0:T(8,128)S(1)}, u32[]{:S(2)}, u32[]{:S(2)}) async-start(f32[16,64,128]{2,1,0:T(8,128)} %broadcast_in_dim.89), calls=%async_computation.4 | async-start | bytes 1048576 | tf_op jit(solution)/shard_map/all_to_all | solution.py:16
  129.4 11.7 %all-to-all-done.3 = f32[16,64,128]{2,1,0:T(8,128)S(1)} async-done(((f32[16,64,128]{2,1,0:T(8,128)}), f32[16,64,128]{2,1,0:T(8,128)S(1)}, u32[]{:S(2)}, u32[]{:S(2)}) %all-to-all-start.3) | async-done | bytes 524320 | tf_op jit(solution)/shard_map/all_to_all | solution.py:16
  141.1 0.3 convolution_bitcast_fusion.1
  141.4 1.1 fusion
  142.6 13.9 %all_to_all.25 = f32[16,64,128]{2,1,0:T(8,128)S(1)} all-to-all(f32[16,64,128]{2,1,0:T(8,128)S(1)} %broadcast_in_dim.90), channel_id=1, replica_groups=mesh['y'=4,'x'=4,'zh'=2,'zl'=8,'core'=2] {'y','x'}, dimensions={0} | all-to-all | bytes 1048576 | tf_op jit(solution)/shard_map/all_to_all | solution.py:16
  156.5 0.3 convolution_bitcast_fusion
  156.8 0.6 pad_maximum_fusion.1
  (17 shorter events, 0.2 us)
Async XLA Ops:
  6.5 5.4 %copy-start = (f32[2,32,512]{2,1,0:T(8,128)S(1)}, f32[2,32,512]{2,1,0:T(8,128)}, u32[]{:S(2)}) copy-start(f32[2,32,512]{2,1,0:T(8,128)} %param.8) | copy-start | bytes 393220
  11.9 7.9 %copy-start.3 = (f32[2,32,128]{2,1,0:T(8,128)S(1)}, f32[2,32,128]{2,1,0:T(8,128)}, u32[]{:S(2)}) copy-start(f32[2,32,128]{2,1,0:T(8,128)} %param.5) | copy-start | bytes 98308
  11.9 24.0 %slice-start = ((f32[2,32,1024]{2,1,0:T(8,128)}), f32[1,32,1024]{2,1,0:T(8,128)S(1)}, s32[]{:S(2)}) async-start(f32[2,32,1024]{2,1,0:T(8,128)} %param.6), calls=%async_computation.7 | async-start | bytes 262144 | tf_op jit(solution)/shard_map/slice | solution.py:29
  11.9 24.0 %copy-start.2 = (f32[32,1024]{1,0:T(8,128)S(1)}, f32[32,1024]{1,0:T(8,128)}, u32[]{:S(2)}) copy-start(f32[32,1024]{1,0:T(8,128)} %param.7) | copy-start | bytes 393220
  16.2 64.4 %copy-start.1 = (f32[2,32,1024]{2,1,0:T(8,128)S(1)}, f32[2,32,1024]{2,1,0:T(8,128)}, u32[]{:S(2)}) copy-start(f32[2,32,1024]{2,1,0:T(8,128)} %param.6) | copy-start | bytes 786436
  16.3 3.6 %collective-permute-start = (f32[64,8,128]{2,0,1:T(8,128)S(1)}, f32[64,8,128]{2,0,1:T(8,128)S(1)}, u32[]{:S(2)}, u32[]{:S(2)}) collective-permute-start(f32[64,8,128]{2,0,1:T(8,128)S(1)} %dynamic-slice_bitcast_fusion), channel_id=1, source_target_pairs={{0,1},{1,0},{2,3},{3,2},{4,5},{5,4},{6,7},{7,6},{8,9},{9,8},{10,11... | collective-permute-start | bytes 786440 | tf_op jit(solution)/shard_map/ppermute | solution.py:36
  20.7 33.6 %all-to-all-start = ((f32[16,32,128]{2,1,0:T(8,128)}), f32[16,32,128]{2,1,0:T(8,128)S(1)}, u32[]{:S(2)}, u32[]{:S(2)}) async-start(f32[16,32,128]{2,1,0:T(8,128)} %bitcast.10), calls=%async_computation | async-start | bytes 524288 | tf_op jit(solution)/shard_map/all_to_all | solution.py:22
  55.1 17.9 %all-to-all-start.1 = ((f32[16,64,128]{2,1,0:T(8,128)}), f32[16,64,128]{2,1,0:T(8,128)S(1)}, u32[]{:S(2)}, u32[]{:S(2)}) async-start(f32[16,64,128]{2,1,0:T(8,128)} %broadcast_in_dim.83), calls=%async_computation.1 | async-start | bytes 1048576 | tf_op jit(solution)/shard_map/all_to_all | solution.py:16
  62.2 57.3 %reduce-scatter.2.cloned.1.call-start = ((), (), s32[]{:S(2)}) async-start(), calls=%async_computation.6 | async-start | bytes 786432 | tf_op jit(solution)/shard_map/reduce_scatter | solution.py:31
  73.8 46.9 %all-to-all-start.2 = ((f32[16,32,128]{2,1,0:T(8,128)}), f32[16,32,128]{2,1,0:T(8,128)S(1)}, u32[]{:S(2)}, u32[]{:S(2)}) async-start(f32[16,32,128]{2,1,0:T(8,128)} %bitcast.18), calls=%async_computation.2 | async-start | bytes 524288 | tf_op jit(solution)/shard_map/all_to_all | solution.py:22
  121.5 19.6 %all-to-all-start.3 = ((f32[16,64,128]{2,1,0:T(8,128)}), f32[16,64,128]{2,1,0:T(8,128)S(1)}, u32[]{:S(2)}, u32[]{:S(2)}) async-start(f32[16,64,128]{2,1,0:T(8,128)} %broadcast_in_dim.89), calls=%async_computation.4 | async-start | bytes 1048576 | tf_op jit(solution)/shard_map/all_to_all | solution.py:16
Sparse Core Ops, SparseCore 0:
  65.8 53.6 reduce-scatter.1

commit v2 on v1

v2 whole, which is shorter than its diff:
```python
import functools

import jax
import jax.numpy as jnp
from jax import lax
from jax.experimental import pallas as pl
from jax.experimental.pallas import tpu as pltpu
from jax.sharding import Mesh, PartitionSpec as P

ROWS = ("y", "x", "zh")
LINE = ("q", "b")
COLS = LINE + ("core",)


def mul(a, b):
    return jnp.dot(a, b, precision=lax.Precision.HIGHEST, preferred_element_type=jnp.float32)


def halves(x):
    high = x.astype(jnp.bfloat16)
    return high, (x - high.astype(jnp.float32)).astype(jnp.bfloat16)


def product_kernel(add, where_ref, panel_ref, even_ref, odd_ref, *rest):
    out_ref = rest[-1]
    step = pl.program_id(0)
    p_high, p_low = halves(-panel_ref[...])
    s_high, s_low = halves(jnp.concatenate([even_ref[...], odd_ref[...]], axis=1))
    dot = functools.partial(jnp.dot, preferred_element_type=jnp.float32)
    wide = dot(jnp.concatenate([p_high, p_low], axis=0), s_high)
    got = wide[64:] + dot(p_high, s_low) + wide[:64]
    for b in range(2):
        part = got[:, 128 * b : 128 * (b + 1)]
        if add:
            mine = jnp.logical_and(where_ref[1] == step, where_ref[2] == b)
            part = part + jnp.where(mine, rest[0][...], 0.0)
        out_ref[b, 0] = part


def product(where, panel, solved, add=None):
    whole = lambda shape: pl.BlockSpec(shape, lambda i, w: (0, 0))
    cols = lambda b: pl.BlockSpec((512, 128), lambda i, w: (0, 4 * i + 2 * b + w[0]))
    args = (panel, solved, solved) + (() if add is None else (add,))
    return pl.pallas_call(
        functools.partial(product_kernel, add is not None),
        out_shape=jax.ShapeDtypeStruct((2, 4, 64, 128), jnp.float32),
        grid_spec=pltpu.PrefetchScalarGridSpec(
            num_scalar_prefetch=1,
            grid=(4,),
            in_specs=[whole((64, 512)), cols(0), cols(1)] + ([] if add is None else [whole((64, 128))]),
            out_specs=pl.BlockSpec((2, 1, 64, 128), lambda i, w: (0, i, 0, 0)),
        ),
        compiler_params=pltpu.CompilerParams(vmem_limit_bytes=16 << 20),
        cost_estimate=pl.CostEstimate(flops=6 * 64 * 512 * 1024, bytes_accessed=3 << 20, transcendentals=0),
    )(where, *args)


def gather_plane(block):
    copies = jnp.broadcast_to(block[None], (16,) + block.shape)
    got = lax.all_to_all(copies, ("y", "x"), 0, 0, tiled=True)
    return got.reshape(16 * block.shape[0], block.shape[1])


def on_device(right_side, diag_inverse, coupling, panel, solved):
    zh, q, b, core = (lax.axis_index(a) for a in ("zh", "q", "b", "core"))
    swap = [(0, 1), (1, 0)]

    factor = jnp.where(core == 0, diag_inverse[0], coupling)
    slots = jnp.where((jnp.arange(2) == 1 - zh)[:, None, None], factor[None], 0.0)
    pairs = [[z, 15 - z] for z in range(8)]
    got = lax.psum_scatter(slots, ("zh",) + LINE, scatter_dimension=0, axis_index_groups=pairs, tiled=True)[0]
    where = lambda c: jnp.stack([c, q, b]).astype(jnp.int32)
    panel = panel.reshape(64, 512)
    send = product(where(1 - core), panel, solved)
    moved = lax.ppermute(send, "core", swap)
    keep = product(where(core), panel, solved, right_side.reshape(64, 128))
    total = keep + moved
    moved = lax.ppermute(lax.dynamic_index_in_dim(total, 1 - b, 0, keepdims=False), "b", swap)
    total = lax.dynamic_index_in_dim(total, b, 0, keepdims=False) + moved
    copies = jnp.broadcast_to(total[None], (2, 4, 64, 128)).reshape(8, 64, 128)
    got_all = lax.all_to_all(copies, ("zh", "q"), 0, 0, tiled=True)
    got_all, got = lax.optimization_barrier((got_all, got))
    partner = lax.ppermute(got, "core", swap)
    other = (jnp.where(core == 0, got, partner), jnp.where(core == 0, partner, got))
    residual = got_all.reshape(2, 4, 2, 32, 128).sum(1)
    first_res = residual[:, 0].reshape(64, 128)
    second_part = residual[:, 1].reshape(64, 128)

    def both(mine, theirs, x):
        a, c = mul(mine, x), mul(theirs, x)
        return jnp.where(zh == 0, jnp.concatenate([a, c]), jnp.concatenate([c, a])), a

    first_sol, first_mine = both(diag_inverse[0], other[0], gather_plane(first_res))
    cross, _ = both(coupling, other[1], gather_plane(first_sol))
    second_mine = mul(diag_inverse[1], gather_plane(second_part - cross))
    return jnp.stack([first_mine, second_mine])


def solution(mesh):
    fine = Mesh(mesh.devices.reshape(4, 4, 2, 4, 2, 2), ROWS + COLS)
    return jax.shard_map(
        on_device,
        mesh=fine,
        in_specs=(
            P(None, ROWS, COLS),
            P(None, ROWS, None),
            P(ROWS, None),
            P(None, ROWS, COLS),
            P(COLS, None),
        ),
        out_specs=P(None, ROWS, COLS),
        check_vma=False,
    )
```

time: 165 us -> 135 us (0.82)
  the two profiles are of different devices: /device:TPU:32 before, /device:TPU:2 now
where the time goes in v2:
time: 135 us; the launch traced here: 134 us
  waiting for transfers between devices  49.3 us (37%)
  starting transfers between devices  29.9 us (22%)
  blocking collectives  26.2 us (19%)
  between operations  13.6 us (10%)
  local copies, waits for them, and re-layouts  6.97 us (5%)
  Pallas kernels  3.86 us (3%)
  matrix products  2.94 us (2%)
  other arithmetic  1.68 us (1%)
    reduce_scatter x1, waiting for transfers between devices, on_device(): lax.psum_scatter(slots, ('zh',) + LINE, scatter_dimension=0, axis_index_g...  36.9 us
    all_to_all x2, blocking collectives, gather_plane(): got = lax.all_to_all(copies, ('y', 'x'), 0, 0, tiled=True)  26.2 us
    all_to_all x1, starting transfers between devices, on_device(): got_all = lax.all_to_all(copies, ('zh', 'q'), 0, 0, tiled=True)  14.9 us
    all_to_all x1, waiting for transfers between devices, gather_plane(): got = lax.all_to_all(copies, ('y', 'x'), 0, 0, tiled=True)  8.25 us
    all_to_all x1, starting transfers between devices, gather_plane(): got = lax.all_to_all(copies, ('y', 'x'), 0, 0, tiled=True)  7.28 us
    unnamed x16, local copies, waits for them, and re-layouts  5.3 us
    ppermute x1, waiting for transfers between devices, on_device(): lax.ppermute(lax.dynamic_index_in_dim(total, 1 - b, 0, keepdims=False), '...  4.14 us
    pallas_call x2, Pallas kernels, product(): pl.pallas_call(functools.partial(product_kernel, add is not None), out_sh...  3.86 us
  transfers between devices with their start and end apart: 6, of which 3 were waited for; matrix products, arithmetic and copies ran while one was open for 1% of the time, Pallas kernels for 1%

profile of v2, /device:TPU:2, one launch (start us, length us, event | category | flops | bytes accessed | tf_op | source)
XLA Modules:
  0.0 134.5 jit_solution(11874815477284663583)
XLA Ops:
  6.5 0.1 add_add_fusion.1.where_ref
  6.6 2.2 %copy-done = f32[512,2048]{1,0:T(8,128)S(1)} copy-done((f32[512,2048]{1,0:T(8,128)S(1)}, f32[512,2048]{1,0:T(8,128)}, u32[]{:S(2)}) %copy-start) | copy-done | bytes 4194328
  8.8 0.9 copy-done.2
  9.7 1.9 %shard_map.56 = f32[2,4,64,128]{3,2,1,0:T(8,128)S(1)} custom-call(s32[3]{0:T(128)S(1)} %add_add_fusion.1.where_ref, f32[64,512]{1,0:T(8,128)S(1)} %bitcast.41, f32[512,2048]{1,0:T(8,128)S(1)} %copy-done, f32[512,2048]{1,0:T(8,128)S(1)} %copy-done), custom_call_target="tpu_custom_call" | custom-call | flops 201326592 | bytes 3145728 | tf_op jit(solution)/shard_map/pallas_call | solution.py:44
  11.6 1.9 %collective-permute-start = (f32[2,4,64,128]{3,2,1,0:T(8,128)S(1)}, f32[2,4,64,128]{3,2,1,0:T(8,128)S(1)}, u32[]{:S(2)}, u32[]{:S(2)}) collective-permute-start(f32[2,4,64,128]{3,2,1,0:T(8,128)S(1)} %shard_map.56), channel_id=1, source_target_pairs={{0,1},{1,0},{2,3},{3,2},{4,5},{5,4},{6,7},{7,6},{8,9},{9,8},{10,11... | collective-permute-start | bytes 786440 | tf_op jit(solution)/shard_map/ppermute | solution.py:75
  13.6 0.1 add_add_fusion.where_ref
  13.7 0.0 copy-done.3
  13.7 2.2 %copy-done.1 = f32[512,2048]{1,0:T(8,128)S(1)} copy-done((f32[512,2048]{1,0:T(8,128)S(1)}, f32[512,2048]{1,0:T(8,128)}, u32[]{:S(2)}) %copy-start.1) | copy-done | bytes 4194328
  15.9 1.9 %shard_map.55 = f32[2,4,64,128]{3,2,1,0:T(8,128)S(1)} custom-call(s32[3]{0:T(128)S(1)} %add_add_fusion.where_ref, f32[64,512]{1,0:T(8,128)S(1)} %bitcast.42, f32[512,2048]{1,0:T(8,128)S(1)} %copy-done.1, f32[512,2048]{1,0:T(8,128)S(1)} %copy-done.1, f32[64,128]{1,0:T(8,128)S(1)} %bitcast.43), custom_call_target="tpu_custom_call" | custom-call | flops 201326592 | bytes 3145728 | tf_op jit(solution)/shard_map/pallas_call | solution.py:44
  17.8 0.0 collective-permute-done
  17.9 3.8 %collective-permute-start.1 = (f32[4,64,128]{2,1,0:T(8,128)S(1)}, f32[4,64,128]{2,1,0:T(8,128)S(1)}, u32[]{:S(2)}, u32[]{:S(2)}) collective-permute-start(f32[4,64,128]{2,1,0:T(8,128)S(1)} %dynamic-slice_bitcast_fusion), channel_id=1, source_target_pairs={{0,2},{2,0},{1,3},{3,1},{4,6},{6,4},{5,7},{7,5},{8,10},{10,8},{9,1... | collective-permute-start | bytes 393224 | tf_op jit(solution)/shard_map/ppermute | solution.py:78
  21.7 4.1 %collective-permute-done.1 = f32[4,64,128]{2,1,0:T(8,128)S(1)} collective-permute-done((f32[4,64,128]{2,1,0:T(8,128)S(1)}, f32[4,64,128]{2,1,0:T(8,128)S(1)}, u32[]{:S(2)}, u32[]{:S(2)}) %collective-permute-start.1) | collective-permute-done | bytes 131104 | tf_op jit(solution)/shard_map/ppermute | solution.py:78
  25.9 0.7 broadcast_in_dim.30
  26.6 14.9 %all-to-all-start = ((f32[8,64,128]{2,1,0:T(8,128)}), f32[8,64,128]{2,1,0:T(8,128)S(1)}, u32[]{:S(2)}, u32[]{:S(2)}) async-start(f32[8,64,128]{2,1,0:T(8,128)} %bitcast.8), calls=%async_computation | async-start | bytes 524288 | tf_op jit(solution)/shard_map/all_to_all | solution.py:81
  41.5 0.0 reduce-scatter.2.cloned.1.call-start
  41.6 0.8 broadcast_select_fusion
  42.4 0.0 reduce-scatter.2.cloned.1.call-update
  42.4 36.9 %reduce-scatter.2.cloned.1.call-done = f32[1,32,1024]{2,1,0:T(8,128)} async-done(((f32[2,32,1024]{2,1,0:T(8,128)}), f32[1,32,1024]{2,1,0:T(8,128)}) %reduce-scatter.2.cloned.1.call-update) | async-done | bytes 131088 | tf_op jit(solution)/shard_map/reduce_scatter | solution.py:71
  79.4 0.0 all-to-all-done
  79.4 0.8 broadcast_in_dim.52
  80.2 7.3 %all-to-all-start.1 = ((f32[16,64,128]{2,1,0:T(8,128)}), f32[16,64,128]{2,1,0:T(8,128)S(1)}, u32[]{:S(2)}, u32[]{:S(2)}) async-start(f32[16,64,128]{2,1,0:T(8,128)} %broadcast_in_dim.52), calls=%async_computation.2 | async-start | bytes 1048576 | tf_op jit(solution)/shard_map/all_to_all | solution.py:60
  87.5 1.9 %collective-permute-start.2 = (f32[32,1024]{1,0:T(8,128)}, f32[32,1024]{1,0:T(8,128)S(1)}, u32[]{:S(2)}, u32[]{:S(2)}) collective-permute-start(f32[32,1024]{1,0:T(8,128)} %bitcast.50), channel_id=1, source_target_pairs={{0,1},{1,0},{2,3},{3,2},{4,5},{5,4},{6,7},{7,6},{8,9},{9,8},{10,11... | collective-permute-start | bytes 393224 | tf_op jit(solution)/shard_map/ppermute | solution.py:83
  89.4 8.2 %all-to-all-done.1 = f32[16,64,128]{2,1,0:T(8,128)S(1)} async-done(((f32[16,64,128]{2,1,0:T(8,128)}), f32[16,64,128]{2,1,0:T(8,128)S(1)}, u32[]{:S(2)}, u32[]{:S(2)}) %all-to-all-start.1) | async-done | bytes 524320 | tf_op jit(solution)/shard_map/all_to_all | solution.py:60
  97.7 0.4 fusion.1
  98.1 0.0 collective-permute-done.2
  98.1 1.3 fusion.6
  99.5 13.0 %all_to_all.20 = f32[16,64,128]{2,1,0:T(8,128)S(1)} all-to-all(f32[16,64,128]{2,1,0:T(8,128)S(1)} %broadcast_in_dim.53), channel_id=1, replica_groups=mesh['y'=4,'x'=4,'zh'=2,'q'=4,'b'=2,'core'=2] {'y','x'}, dimensions={0} | all-to-all | bytes 1048576 | tf_op jit(solution)/shard_map/all_to_all | solution.py:60
  112.5 0.4 convolution_bitcast_fusion.1
  113.0 0.4 fusion.4
  113.4 13.2 %all_to_all.21 = f32[16,64,128]{2,1,0:T(8,128)S(1)} all-to-all(f32[16,64,128]{2,1,0:T(8,128)S(1)} %broadcast_in_dim.54), channel_id=1, replica_groups=mesh['y'=4,'x'=4,'zh'=2,'q'=4,'b'=2,'core'=2] {'y','x'}, dimensions={0} | all-to-all | bytes 1048576 | tf_op jit(solution)/shard_map/all_to_all | solution.py:60
  126.6 0.4 convolution_bitcast_fusion
  127.0 0.6 pad_maximum_fusion
  (23 shorter events, 0.2 us)
Async XLA Ops:
  6.6 2.2 %copy-start = (f32[512,2048]{1,0:T(8,128)S(1)}, f32[512,2048]{1,0:T(8,128)}, u32[]{:S(2)}) copy-start(f32[512,2048]{1,0:T(8,128)} %odd_ref.3) | copy-start | bytes 12582916
  8.8 0.9 copy-start.2
  9.7 4.0 %copy-start.3 = (f32[2,32,512]{2,1,0:T(8,128)S(1)}, f32[2,32,512]{2,1,0:T(8,128)}, u32[]{:S(2)}) copy-start(f32[2,32,512]{2,1,0:T(8,128)} %param.8) | copy-start | bytes 393220
  9.7 4.0 %copy-start.4 = (f32[2,32,128]{2,1,0:T(8,128)S(1)}, f32[2,32,128]{2,1,0:T(8,128)}, u32[]{:S(2)}) copy-start(f32[2,32,128]{2,1,0:T(8,128)} %param.5) | copy-start | bytes 98308
  11.6 6.2 %collective-permute-start = (f32[2,4,64,128]{3,2,1,0:T(8,128)S(1)}, f32[2,4,64,128]{3,2,1,0:T(8,128)S(1)}, u32[]{:S(2)}, u32[]{:S(2)}) collective-permute-start(f32[2,4,64,128]{3,2,1,0:T(8,128)S(1)} %shard_map.56), channel_id=1, source_target_pairs={{0,1},{1,0},{2,3},{3,2},{4,5},{5,4},{6,7},{7,6},{8,9},{9,8},{10,11... | collective-permute-start | bytes 786440 | tf_op jit(solution)/shard_map/ppermute | solution.py:75
  13.7 2.2 %copy-start.1 = (f32[512,2048]{1,0:T(8,128)S(1)}, f32[512,2048]{1,0:T(8,128)}, u32[]{:S(2)}) copy-start(f32[512,2048]{1,0:T(8,128)} %odd_ref.3) | copy-start | bytes 12582916
  15.8 25.7 %copy-start.5 = (f32[2,32,1024]{2,1,0:T(8,128)S(1)}, f32[2,32,1024]{2,1,0:T(8,128)}, u32[]{:S(2)}) copy-start(f32[2,32,1024]{2,1,0:T(8,128)} %param.6) | copy-start | bytes 786436
  15.9 25.7 %copy-start.6 = (f32[32,1024]{1,0:T(8,128)S(1)}, f32[32,1024]{1,0:T(8,128)}, u32[]{:S(2)}) copy-start(f32[32,1024]{1,0:T(8,128)} %param.7) | copy-start | bytes 393220
  17.9 8.0 %collective-permute-start.1 = (f32[4,64,128]{2,1,0:T(8,128)S(1)}, f32[4,64,128]{2,1,0:T(8,128)S(1)}, u32[]{:S(2)}, u32[]{:S(2)}) collective-permute-start(f32[4,64,128]{2,1,0:T(8,128)S(1)} %dynamic-slice_bitcast_fusion), channel_id=1, source_target_pairs={{0,2},{2,0},{1,3},{3,1},{4,6},{6,4},{5,7},{7,5},{8,10},{10,8},{9,1... | collective-permute-start | bytes 393224 | tf_op jit(solution)/shard_map/ppermute | solution.py:78
  26.6 52.8 %all-to-all-start = ((f32[8,64,128]{2,1,0:T(8,128)}), f32[8,64,128]{2,1,0:T(8,128)S(1)}, u32[]{:S(2)}, u32[]{:S(2)}) async-start(f32[8,64,128]{2,1,0:T(8,128)} %bitcast.8), calls=%async_computation | async-start | bytes 524288 | tf_op jit(solution)/shard_map/all_to_all | solution.py:81
  41.5 37.9 %reduce-scatter.2.cloned.1.call-start = ((), (), s32[]{:S(2)}) async-start(), calls=%async_computation.5 | async-start | bytes 393216 | tf_op jit(solution)/shard_map/reduce_scatter | solution.py:71
  79.4 33.6 %copy-start.7 = (f32[1,32,1024]{2,1,0:T(8,128)S(1)}, f32[1,32,1024]{2,1,0:T(8,128)}, u32[]{:S(2)}) copy-start(f32[1,32,1024]{2,1,0:T(8,128)} %reduce-scatter.2.cloned.1.call-done) | copy-start | bytes 393220
  80.2 17.4 %all-to-all-start.1 = ((f32[16,64,128]{2,1,0:T(8,128)}), f32[16,64,128]{2,1,0:T(8,128)S(1)}, u32[]{:S(2)}, u32[]{:S(2)}) async-start(f32[16,64,128]{2,1,0:T(8,128)} %broadcast_in_dim.52), calls=%async_computation.2 | async-start | bytes 1048576 | tf_op jit(solution)/shard_map/all_to_all | solution.py:60
  87.5 10.6 %collective-permute-start.2 = (f32[32,1024]{1,0:T(8,128)}, f32[32,1024]{1,0:T(8,128)S(1)}, u32[]{:S(2)}, u32[]{:S(2)}) collective-permute-start(f32[32,1024]{1,0:T(8,128)} %bitcast.50), channel_id=1, source_target_pairs={{0,1},{1,0},{2,3},{3,2},{4,5},{5,4},{6,7},{7,6},{8,9},{9,8},{10,11... | collective-permute-start | bytes 393224 | tf_op jit(solution)/shard_map/ppermute | solution.py:83
Sparse Core Ops, SparseCore 0:
  45.1 34.2 reduce-scatter.1

commit v3 on v2

--- a/solution.py
+++ b/solution.py
@@ -50,7 +50,7 @@
             in_specs=[whole((64, 512)), cols(0), cols(1)] + ([] if add is None else [whole((64, 128))]),
             out_specs=pl.BlockSpec((2, 1, 64, 128), lambda i, w: (0, i, 0, 0)),
         ),
-        compiler_params=pltpu.CompilerParams(vmem_limit_bytes=16 << 20),
+        compiler_params=pltpu.CompilerParams(vmem_limit_bytes=60 << 20),
         cost_estimate=pl.CostEstimate(flops=6 * 64 * 512 * 1024, bytes_accessed=3 << 20, transcendentals=0),
     )(where, *args)
 
@@ -66,9 +66,8 @@
     swap = [(0, 1), (1, 0)]
 
     factor = jnp.where(core == 0, diag_inverse[0], coupling)
-    slots = jnp.where((jnp.arange(2) == 1 - zh)[:, None, None], factor[None], 0.0)
-    pairs = [[z, 15 - z] for z in range(8)]
-    got = lax.psum_scatter(slots, ("zh",) + LINE, scatter_dimension=0, axis_index_groups=pairs, tiled=True)[0]
+    got = lax.ppermute(factor, ("zh",) + LINE, [(z, 15 - z) for z in range(16)])
+
     where = lambda c: jnp.stack([c, q, b]).astype(jnp.int32)
     panel = panel.reshape(64, 512)
     send = product(where(1 - core), panel, solved)

time: 135 us -> 113 us (0.84)
  the two profiles are of different devices: /device:TPU:2 before, /device:TPU:64 now
where the time goes in v3:
time: 113 us
  starting transfers between devices  36.1 us (32%)
  waiting for transfers between devices  34.4 us (30%)
  blocking collectives  26.2 us (23%)
  Pallas kernels  9.26 us (8%)
  other arithmetic  2.95 us (3%)
  matrix products  2.03 us (2%)
  local copies, waits for them, and re-layouts  1.69 us (1%)
    all_to_all x2, blocking collectives, gather_plane(): got = lax.all_to_all(copies, ('y', 'x'), 0, 0, tiled=True)  26.2 us
    ppermute x1, waiting for transfers between devices, on_device(): got = lax.ppermute(factor, ('zh',) + LINE, [(z, 15 - z) for z in range(16)])  14.7 us
    all_to_all x1, starting transfers between devices, on_device(): got_all = lax.all_to_all(copies, ('zh', 'q'), 0, 0, tiled=True)  14.6 us
    pallas_call x2, Pallas kernels, product(): pl.pallas_call(functools.partial(product_kernel, add is not None), out_sh...  9.26 us
    all_to_all x1, waiting for transfers between devices, gather_plane(): got = lax.all_to_all(copies, ('y', 'x'), 0, 0, tiled=True)  8.2 us
    all_to_all x1, waiting for transfers between devices, on_device(): got_all = lax.all_to_all(copies, ('zh', 'q'), 0, 0, tiled=True)  7.33 us
    all_to_all x1, starting transfers between devices, gather_plane(): got = lax.all_to_all(copies, ('y', 'x'), 0, 0, tiled=True)  7.03 us
    ppermute x1, starting transfers between devices, on_device(): got = lax.ppermute(factor, ('zh',) + LINE, [(z, 15 - z) for z in range(16)])  6.84 us
  transfers between devices with their start and end apart: 6, of which 4 were waited for; matrix products, arithmetic and copies ran while one was open for 1% of the time, Pallas kernels for 4%

profile of v3, /device:TPU:64, one launch (start us, length us, event | category | flops | bytes accessed | tf_op | source)
XLA Modules:
  0.0 112.7 jit_solution(6849033025199510857)
XLA Ops:
  0.0 0.7 add_add_fusion.1.where_ref
  0.7 4.5 %shard_map.56 = f32[2,4,64,128]{3,2,1,0:T(8,128)} custom-call(s32[3]{0:T(128)} %add_add_fusion.1.where_ref, f32[64,512]{1,0:T(8,128)} %bitcast.46, f32[512,2048]{1,0:T(8,128)} %odd_ref.3, f32[512,2048]{1,0:T(8,128)} %odd_ref.3), custom_call_target="tpu_custom_call" | custom-call | flops 201326592 | bytes 3145728 | tf_op jit(solution)/shard_map/pallas_call | solution.py:44
  5.2 1.9 %collective-permute-start = (f32[2,4,64,128]{3,2,1,0:T(8,128)}, f32[2,4,64,128]{3,2,1,0:T(8,128)S(1)}, u32[]{:S(2)}, u32[]{:S(2)}) collective-permute-start(f32[2,4,64,128]{3,2,1,0:T(8,128)} %shard_map.56), channel_id=1, source_target_pairs={{0,1},{1,0},{2,3},{3,2},{4,5},{5,4},{6,7},{7,6},{8,9},{9,8},{10,11... | collective-permute-start | bytes 786440 | tf_op jit(solution)/shard_map/ppermute | solution.py:74
  7.1 0.6 add_add_fusion.where_ref
  7.7 0.0 copy-start
  7.8 0.0 copy-start.1
  7.8 4.7 %shard_map.55 = f32[2,4,64,128]{3,2,1,0:T(8,128)} custom-call(s32[3]{0:T(128)} %add_add_fusion.where_ref, f32[64,512]{1,0:T(8,128)} %bitcast.47, f32[512,2048]{1,0:T(8,128)} %odd_ref.3, f32[512,2048]{1,0:T(8,128)} %odd_ref.3, f32[64,128]{1,0:T(8,128)} %bitcast.51), custom_call_target="tpu_custom_call" | custom-call | flops 201326592 | bytes 3145728 | tf_op jit(solution)/shard_map/pallas_call | solution.py:44
  12.5 0.0 collective-permute-done
  12.5 1.0 add.14
  13.5 3.8 %collective-permute-start.1 = (f32[4,64,128]{2,1,0:T(8,128)S(1)}, f32[4,64,128]{2,1,0:T(8,128)S(1)}, u32[]{:S(2)}, u32[]{:S(2)}) collective-permute-start(f32[4,64,128]{2,1,0:T(8,128)S(1)} %dynamic-slice_bitcast_fusion), channel_id=1, source_target_pairs={{0,2},{2,0},{1,3},{3,1},{4,6},{6,4},{5,7},{7,5},{8,10},{10,8},{9,1... | collective-permute-start | bytes 393224 | tf_op jit(solution)/shard_map/ppermute | solution.py:77
  17.3 4.1 %collective-permute-done.1 = f32[4,64,128]{2,1,0:T(8,128)S(1)} collective-permute-done((f32[4,64,128]{2,1,0:T(8,128)S(1)}, f32[4,64,128]{2,1,0:T(8,128)S(1)}, u32[]{:S(2)}, u32[]{:S(2)}) %collective-permute-start.1) | collective-permute-done | bytes 131104 | tf_op jit(solution)/shard_map/ppermute | solution.py:77
  21.5 0.7 broadcast_in_dim.10
  22.2 14.6 %all-to-all-start = ((f32[8,64,128]{2,1,0:T(8,128)}), f32[8,64,128]{2,1,0:T(8,128)S(1)}, u32[]{:S(2)}, u32[]{:S(2)}) async-start(f32[8,64,128]{2,1,0:T(8,128)} %bitcast.8), calls=%async_computation | async-start | bytes 524288 | tf_op jit(solution)/shard_map/all_to_all | solution.py:80
  36.7 0.0 copy-done
  36.7 0.0 copy-done.1
  36.8 6.8 %collective-permute-start.2 = (f32[32,1024]{1,0:T(8,128)S(1)}, f32[32,1024]{1,0:T(8,128)S(1)}, u32[]{:S(2)}, u32[]{:S(2)}) collective-permute-start(f32[32,1024]{1,0:T(8,128)S(1)} %bitcast_select_fusion), channel_id=1, source_target_pairs={{0,30},{2,28},{4,26},{6,24},{8,22},{10,20},{12,18},{14,16},{16,14}... | collective-permute-start | bytes 393224 | tf_op jit(solution)/shard_map/ppermute | solution.py:69
  43.6 14.7 %collective-permute-done.2 = f32[32,1024]{1,0:T(8,128)S(1)} collective-permute-done((f32[32,1024]{1,0:T(8,128)S(1)}, f32[32,1024]{1,0:T(8,128)S(1)}, u32[]{:S(2)}, u32[]{:S(2)}) %collective-permute-start.2) | collective-permute-done | bytes 131104 | tf_op jit(solution)/shard_map/ppermute | solution.py:69
  58.3 7.3 %all-to-all-done = f32[8,64,128]{2,1,0:T(8,128)S(1)} async-done(((f32[8,64,128]{2,1,0:T(8,128)}), f32[8,64,128]{2,1,0:T(8,128)S(1)}, u32[]{:S(2)}, u32[]{:S(2)}) %all-to-all-start) | async-done | bytes 262176 | tf_op jit(solution)/shard_map/all_to_all | solution.py:80
  65.7 0.9 broadcast_in_dim.12
  66.5 7.0 %all-to-all-start.1 = ((f32[16,64,128]{2,1,0:T(8,128)}), f32[16,64,128]{2,1,0:T(8,128)S(1)}, u32[]{:S(2)}, u32[]{:S(2)}) async-start(f32[16,64,128]{2,1,0:T(8,128)} %broadcast_in_dim.12), calls=%async_computation.1 | async-start | bytes 1048576 | tf_op jit(solution)/shard_map/all_to_all | solution.py:60
  73.6 1.9 %collective-permute-start.3 = (f32[32,1024]{1,0:T(8,128)S(1)}, f32[32,1024]{1,0:T(8,128)S(1)}, u32[]{:S(2)}, u32[]{:S(2)}) collective-permute-start(f32[32,1024]{1,0:T(8,128)S(1)} %collective-permute-done.2), channel_id=1, source_target_pairs={{0,1},{1,0},{2,3},{3,2},{4,5},{5,4},{6,7},{7,6},{8,9},{9,8},{10,11... | collective-permute-start | bytes 393224 | tf_op jit(solution)/shard_map/ppermute | solution.py:82
  75.5 8.2 %all-to-all-done.1 = f32[16,64,128]{2,1,0:T(8,128)S(1)} async-done(((f32[16,64,128]{2,1,0:T(8,128)}), f32[16,64,128]{2,1,0:T(8,128)S(1)}, u32[]{:S(2)}, u32[]{:S(2)}) %all-to-all-start.1) | async-done | bytes 524320 | tf_op jit(solution)/shard_map/all_to_all | solution.py:60
  83.7 0.4 fusion.1
  84.1 0.0 collective-permute-done.3
  84.1 0.4 fusion.6
  84.6 13.1 %all_to_all.20 = f32[16,64,128]{2,1,0:T(8,128)S(1)} all-to-all(f32[16,64,128]{2,1,0:T(8,128)S(1)} %broadcast_in_dim.13), channel_id=1, replica_groups=mesh['y'=4,'x'=4,'zh'=2,'q'=4,'b'=2,'core'=2] {'y','x'}, dimensions={0} | all-to-all | bytes 1048576 | tf_op jit(solution)/shard_map/all_to_all | solution.py:60
  97.7 0.4 convolution_bitcast_fusion.1
  98.1 0.4 fusion.4
  98.6 13.1 %all_to_all.21 = f32[16,64,128]{2,1,0:T(8,128)S(1)} all-to-all(f32[16,64,128]{2,1,0:T(8,128)S(1)} %broadcast_in_dim.14), channel_id=1, replica_groups=mesh['y'=4,'x'=4,'zh'=2,'q'=4,'b'=2,'core'=2] {'y','x'}, dimensions={0} | all-to-all | bytes 1048576 | tf_op jit(solution)/shard_map/all_to_all | solution.py:60
  111.7 0.4 convolution_bitcast_fusion
  112.1 0.6 pad_maximum_fusion
  (9 shorter events, 0.2 us)
Async XLA Ops:
  5.2 7.2 %collective-permute-start = (f32[2,4,64,128]{3,2,1,0:T(8,128)}, f32[2,4,64,128]{3,2,1,0:T(8,128)S(1)}, u32[]{:S(2)}, u32[]{:S(2)}) collective-permute-start(f32[2,4,64,128]{3,2,1,0:T(8,128)} %shard_map.56), channel_id=1, source_target_pairs={{0,1},{1,0},{2,3},{3,2},{4,5},{5,4},{6,7},{7,6},{8,9},{9,8},{10,11... | collective-permute-start | bytes 786440 | tf_op jit(solution)/shard_map/ppermute | solution.py:74
  7.7 29.0 %copy-start = (f32[2,32,1024]{2,1,0:T(8,128)S(1)}, f32[2,32,1024]{2,1,0:T(8,128)}, u32[]{:S(2)}) copy-start(f32[2,32,1024]{2,1,0:T(8,128)} %param.6) | copy-start | bytes 786436
  7.8 29.0 %copy-start.1 = (f32[32,1024]{1,0:T(8,128)S(1)}, f32[32,1024]{1,0:T(8,128)}, u32[]{:S(2)}) copy-start(f32[32,1024]{1,0:T(8,128)} %param.7) | copy-start | bytes 393220
  13.5 8.0 %collective-permute-start.1 = (f32[4,64,128]{2,1,0:T(8,128)S(1)}, f32[4,64,128]{2,1,0:T(8,128)S(1)}, u32[]{:S(2)}, u32[]{:S(2)}) collective-permute-start(f32[4,64,128]{2,1,0:T(8,128)S(1)} %dynamic-slice_bitcast_fusion), channel_id=1, source_target_pairs={{0,2},{2,0},{1,3},{3,1},{4,6},{6,4},{5,7},{7,5},{8,10},{10,8},{9,1... | collective-permute-start | bytes 393224 | tf_op jit(solution)/shard_map/ppermute | solution.py:77
  22.2 43.4 %all-to-all-start = ((f32[8,64,128]{2,1,0:T(8,128)}), f32[8,64,128]{2,1,0:T(8,128)S(1)}, u32[]{:S(2)}, u32[]{:S(2)}) async-start(f32[8,64,128]{2,1,0:T(8,128)} %bitcast.8), calls=%async_computation | async-start | bytes 524288 | tf_op jit(solution)/shard_map/all_to_all | solution.py:80
  36.8 21.5 %collective-permute-start.2 = (f32[32,1024]{1,0:T(8,128)S(1)}, f32[32,1024]{1,0:T(8,128)S(1)}, u32[]{:S(2)}, u32[]{:S(2)}) collective-permute-start(f32[32,1024]{1,0:T(8,128)S(1)} %bitcast_select_fusion), channel_id=1, source_target_pairs={{0,30},{2,28},{4,26},{6,24},{8,22},{10,20},{12,18},{14,16},{16,14}... | collective-permute-start | bytes 393224 | tf_op jit(solution)/shard_map/ppermute | solution.py:69
  66.5 17.2 %all-to-all-start.1 = ((f32[16,64,128]{2,1,0:T(8,128)}), f32[16,64,128]{2,1,0:T(8,128)S(1)}, u32[]{:S(2)}, u32[]{:S(2)}) async-start(f32[16,64,128]{2,1,0:T(8,128)} %broadcast_in_dim.12), calls=%async_computation.1 | async-start | bytes 1048576 | tf_op jit(solution)/shard_map/all_to_all | solution.py:60
  73.6 10.6 %collective-permute-start.3 = (f32[32,1024]{1,0:T(8,128)S(1)}, f32[32,1024]{1,0:T(8,128)S(1)}, u32[]{:S(2)}, u32[]{:S(2)}) collective-permute-start(f32[32,1024]{1,0:T(8,128)S(1)} %collective-permute-done.2), channel_id=1, source_target_pairs={{0,1},{1,0},{2,3},{3,2},{4,5},{5,4},{6,7},{7,6},{8,9},{9,8},{10,11... | collective-permute-start | bytes 393224 | tf_op jit(solution)/shard_map/ppermute | solution.py:82

commit v4 on v3

v4 whole, which is shorter than its diff:
```python
import functools

import jax
import jax.numpy as jnp
from jax import lax
from jax.experimental import pallas as pl
from jax.experimental.pallas import tpu as pltpu
from jax.sharding import Mesh, PartitionSpec as P

ROWS = ("y", "x", "zh")
LINE = ("q", "b")
COLS = LINE + ("core",)


def mul(a, b):
    return jnp.dot(a, b, precision=lax.Precision.HIGHEST, preferred_element_type=jnp.float32)


def halves(x):
    high = x.astype(jnp.bfloat16)
    return high, (x - high.astype(jnp.float32)).astype(jnp.bfloat16)


def product_kernel(mine, panel_ref, solved_ref, *rest):
    out_ref, slots, sems = rest[-3:]
    core, q, b = (lax.axis_index(a) for a in ("core", "q", "b"))
    parity = core if mine else 1 - core
    copies = []
    for step in range(4):
        for half in range(2):
            columns = pl.ds(pl.multiple_of((4 * step + 2 * half + parity) * 128, 128), 128)
            copy = pltpu.make_async_copy(
                solved_ref.at[:, columns],
                slots.at[step, :, pl.ds(128 * half, 128)],
                sems.at[step, half],
            )
            copy.start()
            copies.append(copy)
    p_high, p_low = halves(-panel_ref[...])
    p_both = jnp.concatenate([p_high, p_low], axis=0)
    dot = functools.partial(jnp.dot, preferred_element_type=jnp.float32)
    for step in range(4):
        copies[2 * step].wait()
        copies[2 * step + 1].wait()
        s_high, s_low = halves(slots[step])
        wide = dot(p_both, s_high)
        got = wide[64:] + dot(p_high, s_low) + wide[:64]
        for half in range(2):
            part = got[:, 128 * half : 128 * (half + 1)]
            if mine:
                here = jnp.logical_and(q == step, b == half)
                part = part + jnp.where(here, rest[0][...], 0.0)
            out_ref[half, step] = part


def product(panel, solved, add=None):
    args = (panel, solved) + (() if add is None else (add,))
    vmem = pl.BlockSpec(memory_space=pltpu.VMEM)
    return pl.pallas_call(
        functools.partial(product_kernel, add is not None),
        out_shape=jax.ShapeDtypeStruct((2, 4, 64, 128), jnp.float32),
        in_specs=[vmem, pl.BlockSpec(memory_space=pl.ANY)] + [vmem] * (add is not None),
        out_specs=vmem,
        scratch_shapes=[pltpu.VMEM((4, 512, 256), jnp.float32), pltpu.SemaphoreType.DMA((4, 2))],
        compiler_params=pltpu.CompilerParams(vmem_limit_bytes=56 << 20),
        cost_estimate=pl.CostEstimate(flops=6 * 64 * 512 * 1024, bytes_accessed=3 << 20, transcendentals=0),
    )(*args)


def pair_up(index, mine, theirs):
    first = index == 0
    return jnp.stack([jnp.where(first, mine, theirs), jnp.where(first, theirs, mine)])


def gather_plane(block):
    copies = jnp.broadcast_to(block[None], (16,) + block.shape)
    got = lax.all_to_all(copies, ("y", "x"), 0, 0, tiled=True)
    return got.reshape(16 * block.shape[0], block.shape[1])


def on_device(right_side, diag_inverse, coupling, panel, solved):
    zh, b, core = (lax.axis_index(a) for a in ("zh", "b", "core"))
    swap = [(0, 1), (1, 0)]

    rows = lambda x: lax.dynamic_slice_in_dim(x, 16 * core, 16, 0)
    quarter = jnp.where(b == 1, rows(diag_inverse[0]), rows(coupling))
    quarter = lax.ppermute(quarter, ("zh",) + LINE, [(z, 15 - z) for z in range(16)])

    panel = panel.reshape(64, 512)
    send = product(panel, solved)
    moved = lax.ppermute(send, "core", swap)
    keep = product(panel, solved, right_side.reshape(64, 128))
    total = keep + moved
    moved = lax.ppermute(lax.dynamic_index_in_dim(total, 1 - b, 0, keepdims=False), "b", swap)
    total = lax.dynamic_index_in_dim(total, b, 0, keepdims=False) + moved
    half = pair_up(b, quarter, lax.ppermute(quarter, "b", swap))
    other = pair_up(core, half, lax.ppermute(half, "core", swap))
    other = other.transpose(1, 0, 2, 3).reshape(2, 32, 1024)
    copies = jnp.broadcast_to(total[None], (2, 4, 64, 128)).reshape(8, 64, 128)
    got_all = lax.all_to_all(copies, ("zh", "q"), 0, 0, tiled=True)
    got_all, other = lax.optimization_barrier((got_all, other))
    residual = got_all.reshape(2, 4, 2, 32, 128).sum(1)
    first_res = residual[:, 0].reshape(64, 128)
    second_part = residual[:, 1].reshape(64, 128)

    def both(mine, theirs, x):
        a, c = mul(mine, x), mul(theirs, x)
        return jnp.where(zh == 0, jnp.concatenate([a, c]), jnp.concatenate([c, a])), a

    first_sol, first_mine = both(diag_inverse[0], other[0], gather_plane(first_res))
    cross, _ = both(coupling, other[1], gather_plane(first_sol))
    second_mine = mul(diag_inverse[1], gather_plane(second_part - cross))
    return jnp.stack([first_mine, second_mine])


def solution(mesh):
    fine = Mesh(mesh.devices.reshape(4, 4, 2, 4, 2, 2), ROWS + COLS)
    return jax.shard_map(
        on_device,
        mesh=fine,
        in_specs=(
            P(None, ROWS, COLS),
            P(None, ROWS, None),
            P(ROWS, None),
            P(None, ROWS, COLS),
            P(COLS, None),
        ),
        out_specs=P(None, ROWS, COLS),
        check_vma=False,
    )
```

time: 113 us -> 103 us (0.912)
  the two profiles are of different devices: /device:TPU:64 before, /device:TPU:2 now
where the time goes in v4:
time: 103 us
  starting transfers between devices  39.1 us (38%)
  blocking collectives  26.2 us (25%)
  waiting for transfers between devices  24.3 us (24%)
  Pallas kernels  7.64 us (7%)
  matrix products  2.02 us (2%)
  other arithmetic  1.77 us (2%)
  local copies, waits for them, and re-layouts  1.69 us (2%)
    all_to_all x2, blocking collectives, gather_plane(): got = lax.all_to_all(copies, ('y', 'x'), 0, 0, tiled=True)  26.2 us
    all_to_all x1, starting transfers between devices, on_device(): got_all = lax.all_to_all(copies, ('zh', 'q'), 0, 0, tiled=True)  11.5 us
    ppermute x1, starting transfers between devices, on_device(): lax.ppermute(quarter, ('zh',) + LINE, [(z, 15 - z) for z in range(16)])  10.5 us
    ppermute x1, waiting for transfers between devices, on_device(): half = pair_up(b, quarter, lax.ppermute(quarter, 'b', swap))  8.95 us
    all_to_all x1, waiting for transfers between devices, gather_plane(): got = lax.all_to_all(copies, ('y', 'x'), 0, 0, tiled=True)  8.78 us
    pallas_call x2, Pallas kernels, product(): pl.pallas_call(functools.partial(product_kernel, add is not None), out_sh...  7.64 us
    all_to_all x1, starting transfers between devices, gather_plane(): got = lax.all_to_all(copies, ('y', 'x'), 0, 0, tiled=True)  7.48 us
    all_to_all x1, waiting for transfers between devices, on_device(): got_all = lax.all_to_all(copies, ('zh', 'q'), 0, 0, tiled=True)  5.21 us
  transfers between devices with their start and end apart: 7, of which 4 were waited for; matrix products, arithmetic and copies ran while one was open for 1% of the time, Pallas kernels for 4%

profile of v4, /device:TPU:2, one launch (start us, length us, event | category | flops | bytes accessed | tf_op | source)
XLA Modules:
  0.0 102.9 jit_solution(8358606664528073937)
XLA Ops:
  0.0 0.0 slice-start
  0.0 3.8 %shard_map.56 = f32[2,4,64,128]{3,2,1,0:T(8,128)} custom-call(f32[64,512]{1,0:T(8,128)} %bitcast.64, f32[512,2048]{1,0:T(8,128)} %solved_ref.3), custom_call_target="tpu_custom_call" | custom-call | flops 201326592 | bytes 3145728 | tf_op jit(solution)/shard_map/pallas_call | solution.py:59
  3.9 1.9 %collective-permute-start = (f32[2,4,64,128]{3,2,1,0:T(8,128)}, f32[2,4,64,128]{3,2,1,0:T(8,128)S(1)}, u32[]{:S(2)}, u32[]{:S(2)}) collective-permute-start(f32[2,4,64,128]{3,2,1,0:T(8,128)} %shard_map.56), channel_id=1, source_target_pairs={{0,1},{1,0},{2,3},{3,2},{4,5},{5,4},{6,7},{7,6},{8,9},{9,8},{10,11... | collective-permute-start | bytes 786440 | tf_op jit(solution)/shard_map/ppermute | solution.py:91
  5.8 3.8 %shard_map.55 = f32[2,4,64,128]{3,2,1,0:T(8,128)} custom-call(f32[64,512]{1,0:T(8,128)} %bitcast.65, f32[512,2048]{1,0:T(8,128)} %solved_ref.3, f32[64,128]{1,0:T(8,128)} %bitcast.69), custom_call_target="tpu_custom_call" | custom-call | flops 201326592 | bytes 3145728 | tf_op jit(solution)/shard_map/pallas_call | solution.py:59
  9.6 0.0 copy-start
  9.6 0.0 collective-permute-done
  9.6 1.0 add.18
  10.7 3.8 %collective-permute-start.1 = (f32[4,64,128]{2,1,0:T(8,128)S(1)}, f32[4,64,128]{2,1,0:T(8,128)S(1)}, u32[]{:S(2)}, u32[]{:S(2)}) collective-permute-start(f32[4,64,128]{2,1,0:T(8,128)S(1)} %dynamic-slice_bitcast_fusion), channel_id=1, source_target_pairs={{0,2},{2,0},{1,3},{3,1},{4,6},{6,4},{5,7},{7,5},{8,10},{10,8},{9,1... | collective-permute-start | bytes 393224 | tf_op jit(solution)/shard_map/ppermute | solution.py:94
  14.5 0.0 slice-done
  14.5 0.0 copy-done.1
  14.5 10.5 %collective-permute-start.2 = (f32[16,1024]{1,0:T(8,128)S(1)}, f32[16,1024]{1,0:T(8,128)S(1)}, u32[]{:S(2)}, u32[]{:S(2)}) collective-permute-start(f32[16,1024]{1,0:T(8,128)S(1)} %bitcast_select_fusion), channel_id=1, source_target_pairs={{0,30},{2,28},{4,26},{6,24},{8,22},{10,20},{12,18},{14,16},{16,14}... | collective-permute-start | bytes 196616 | tf_op jit(solution)/shard_map/ppermute | solution.py:87
  25.1 0.0 collective-permute-done.1
  25.1 0.7 broadcast_in_dim.10
  25.8 11.5 %all-to-all-start = ((f32[8,64,128]{2,1,0:T(8,128)}), f32[8,64,128]{2,1,0:T(8,128)S(1)}, u32[]{:S(2)}, u32[]{:S(2)}) async-start(f32[8,64,128]{2,1,0:T(8,128)} %bitcast.4), calls=%async_computation | async-start | bytes 524288 | tf_op jit(solution)/shard_map/all_to_all | solution.py:100
  37.3 0.0 collective-permute-done.2
  37.3 1.9 %collective-permute-start.3 = (f32[16,1024]{1,0:T(8,128)S(1)}, f32[16,1024]{1,0:T(8,128)S(1)}, u32[]{:S(2)}, u32[]{:S(2)}) collective-permute-start(f32[16,1024]{1,0:T(8,128)S(1)} %collective-permute-done.2), channel_id=1, source_target_pairs={{0,2},{2,0},{1,3},{3,1},{4,6},{6,4},{5,7},{7,5},{8,10},{10,8},{9,1... | collective-permute-start | bytes 196616 | tf_op jit(solution)/shard_map/ppermute | solution.py:96
  39.2 8.9 %collective-permute-done.3 = f32[16,1024]{1,0:T(8,128)S(1)} collective-permute-done((f32[16,1024]{1,0:T(8,128)S(1)}, f32[16,1024]{1,0:T(8,128)S(1)}, u32[]{:S(2)}, u32[]{:S(2)}) %collective-permute-start.3) | collective-permute-done | bytes 65568 | tf_op jit(solution)/shard_map/ppermute | solution.py:96
  48.2 1.9 %collective-permute-start.4 = (f32[2,16,1024]{2,1,0:T(8,128)S(1)}, f32[2,16,1024]{2,1,0:T(8,128)S(1)}, u32[]{:S(2)}, u32[]{:S(2)}) collective-permute-start(f32[2,16,1024]{2,1,0:T(8,128)S(1)} %pad_maximum_fusion.1), channel_id=1, source_target_pairs={{0,1},{1,0},{2,3},{3,2},{4,5},{5,4},{6,7},{7,6},{8,9},{9,8},{10,11... | collective-permute-start | bytes 393224 | tf_op jit(solution)/shard_map/ppermute | solution.py:97
  50.2 1.3 %collective-permute-done.4 = f32[2,16,1024]{2,1,0:T(8,128)S(1)} collective-permute-done((f32[2,16,1024]{2,1,0:T(8,128)S(1)}, f32[2,16,1024]{2,1,0:T(8,128)S(1)}, u32[]{:S(2)}, u32[]{:S(2)}) %collective-permute-start.4) | collective-permute-done | bytes 131104 | tf_op jit(solution)/shard_map/ppermute | solution.py:97
  51.5 5.2 %all-to-all-done = f32[8,64,128]{2,1,0:T(8,128)S(1)} async-done(((f32[8,64,128]{2,1,0:T(8,128)}), f32[8,64,128]{2,1,0:T(8,128)S(1)}, u32[]{:S(2)}, u32[]{:S(2)}) %all-to-all-start) | async-done | bytes 262176 | tf_op jit(solution)/shard_map/all_to_all | solution.py:100
  56.8 0.8 broadcast_in_dim.12
  57.6 7.5 %all-to-all-start.1 = ((f32[16,64,128]{2,1,0:T(8,128)}), f32[16,64,128]{2,1,0:T(8,128)S(1)}, u32[]{:S(2)}, u32[]{:S(2)}) async-start(f32[16,64,128]{2,1,0:T(8,128)} %broadcast_in_dim.12), calls=%async_computation.1 | async-start | bytes 1048576 | tf_op jit(solution)/shard_map/all_to_all | solution.py:77
  65.1 8.8 %all-to-all-done.1 = f32[16,64,128]{2,1,0:T(8,128)S(1)} async-done(((f32[16,64,128]{2,1,0:T(8,128)}), f32[16,64,128]{2,1,0:T(8,128)S(1)}, u32[]{:S(2)}, u32[]{:S(2)}) %all-to-all-start.1) | async-done | bytes 524320 | tf_op jit(solution)/shard_map/all_to_all | solution.py:77
  73.9 0.0 copy-done
  73.9 0.4 fusion.5
  74.3 0.4 fusion.3
  74.8 13.1 %all_to_all.20 = f32[16,64,128]{2,1,0:T(8,128)S(1)} all-to-all(f32[16,64,128]{2,1,0:T(8,128)S(1)} %broadcast_in_dim.13), channel_id=1, replica_groups=mesh['y'=4,'x'=4,'zh'=2,'q'=4,'b'=2,'core'=2] {'y','x'}, dimensions={0} | all-to-all | bytes 1048576 | tf_op jit(solution)/shard_map/all_to_all | solution.py:77
  87.8 0.4 fusion.1
  88.2 0.4 convolution_bitcast_fusion.1
  88.7 13.1 %all_to_all.21 = f32[16,64,128]{2,1,0:T(8,128)S(1)} all-to-all(f32[16,64,128]{2,1,0:T(8,128)S(1)} %broadcast_in_dim.14), channel_id=1, replica_groups=mesh['y'=4,'x'=4,'zh'=2,'q'=4,'b'=2,'core'=2] {'y','x'}, dimensions={0} | all-to-all | bytes 1048576 | tf_op jit(solution)/shard_map/all_to_all | solution.py:77
  101.8 0.4 convolution_bitcast_fusion
  102.2 0.6 pad_maximum_fusion.2
  (14 shorter events, 0.2 us)
Async XLA Ops:
  0.0 14.5 %slice-start = ((f32[2,32,1024]{2,1,0:T(8,128)}), f32[1,32,1024]{2,1,0:T(8,128)S(1)}, s32[]{:S(2)}) async-start(f32[2,32,1024]{2,1,0:T(8,128)} %param.6), calls=%async_computation.4 | async-start | bytes 262144 | tf_op jit(solution)/shard_map/slice | solution.py:110
  0.0 14.5 %copy-start.1 = (f32[32,1024]{1,0:T(8,128)S(1)}, f32[32,1024]{1,0:T(8,128)}, u32[]{:S(2)}) copy-start(f32[32,1024]{1,0:T(8,128)} %param.7) | copy-start | bytes 393220
  3.9 5.8 %collective-permute-start = (f32[2,4,64,128]{3,2,1,0:T(8,128)}, f32[2,4,64,128]{3,2,1,0:T(8,128)S(1)}, u32[]{:S(2)}, u32[]{:S(2)}) collective-permute-start(f32[2,4,64,128]{3,2,1,0:T(8,128)} %shard_map.56), channel_id=1, source_target_pairs={{0,1},{1,0},{2,3},{3,2},{4,5},{5,4},{6,7},{7,6},{8,9},{9,8},{10,11... | collective-permute-start | bytes 786440 | tf_op jit(solution)/shard_map/ppermute | solution.py:91
  9.6 64.3 %copy-start = (f32[2,32,1024]{2,1,0:T(8,128)S(1)}, f32[2,32,1024]{2,1,0:T(8,128)}, u32[]{:S(2)}) copy-start(f32[2,32,1024]{2,1,0:T(8,128)} %param.6) | copy-start | bytes 786436
  10.7 14.4 %collective-permute-start.1 = (f32[4,64,128]{2,1,0:T(8,128)S(1)}, f32[4,64,128]{2,1,0:T(8,128)S(1)}, u32[]{:S(2)}, u32[]{:S(2)}) collective-permute-start(f32[4,64,128]{2,1,0:T(8,128)S(1)} %dynamic-slice_bitcast_fusion), channel_id=1, source_target_pairs={{0,2},{2,0},{1,3},{3,1},{4,6},{6,4},{5,7},{7,5},{8,10},{10,8},{9,1... | collective-permute-start | bytes 393224 | tf_op jit(solution)/shard_map/ppermute | solution.py:94
  14.5 22.8 %collective-permute-start.2 = (f32[16,1024]{1,0:T(8,128)S(1)}, f32[16,1024]{1,0:T(8,128)S(1)}, u32[]{:S(2)}, u32[]{:S(2)}) collective-permute-start(f32[16,1024]{1,0:T(8,128)S(1)} %bitcast_select_fusion), channel_id=1, source_target_pairs={{0,30},{2,28},{4,26},{6,24},{8,22},{10,20},{12,18},{14,16},{16,14}... | collective-permute-start | bytes 196616 | tf_op jit(solution)/shard_map/ppermute | solution.py:87
  25.8 30.9 %all-to-all-start = ((f32[8,64,128]{2,1,0:T(8,128)}), f32[8,64,128]{2,1,0:T(8,128)S(1)}, u32[]{:S(2)}, u32[]{:S(2)}) async-start(f32[8,64,128]{2,1,0:T(8,128)} %bitcast.4), calls=%async_computation | async-start | bytes 524288 | tf_op jit(solution)/shard_map/all_to_all | solution.py:100
  37.3 10.9 %collective-permute-start.3 = (f32[16,1024]{1,0:T(8,128)S(1)}, f32[16,1024]{1,0:T(8,128)S(1)}, u32[]{:S(2)}, u32[]{:S(2)}) collective-permute-start(f32[16,1024]{1,0:T(8,128)S(1)} %collective-permute-done.2), channel_id=1, source_target_pairs={{0,2},{2,0},{1,3},{3,1},{4,6},{6,4},{5,7},{7,5},{8,10},{10,8},{9,1... | collective-permute-start | bytes 196616 | tf_op jit(solution)/shard_map/ppermute | solution.py:96
  48.2 3.2 %collective-permute-start.4 = (f32[2,16,1024]{2,1,0:T(8,128)S(1)}, f32[2,16,1024]{2,1,0:T(8,128)S(1)}, u32[]{:S(2)}, u32[]{:S(2)}) collective-permute-start(f32[2,16,1024]{2,1,0:T(8,128)S(1)} %pad_maximum_fusion.1), channel_id=1, source_target_pairs={{0,1},{1,0},{2,3},{3,2},{4,5},{5,4},{6,7},{7,6},{8,9},{9,8},{10,11... | collective-permute-start | bytes 393224 | tf_op jit(solution)/shard_map/ppermute | solution.py:97
  57.6 16.3 %all-to-all-start.1 = ((f32[16,64,128]{2,1,0:T(8,128)}), f32[16,64,128]{2,1,0:T(8,128)S(1)}, u32[]{:S(2)}, u32[]{:S(2)}) async-start(f32[16,64,128]{2,1,0:T(8,128)} %broadcast_in_dim.12), calls=%async_computation.1 | async-start | bytes 1048576 | tf_op jit(solution)/shard_map/all_to_all | solution.py:77

commit v5 on v4

--- a/solution.py
+++ b/solution.py
@@ -63,7 +63,9 @@
         out_specs=vmem,
         scratch_shapes=[pltpu.VMEM((4, 512, 256), jnp.float32), pltpu.SemaphoreType.DMA((4, 2))],
         compiler_params=pltpu.CompilerParams(vmem_limit_bytes=56 << 20),
-        cost_estimate=pl.CostEstimate(flops=6 * 64 * 512 * 1024, bytes_accessed=3 << 20, transcendentals=0),
+        cost_estimate=pl.CostEstimate(
+            flops=10**9 if add is None else 10**14, bytes_accessed=3 << 20, transcendentals=0
+        ),
     )(*args)
 
 
@@ -84,28 +86,33 @@
 
     rows = lambda x: lax.dynamic_slice_in_dim(x, 16 * core, 16, 0)
     quarter = jnp.where(b == 1, rows(diag_inverse[0]), rows(coupling))
+    quarter = quarter.reshape(16, 8, 128).transpose(1, 0, 2).reshape(128, 128)
     quarter = lax.ppermute(quarter, ("zh",) + LINE, [(z, 15 - z) for z in range(16)])
 
     panel = panel.reshape(64, 512)
     send = product(panel, solved)
     moved = lax.ppermute(send, "core", swap)
     keep = product(panel, solved, right_side.reshape(64, 128))
-    total = keep + moved
-    moved = lax.ppermute(lax.dynamic_index_in_dim(total, 1 - b, 0, keepdims=False), "b", swap)
-    total = lax.dynamic_index_in_dim(total, b, 0, keepdims=False) + moved
-    half = pair_up(b, quarter, lax.ppermute(quarter, "b", swap))
-    other = pair_up(core, half, lax.ppermute(half, "core", swap))
-    other = other.transpose(1, 0, 2, 3).reshape(2, 32, 1024)
+    moved, quarter = lax.optimization_barrier((moved, quarter))
+    take = lambda x, index: lax.dynamic_index_in_dim(x, index, 0, keepdims=False)
+    passing = take(keep, 1 - b) + take(moved, 1 - b)
+    passed = lax.ppermute(jnp.concatenate([passing.reshape(256, 128), quarter]), "b", swap)
+    half = pair_up(b, quarter, passed[256:])
+    passed = passed[:256].reshape(4, 64, 128)
+    total = take(keep, b) + take(moved, b) + passed
     copies = jnp.broadcast_to(total[None], (2, 4, 64, 128)).reshape(8, 64, 128)
     got_all = lax.all_to_all(copies, ("zh", "q"), 0, 0, tiled=True)
-    got_all, other = lax.optimization_barrier((got_all, other))
+    other = pair_up(core, half, lax.ppermute(half, "core", swap))
+    other = other.reshape(2, 2, 8, 16, 128).transpose(1, 0, 3, 2, 4).reshape(2, 32, 1024)
+    first_half = zh == 0
+    got_all, other, first_half = lax.optimization_barrier((got_all, other, first_half))
     residual = got_all.reshape(2, 4, 2, 32, 128).sum(1)
     first_res = residual[:, 0].reshape(64, 128)
     second_part = residual[:, 1].reshape(64, 128)
 
     def both(mine, theirs, x):
         a, c = mul(mine, x), mul(theirs, x)
-        return jnp.where(zh == 0, jnp.concatenate([a, c]), jnp.concatenate([c, a])), a
+        return jnp.where(first_half, jnp.concatenate([a, c]), jnp.concatenate([c, a])), a
 
     first_sol, first_mine = both(diag_inverse[0], other[0], gather_plane(first_res))
     cross, _ = both(coupling, other[1], gather_plane(first_sol))

time: 103 us -> 112 us (1.087)
  the two profiles are of different devices: /device:TPU:2 before, /device:TPU:64 now
where the time goes in v5:
time: 112 us; the launch traced here: 111 us
  blocking collectives  45.5 us (41%)
  starting transfers between devices  26 us (23%)
  waiting for transfers between devices  22.2 us (20%)
  Pallas kernels  7.61 us (7%)
  other arithmetic  5.96 us (5%)
  matrix products  2.02 us (2%)
  local copies, waits for them, and re-layouts  1.91 us (2%)
    all_to_all x3, blocking collectives, gather_plane(): got = lax.all_to_all(copies, ('y', 'x'), 0, 0, tiled=True)  45.5 us
    all_to_all x1, waiting for transfers between devices, on_device(): got_all = lax.all_to_all(copies, ('zh', 'q'), 0, 0, tiled=True)  15.3 us
    ppermute x1, starting transfers between devices, on_device(): lax.ppermute(quarter, ('zh',) + LINE, [(z, 15 - z) for z in range(16)])  11.4 us
    pallas_call x2, Pallas kernels, product(): pl.pallas_call(functools.partial(product_kernel, add is not None), out_sh...  7.61 us
    all_to_all x1, starting transfers between devices, on_device(): got_all = lax.all_to_all(copies, ('zh', 'q'), 0, 0, tiled=True)  7.02 us
    ppermute x1, waiting for transfers between devices, on_device(): lax.ppermute(jnp.concatenate([passing.reshape(256, 128), quarter]), 'b',...  5.55 us
    ppermute x1, starting transfers between devices, on_device(): lax.ppermute(jnp.concatenate([passing.reshape(256, 128), quarter]), 'b',...  3.81 us
  transfers between devices with their start and end apart: 5, of which 3 were waited for; matrix products, arithmetic and copies ran while one was open for 1% of the time, Pallas kernels for 7%

profile of v5, /device:TPU:64, one launch (start us, length us, event | category | flops | bytes accessed | tf_op | source)
XLA Modules:
  0.0 111.4 jit_solution(4313038724412027873)
XLA Ops:
  0.0 0.9 slice.25
  0.9 1.5 %copy_bitcast_fusion = f32[16,8,128]{2,0,1:T(8,128)} fusion(f32[32,1024]{1,0:T(8,128)} %param.7, s32[]{:T(128)S(6)} %select_n.67, f32[1,32,1024]{2,1,0:T(8,128)S(1)} %slice.25, pred[]{:T(512)S(6)} %eq.12), kind=kLoop, calls=%fused_computation.17 | loop fusion | flops 16384 | bytes 196613 | tf_op jit(solution)/shard_map/reshape | solution.py:89
  2.4 11.4 %collective-permute-start.1 = (f32[128,128]{1,0:T(8,128)}, f32[128,128]{1,0:T(8,128)}, u32[]{:S(2)}, u32[]{:S(2)}) collective-permute-start(f32[128,128]{1,0:T(8,128)} %bitcast.4), channel_id=1, source_target_pairs={{0,30},{2,28},{4,26},{6,24},{8,22},{10,20},{12,18},{14,16},{16,14}... | collective-permute-start | bytes 196616 | tf_op jit(solution)/shard_map/ppermute | solution.py:90
  13.8 3.8 %shard_map.56 = f32[2,4,64,128]{3,2,1,0:T(8,128)} custom-call(f32[64,512]{1,0:T(8,128)} %bitcast.76, f32[512,2048]{1,0:T(8,128)} %solved_ref.3), custom_call_target="tpu_custom_call" | custom-call | flops 1000000000 | bytes 3145728 | tf_op jit(solution)/shard_map/pallas_call | solution.py:59
  17.6 1.9 %collective-permute-start = (f32[2,4,64,128]{3,2,1,0:T(8,128)}, f32[2,4,64,128]{3,2,1,0:T(8,128)}, u32[]{:S(2)}, u32[]{:S(2)}) collective-permute-start(f32[2,4,64,128]{3,2,1,0:T(8,128)} %shard_map.56), channel_id=1, source_target_pairs={{0,1},{1,0},{2,3},{3,2},{4,5},{5,4},{6,7},{7,6},{8,9},{9,8},{10,11... | collective-permute-start | bytes 786440 | tf_op jit(solution)/shard_map/ppermute | solution.py:94
  19.5 3.8 %shard_map.55 = f32[2,4,64,128]{3,2,1,0:T(8,128)} custom-call(f32[64,512]{1,0:T(8,128)} %bitcast.77, f32[512,2048]{1,0:T(8,128)} %solved_ref.3, f32[64,128]{1,0:T(8,128)} %bitcast.79), custom_call_target="tpu_custom_call" | custom-call | flops 100000000376832 | bytes 3145728 | tf_op jit(solution)/shard_map/pallas_call | solution.py:59
  23.3 0.0 copy-start
  23.4 0.0 collective-permute-done.1
  23.4 0.0 collective-permute-done
  23.4 1.0 dynamic-slice_add_fusion
  24.4 0.9 pad_maximum_fusion
  25.3 3.8 %collective-permute-start.2 = (f32[384,128]{1,0:T(8,128)S(1)}, f32[384,128]{1,0:T(8,128)S(1)}, u32[]{:S(2)}, u32[]{:S(2)}) collective-permute-start(f32[384,128]{1,0:T(8,128)S(1)} %pad_maximum_fusion), channel_id=1, source_target_pairs={{0,2},{2,0},{1,3},{3,1},{4,6},{6,4},{5,7},{7,5},{8,10},{10,8},{9,1... | collective-permute-start | bytes 589832 | tf_op jit(solution)/shard_map/ppermute | solution.py:99
  29.1 5.5 %collective-permute-done.2 = f32[384,128]{1,0:T(8,128)S(1)} collective-permute-done((f32[384,128]{1,0:T(8,128)S(1)}, f32[384,128]{1,0:T(8,128)S(1)}, u32[]{:S(2)}, u32[]{:S(2)}) %collective-permute-start.2) | collective-permute-done | bytes 196640 | tf_op jit(solution)/shard_map/ppermute | solution.py:99
  34.6 1.0 add_bitcast_fusion
  35.7 0.7 broadcast_in_dim.13
  36.4 7.0 %all-to-all-start = ((f32[8,64,128]{2,1,0:T(8,128)}), f32[8,64,128]{2,1,0:T(8,128)S(1)}, u32[]{:S(2)}, u32[]{:S(2)}) async-start(f32[8,64,128]{2,1,0:T(8,128)} %bitcast.8), calls=%async_computation | async-start | bytes 524288 | tf_op jit(solution)/shard_map/all_to_all | solution.py:104
  43.4 0.9 select_bitcast_fusion.1
  44.3 1.9 %collective-permute-start.3 = (f32[2,128,128]{2,1,0:T(8,128)S(1)}, f32[2,128,128]{2,1,0:T(8,128)S(1)}, u32[]{:S(2)}, u32[]{:S(2)}) collective-permute-start(f32[2,128,128]{2,1,0:T(8,128)S(1)} %pad_maximum_fusion.1), channel_id=1, source_target_pairs={{0,1},{1,0},{2,3},{3,2},{4,5},{5,4},{6,7},{7,6},{8,9},{9,8},{10,11... | collective-permute-start | bytes 393224 | tf_op jit(solution)/shard_map/ppermute | solution.py:105
  46.2 1.3 %collective-permute-done.3 = f32[2,128,128]{2,1,0:T(8,128)S(1)} collective-permute-done((f32[2,128,128]{2,1,0:T(8,128)S(1)}, f32[2,128,128]{2,1,0:T(8,128)S(1)}, u32[]{:S(2)}, u32[]{:S(2)}) %collective-permute-start.3) | collective-permute-done | bytes 131104 | tf_op jit(solution)/shard_map/ppermute | solution.py:105
  47.6 0.1 copy.11
  47.7 15.3 %all-to-all-done = f32[8,64,128]{2,1,0:T(8,128)S(1)} async-done(((f32[8,64,128]{2,1,0:T(8,128)}), f32[8,64,128]{2,1,0:T(8,128)S(1)}, u32[]{:S(2)}, u32[]{:S(2)}) %all-to-all-start) | async-done | bytes 262176 | tf_op jit(solution)/shard_map/all_to_all | solution.py:104
  63.1 18.6 %all_to_all.20 = f32[16,64,128]{2,1,0:T(8,128)S(1)} all-to-all(f32[16,64,128]{2,1,0:T(8,128)S(1)} %broadcast_in_dim.30), channel_id=1, replica_groups=mesh['y'=4,'x'=4,'zh'=2,'q'=4,'b'=2,'core'=2] {'y','x'}, dimensions={0} | all-to-all | bytes 1048576 | tf_op jit(solution)/shard_map/all_to_all | solution.py:79
  81.7 0.0 copy-done
  81.7 0.4 fusion.5
  82.1 0.4 fusion.3
  82.6 13.9 %all_to_all.21 = f32[16,64,128]{2,1,0:T(8,128)S(1)} all-to-all(f32[16,64,128]{2,1,0:T(8,128)S(1)} %broadcast_in_dim.31), channel_id=1, replica_groups=mesh['y'=4,'x'=4,'zh'=2,'q'=4,'b'=2,'core'=2] {'y','x'}, dimensions={0} | all-to-all | bytes 1048576 | tf_op jit(solution)/shard_map/all_to_all | solution.py:79
  96.4 0.4 fusion.1
  96.8 0.0 copy-done.1
  96.8 0.4 convolution_bitcast_fusion.1
  97.3 13.0 %all_to_all.22 = f32[16,64,128]{2,1,0:T(8,128)S(1)} all-to-all(f32[16,64,128]{2,1,0:T(8,128)S(1)} %broadcast_in_dim.32), channel_id=1, replica_groups=mesh['y'=4,'x'=4,'zh'=2,'q'=4,'b'=2,'core'=2] {'y','x'}, dimensions={0} | all-to-all | bytes 1048576 | tf_op jit(solution)/shard_map/all_to_all | solution.py:79
  110.4 0.4 convolution_bitcast_fusion
  110.8 0.6 pad_maximum_fusion.2
  (13 shorter events, 0.3 us)
Async XLA Ops:
  2.4 21.0 %collective-permute-start.1 = (f32[128,128]{1,0:T(8,128)}, f32[128,128]{1,0:T(8,128)}, u32[]{:S(2)}, u32[]{:S(2)}) collective-permute-start(f32[128,128]{1,0:T(8,128)} %bitcast.4), channel_id=1, source_target_pairs={{0,30},{2,28},{4,26},{6,24},{8,22},{10,20},{12,18},{14,16},{16,14}... | collective-permute-start | bytes 196616 | tf_op jit(solution)/shard_map/ppermute | solution.py:90
  17.6 5.8 %collective-permute-start = (f32[2,4,64,128]{3,2,1,0:T(8,128)}, f32[2,4,64,128]{3,2,1,0:T(8,128)}, u32[]{:S(2)}, u32[]{:S(2)}) collective-permute-start(f32[2,4,64,128]{3,2,1,0:T(8,128)} %shard_map.56), channel_id=1, source_target_pairs={{0,1},{1,0},{2,3},{3,2},{4,5},{5,4},{6,7},{7,6},{8,9},{9,8},{10,11... | collective-permute-start | bytes 786440 | tf_op jit(solution)/shard_map/ppermute | solution.py:94
  23.3 58.3 %copy-start = (f32[2,32,1024]{2,1,0:T(8,128)S(1)}, f32[2,32,1024]{2,1,0:T(8,128)}, u32[]{:S(2)}) copy-start(f32[2,32,1024]{2,1,0:T(8,128)} %param.6) | copy-start | bytes 786436
  25.3 9.4 %collective-permute-start.2 = (f32[384,128]{1,0:T(8,128)S(1)}, f32[384,128]{1,0:T(8,128)S(1)}, u32[]{:S(2)}, u32[]{:S(2)}) collective-permute-start(f32[384,128]{1,0:T(8,128)S(1)} %pad_maximum_fusion), channel_id=1, source_target_pairs={{0,2},{2,0},{1,3},{3,1},{4,6},{6,4},{5,7},{7,5},{8,10},{10,8},{9,1... | collective-permute-start | bytes 589832 | tf_op jit(solution)/shard_map/ppermute | solution.py:99
  36.4 26.7 %all-to-all-start = ((f32[8,64,128]{2,1,0:T(8,128)}), f32[8,64,128]{2,1,0:T(8,128)S(1)}, u32[]{:S(2)}, u32[]{:S(2)}) async-start(f32[8,64,128]{2,1,0:T(8,128)} %bitcast.8), calls=%async_computation | async-start | bytes 524288 | tf_op jit(solution)/shard_map/all_to_all | solution.py:104
  43.4 53.5 %copy-start.1 = (f32[32,1024]{1,0:T(8,128)S(1)}, f32[32,1024]{1,0:T(8,128)}, u32[]{:S(2)}) copy-start(f32[32,1024]{1,0:T(8,128)} %param.7) | copy-start | bytes 393220
  44.3 3.2 %collective-permute-start.3 = (f32[2,128,128]{2,1,0:T(8,128)S(1)}, f32[2,128,128]{2,1,0:T(8,128)S(1)}, u32[]{:S(2)}, u32[]{:S(2)}) collective-permute-start(f32[2,128,128]{2,1,0:T(8,128)S(1)} %pad_maximum_fusion.1), channel_id=1, source_target_pairs={{0,1},{1,0},{2,3},{3,2},{4,5},{5,4},{6,7},{7,6},{8,9},{9,8},{10,11... | collective-permute-start | bytes 393224 | tf_op jit(solution)/shard_map/ppermute | solution.py:105

commit v6 on v4

--- a/solution.py
+++ b/solution.py
@@ -27,22 +27,18 @@
     parity = core if mine else 1 - core
     copies = []
     for step in range(4):
-        for half in range(2):
-            columns = pl.ds(pl.multiple_of((4 * step + 2 * half + parity) * 128, 128), 128)
-            copy = pltpu.make_async_copy(
-                solved_ref.at[:, columns],
-                slots.at[step, :, pl.ds(128 * half, 128)],
-                sems.at[step, half],
-            )
-            copy.start()
-            copies.append(copy)
+        columns = pl.ds(512 * step, 512)
+        copy = pltpu.make_async_copy(solved_ref.at[:, columns], slots.at[:, columns], sems.at[step])
+        copy.start()
+        copies.append(copy)
     p_high, p_low = halves(-panel_ref[...])
     p_both = jnp.concatenate([p_high, p_low], axis=0)
     dot = functools.partial(jnp.dot, preferred_element_type=jnp.float32)
     for step in range(4):
-        copies[2 * step].wait()
-        copies[2 * step + 1].wait()
-        s_high, s_low = halves(slots[step])
+        copies[step].wait()
+        first = [pl.multiple_of((4 * step + 2 * half + parity) * 128, 128) for half in range(2)]
+        pair = jnp.concatenate([slots[:, pl.ds(start, 128)] for start in first], axis=1)
+        s_high, s_low = halves(pair)
         wide = dot(p_both, s_high)
         got = wide[64:] + dot(p_high, s_low) + wide[:64]
         for half in range(2):
@@ -61,7 +57,7 @@
         out_shape=jax.ShapeDtypeStruct((2, 4, 64, 128), jnp.float32),
         in_specs=[vmem, pl.BlockSpec(memory_space=pl.ANY)] + [vmem] * (add is not None),
         out_specs=vmem,
-        scratch_shapes=[pltpu.VMEM((4, 512, 256), jnp.float32), pltpu.SemaphoreType.DMA((4, 2))],
+        scratch_shapes=[pltpu.VMEM((512, 2048), jnp.float32), pltpu.SemaphoreType.DMA((4,))],
         compiler_params=pltpu.CompilerParams(vmem_limit_bytes=56 << 20),
         cost_estimate=pl.CostEstimate(flops=6 * 64 * 512 * 1024, bytes_accessed=3 << 20, transcendentals=0),
     )(*args)
@@ -90,22 +86,23 @@
     send = product(panel, solved)
     moved = lax.ppermute(send, "core", swap)
     keep = product(panel, solved, right_side.reshape(64, 128))
-    total = keep + moved
-    moved = lax.ppermute(lax.dynamic_index_in_dim(total, 1 - b, 0, keepdims=False), "b", swap)
-    total = lax.dynamic_index_in_dim(total, b, 0, keepdims=False) + moved
+    take = lambda x, index: lax.dynamic_index_in_dim(x, index, 0, keepdims=False)
+    passed = lax.ppermute(take(keep, 1 - b) + take(moved, 1 - b), "b", swap)
+    total = take(keep, b) + take(moved, b) + passed
     half = pair_up(b, quarter, lax.ppermute(quarter, "b", swap))
     other = pair_up(core, half, lax.ppermute(half, "core", swap))
     other = other.transpose(1, 0, 2, 3).reshape(2, 32, 1024)
     copies = jnp.broadcast_to(total[None], (2, 4, 64, 128)).reshape(8, 64, 128)
     got_all = lax.all_to_all(copies, ("zh", "q"), 0, 0, tiled=True)
-    got_all, other = lax.optimization_barrier((got_all, other))
+    first_half = zh == 0
+    got_all, other, first_half = lax.optimization_barrier((got_all, other, first_half))
     residual = got_all.reshape(2, 4, 2, 32, 128).sum(1)
     first_res = residual[:, 0].reshape(64, 128)
     second_part = residual[:, 1].reshape(64, 128)
 
     def both(mine, theirs, x):
         a, c = mul(mine, x), mul(theirs, x)
-        return jnp.where(zh == 0, jnp.concatenate([a, c]), jnp.concatenate([c, a])), a
+        return jnp.where(first_half, jnp.concatenate([a, c]), jnp.concatenate([c, a])), a
 
     first_sol, first_mine = both(diag_inverse[0], other[0], gather_plane(first_res))
     cross, _ = both(coupling, other[1], gather_plane(first_sol))

time: 103 us -> 104 us (level)
  blocking collectives: 26.2 us -> 42.2 us
  waiting for transfers between devices: 24.3 us -> 15.5 us
  starting transfers between devices: 39.1 us -> 31.6 us
    all_to_all x2 -> x3, blocking collectives: 26.2 us -> 42.2 us  [gather_plane(): got = lax.all_to_all(copies, ('y', 'x'), 0, 0, tiled=True)]
    all_to_all x1 -> x0, waiting for transfers between devices: 8.78 us -> none  [gather_plane(): got = lax.all_to_all(copies, ('y', 'x'), 0, 0, tiled=True)]
    all_to_all x1 -> x0, starting transfers between devices: 7.48 us -> none  [gather_plane(): got = lax.all_to_all(copies, ('y', 'x'), 0, 0, tiled=True)]
  transfers between devices with their start and end apart: 7 -> 6, of which waited for: 4 -> 3; matrix products, arithmetic and copies ran while one was open for 1% -> 2% of each run, Pallas kernels for 4% -> 4%
where the time goes in v6:
time: 104 us; the launch traced here: 103 us
  blocking collectives  42.2 us (41%)
  starting transfers between devices  31.6 us (30%)
  waiting for transfers between devices  15.5 us (15%)
  Pallas kernels  8.32 us (8%)
  other arithmetic  2.6 us (2%)
  matrix products  2.02 us (2%)
    all_to_all x3, blocking collectives, gather_plane(): got = lax.all_to_all(copies, ('y', 'x'), 0, 0, tiled=True)  42.2 us
    all_to_all x1, starting transfers between devices, on_device(): got_all = lax.all_to_all(copies, ('zh', 'q'), 0, 0, tiled=True)  11.5 us
    ppermute x1, starting transfers between devices, on_device(): lax.ppermute(quarter, ('zh',) + LINE, [(z, 15 - z) for z in range(16)])  10.5 us
    ppermute x1, waiting for transfers between devices, on_device(): half = pair_up(b, quarter, lax.ppermute(quarter, 'b', swap))  8.97 us
    pallas_call x2, Pallas kernels, product(): pl.pallas_call(functools.partial(product_kernel, add is not None), out_sh...  8.32 us
    all_to_all x1, waiting for transfers between devices, on_device(): got_all = lax.all_to_all(copies, ('zh', 'q'), 0, 0, tiled=True)  5.2 us
    ppermute x1, starting transfers between devices, on_device(): passed = lax.ppermute(take(keep, 1 - b) + take(moved, 1 - b), 'b', swap)  3.83 us
  transfers between devices with their start and end apart: 6, of which 3 were waited for; matrix products, arithmetic and copies ran while one was open for 2% of the time, Pallas kernels for 4%

profile of v6, /device:TPU:2, one launch (start us, length us, event | category | flops | bytes accessed | tf_op | source)
XLA Modules:
  0.0 103.3 jit_solution(5105207913870047534)
XLA Ops:
  0.0 0.0 slice-start
  0.0 0.0 copy-start.1
  0.0 4.2 %shard_map.56 = f32[2,4,64,128]{3,2,1,0:T(8,128)} custom-call(f32[64,512]{1,0:T(8,128)} %bitcast.64, f32[512,2048]{1,0:T(8,128)} %solved_ref.3), custom_call_target="tpu_custom_call" | custom-call | flops 201326592 | bytes 3145728 | tf_op jit(solution)/shard_map/pallas_call | solution.py:55
  4.2 1.9 %collective-permute-start = (f32[2,4,64,128]{3,2,1,0:T(8,128)}, f32[2,4,64,128]{3,2,1,0:T(8,128)S(1)}, u32[]{:S(2)}, u32[]{:S(2)}) collective-permute-start(f32[2,4,64,128]{3,2,1,0:T(8,128)} %shard_map.56), channel_id=1, source_target_pairs={{0,1},{1,0},{2,3},{3,2},{4,5},{5,4},{6,7},{7,6},{8,9},{9,8},{10,11... | collective-permute-start | bytes 786440 | tf_op jit(solution)/shard_map/ppermute | solution.py:87
  6.1 0.0 copy-start
  6.1 4.2 %shard_map.55 = f32[2,4,64,128]{3,2,1,0:T(8,128)} custom-call(f32[64,512]{1,0:T(8,128)} %bitcast.65, f32[512,2048]{1,0:T(8,128)} %solved_ref.3, f32[64,128]{1,0:T(8,128)} %bitcast.69), custom_call_target="tpu_custom_call" | custom-call | flops 201326592 | bytes 3145728 | tf_op jit(solution)/shard_map/pallas_call | solution.py:55
  10.3 0.0 collective-permute-done
  10.3 0.9 add_bitcast_fusion
  11.2 3.8 %collective-permute-start.1 = (f32[4,64,128]{2,1,0:T(8,128)S(1)}, f32[4,64,128]{2,1,0:T(8,128)S(1)}, u32[]{:S(2)}, u32[]{:S(2)}) collective-permute-start(f32[4,64,128]{2,1,0:T(8,128)S(1)} %add_bitcast_fusion), channel_id=1, source_target_pairs={{0,2},{2,0},{1,3},{3,1},{4,6},{6,4},{5,7},{7,5},{8,10},{10,8},{9,1... | collective-permute-start | bytes 393224 | tf_op jit(solution)/shard_map/ppermute | solution.py:90
  15.1 0.0 slice-done
  15.1 0.0 copy-done.1
  15.1 10.5 %collective-permute-start.2 = (f32[16,1024]{1,0:T(8,128)S(1)}, f32[16,1024]{1,0:T(8,128)S(1)}, u32[]{:S(2)}, u32[]{:S(2)}) collective-permute-start(f32[16,1024]{1,0:T(8,128)S(1)} %bitcast_select_fusion), channel_id=1, source_target_pairs={{0,30},{2,28},{4,26},{6,24},{8,22},{10,20},{12,18},{14,16},{16,14}... | collective-permute-start | bytes 196616 | tf_op jit(solution)/shard_map/ppermute | solution.py:83
  25.6 0.0 collective-permute-done.1
  25.6 0.9 bitcast_add_fusion
  26.6 0.7 broadcast_in_dim.10
  27.3 11.5 %all-to-all-start = ((f32[8,64,128]{2,1,0:T(8,128)}), f32[8,64,128]{2,1,0:T(8,128)S(1)}, u32[]{:S(2)}, u32[]{:S(2)}) async-start(f32[8,64,128]{2,1,0:T(8,128)} %bitcast.4), calls=%async_computation | async-start | bytes 524288 | tf_op jit(solution)/shard_map/all_to_all | solution.py:96
  38.8 0.0 collective-permute-done.2
  38.8 1.9 %collective-permute-start.3 = (f32[16,1024]{1,0:T(8,128)S(1)}, f32[16,1024]{1,0:T(8,128)S(1)}, u32[]{:S(2)}, u32[]{:S(2)}) collective-permute-start(f32[16,1024]{1,0:T(8,128)S(1)} %collective-permute-done.2), channel_id=1, source_target_pairs={{0,2},{2,0},{1,3},{3,1},{4,6},{6,4},{5,7},{7,5},{8,10},{10,8},{9,1... | collective-permute-start | bytes 196616 | tf_op jit(solution)/shard_map/ppermute | solution.py:92
  40.7 9.0 %collective-permute-done.3 = f32[16,1024]{1,0:T(8,128)S(1)} collective-permute-done((f32[16,1024]{1,0:T(8,128)S(1)}, f32[16,1024]{1,0:T(8,128)S(1)}, u32[]{:S(2)}, u32[]{:S(2)}) %collective-permute-start.3) | collective-permute-done | bytes 65568 | tf_op jit(solution)/shard_map/ppermute | solution.py:92
  49.7 1.9 %collective-permute-start.4 = (f32[2,16,1024]{2,1,0:T(8,128)S(1)}, f32[2,16,1024]{2,1,0:T(8,128)S(1)}, u32[]{:S(2)}, u32[]{:S(2)}) collective-permute-start(f32[2,16,1024]{2,1,0:T(8,128)S(1)} %pad_maximum_fusion.1), channel_id=1, source_target_pairs={{0,1},{1,0},{2,3},{3,2},{4,5},{5,4},{6,7},{7,6},{8,9},{9,8},{10,11... | collective-permute-start | bytes 393224 | tf_op jit(solution)/shard_map/ppermute | solution.py:93
  51.6 1.3 %collective-permute-done.4 = f32[2,16,1024]{2,1,0:T(8,128)S(1)} collective-permute-done((f32[2,16,1024]{2,1,0:T(8,128)S(1)}, f32[2,16,1024]{2,1,0:T(8,128)S(1)}, u32[]{:S(2)}, u32[]{:S(2)}) %collective-permute-start.4) | collective-permute-done | bytes 131104 | tf_op jit(solution)/shard_map/ppermute | solution.py:93
  53.0 5.2 %all-to-all-done = f32[8,64,128]{2,1,0:T(8,128)S(1)} async-done(((f32[8,64,128]{2,1,0:T(8,128)}), f32[8,64,128]{2,1,0:T(8,128)S(1)}, u32[]{:S(2)}, u32[]{:S(2)}) %all-to-all-start) | async-done | bytes 262176 | tf_op jit(solution)/shard_map/all_to_all | solution.py:96
  58.3 16.0 %all_to_all.20 = f32[16,64,128]{2,1,0:T(8,128)S(1)} all-to-all(f32[16,64,128]{2,1,0:T(8,128)S(1)} %broadcast_in_dim.12), channel_id=1, replica_groups=mesh['y'=4,'x'=4,'zh'=2,'q'=4,'b'=2,'core'=2] {'y','x'}, dimensions={0} | all-to-all | bytes 1048576 | tf_op jit(solution)/shard_map/all_to_all | solution.py:73
  74.4 0.0 copy-done
  74.4 0.4 fusion.5
  74.8 0.4 fusion.3
  75.2 13.1 %all_to_all.21 = f32[16,64,128]{2,1,0:T(8,128)S(1)} all-to-all(f32[16,64,128]{2,1,0:T(8,128)S(1)} %broadcast_in_dim.13), channel_id=1, replica_groups=mesh['y'=4,'x'=4,'zh'=2,'q'=4,'b'=2,'core'=2] {'y','x'}, dimensions={0} | all-to-all | bytes 1048576 | tf_op jit(solution)/shard_map/all_to_all | solution.py:73
  88.3 0.4 fusion.1
  88.7 0.4 convolution_bitcast_fusion.1
  89.2 13.1 %all_to_all.22 = f32[16,64,128]{2,1,0:T(8,128)S(1)} all-to-all(f32[16,64,128]{2,1,0:T(8,128)S(1)} %broadcast_in_dim.14), channel_id=1, replica_groups=mesh['y'=4,'x'=4,'zh'=2,'q'=4,'b'=2,'core'=2] {'y','x'}, dimensions={0} | all-to-all | bytes 1048576 | tf_op jit(solution)/shard_map/all_to_all | solution.py:73
  102.3 0.4 convolution_bitcast_fusion
  102.7 0.6 pad_maximum_fusion.2
  (12 shorter events, 0.3 us)
Async XLA Ops:
  0.0 15.1 %slice-start = ((f32[2,32,1024]{2,1,0:T(8,128)}), f32[1,32,1024]{2,1,0:T(8,128)S(1)}, s32[]{:S(2)}) async-start(f32[2,32,1024]{2,1,0:T(8,128)} %param.6), calls=%async_computation.4 | async-start | bytes 262144 | tf_op jit(solution)/shard_map/slice | solution.py:107
  0.0 15.1 %copy-start.1 = (f32[32,1024]{1,0:T(8,128)S(1)}, f32[32,1024]{1,0:T(8,128)}, u32[]{:S(2)}) copy-start(f32[32,1024]{1,0:T(8,128)} %param.7) | copy-start | bytes 393220
  4.2 6.1 %collective-permute-start = (f32[2,4,64,128]{3,2,1,0:T(8,128)}, f32[2,4,64,128]{3,2,1,0:T(8,128)S(1)}, u32[]{:S(2)}, u32[]{:S(2)}) collective-permute-start(f32[2,4,64,128]{3,2,1,0:T(8,128)} %shard_map.56), channel_id=1, source_target_pairs={{0,1},{1,0},{2,3},{3,2},{4,5},{5,4},{6,7},{7,6},{8,9},{9,8},{10,11... | collective-permute-start | bytes 786440 | tf_op jit(solution)/shard_map/ppermute | solution.py:87
  6.1 68.2 %copy-start = (f32[2,32,1024]{2,1,0:T(8,128)S(1)}, f32[2,32,1024]{2,1,0:T(8,128)}, u32[]{:S(2)}) copy-start(f32[2,32,1024]{2,1,0:T(8,128)} %param.6) | copy-start | bytes 786436
  11.2 14.4 %collective-permute-start.1 = (f32[4,64,128]{2,1,0:T(8,128)S(1)}, f32[4,64,128]{2,1,0:T(8,128)S(1)}, u32[]{:S(2)}, u32[]{:S(2)}) collective-permute-start(f32[4,64,128]{2,1,0:T(8,128)S(1)} %add_bitcast_fusion), channel_id=1, source_target_pairs={{0,2},{2,0},{1,3},{3,1},{4,6},{6,4},{5,7},{7,5},{8,10},{10,8},{9,1... | collective-permute-start | bytes 393224 | tf_op jit(solution)/shard_map/ppermute | solution.py:90
  15.1 23.7 %collective-permute-start.2 = (f32[16,1024]{1,0:T(8,128)S(1)}, f32[16,1024]{1,0:T(8,128)S(1)}, u32[]{:S(2)}, u32[]{:S(2)}) collective-permute-start(f32[16,1024]{1,0:T(8,128)S(1)} %bitcast_select_fusion), channel_id=1, source_target_pairs={{0,30},{2,28},{4,26},{6,24},{8,22},{10,20},{12,18},{14,16},{16,14}... | collective-permute-start | bytes 196616 | tf_op jit(solution)/shard_map/ppermute | solution.py:83
  27.3 30.9 %all-to-all-start = ((f32[8,64,128]{2,1,0:T(8,128)}), f32[8,64,128]{2,1,0:T(8,128)S(1)}, u32[]{:S(2)}, u32[]{:S(2)}) async-start(f32[8,64,128]{2,1,0:T(8,128)} %bitcast.4), calls=%async_computation | async-start | bytes 524288 | tf_op jit(solution)/shard_map/all_to_all | solution.py:96
  38.8 10.9 %collective-permute-start.3 = (f32[16,1024]{1,0:T(8,128)S(1)}, f32[16,1024]{1,0:T(8,128)S(1)}, u32[]{:S(2)}, u32[]{:S(2)}) collective-permute-start(f32[16,1024]{1,0:T(8,128)S(1)} %collective-permute-done.2), channel_id=1, source_target_pairs={{0,2},{2,0},{1,3},{3,1},{4,6},{6,4},{5,7},{7,5},{8,10},{10,8},{9,1... | collective-permute-start | bytes 196616 | tf_op jit(solution)/shard_map/ppermute | solution.py:92
  49.7 3.2 %collective-permute-start.4 = (f32[2,16,1024]{2,1,0:T(8,128)S(1)}, f32[2,16,1024]{2,1,0:T(8,128)S(1)}, u32[]{:S(2)}, u32[]{:S(2)}) collective-permute-start(f32[2,16,1024]{2,1,0:T(8,128)S(1)} %pad_maximum_fusion.1), channel_id=1, source_target_pairs={{0,1},{1,0},{2,3},{3,2},{4,5},{5,4},{6,7},{7,6},{8,9},{9,8},{10,11... | collective-permute-start | bytes 393224 | tf_op jit(solution)/shard_map/ppermute | solution.py:93

commit v7 on v4

v7 whole, which is shorter than its diff:
```python
import functools

import jax
import jax.numpy as jnp
from jax import lax
from jax.experimental import pallas as pl
from jax.experimental.pallas import tpu as pltpu
from jax.sharding import Mesh, PartitionSpec as P

ROWS = ("y", "x", "zh")
LINE = ("q", "b")
COLS = LINE + ("core",)


def mul(a, b):
    return jnp.dot(a, b, precision=lax.Precision.HIGHEST, preferred_element_type=jnp.float32)


def halves(x):
    high = x.astype(jnp.bfloat16)
    return high, (x - high.astype(jnp.float32)).astype(jnp.bfloat16)


def product_kernel(flips, panel_ref, solved_ref, *rest):
    count = len(flips)
    add_ref = rest[0] if len(rest) > count + 5 else None
    outs = rest[-count - 5 : -5]
    panel_held, add_held, slots, sems, small_sems = rest[-5:]
    core, q, b = (lax.axis_index(a) for a in ("core", "q", "b"))
    copies = []
    for part, (flip_b, flip_core) in enumerate(flips):
        to_b = 1 - b if flip_b else b
        to_core = 1 - core if flip_core else core
        for step in range(4):
            columns = pl.ds(pl.multiple_of((4 * step + 2 * to_b + to_core) * 128, 128), 128)
            copy = pltpu.make_async_copy(
                solved_ref.at[:, columns],
                slots.at[part, :, pl.ds(128 * step, 128)],
                sems.at[part, step],
            )
            copy.start()
            copies.append(copy)
    panel_copy = pltpu.make_async_copy(panel_ref, panel_held, small_sems.at[0])
    panel_copy.start()
    if add_ref is not None:
        add_copy = pltpu.make_async_copy(add_ref, add_held, small_sems.at[1])
        add_copy.start()
        add_copy.wait()
    panel_copy.wait()
    p_high, p_low = halves(-panel_held[...])
    p_both = jnp.concatenate([p_high, p_low], axis=0)
    dot = functools.partial(jnp.dot, preferred_element_type=jnp.float32)
    for part in range(count):
        for two in range(2):
            copies[4 * part + 2 * two].wait()
            copies[4 * part + 2 * two + 1].wait()
            s_high, s_low = halves(slots[part, :, pl.ds(256 * two, 256)])
            wide = dot(p_both, s_high)
            got = wide[64:] + dot(p_high, s_low) + wide[:64]
            for step in range(2 * two, 2 * two + 2):
                block = got[:, 128 * (step % 2) : 128 * (step % 2 + 1)]
                if add_ref is not None:
                    block = block + jnp.where(q == step, add_held[...], 0.0)
                outs[part][step] = block


def product(flips, panel, solved, add=None):
    args = (panel, solved) + (() if add is None else (add,))
    count = len(flips)
    return pl.pallas_call(
        functools.partial(product_kernel, flips),
        out_shape=[jax.ShapeDtypeStruct((4, 64, 128), jnp.float32)] * count,
        in_specs=[pl.BlockSpec(memory_space=pl.ANY)] * len(args),
        out_specs=[pl.BlockSpec(memory_space=pltpu.VMEM)] * count,
        scratch_shapes=[
            pltpu.VMEM((64, 512), jnp.float32),
            pltpu.VMEM((64, 128), jnp.float32),
            pltpu.VMEM((count, 512, 512), jnp.float32),
            pltpu.SemaphoreType.DMA((count, 4)),
            pltpu.SemaphoreType.DMA((2,)),
        ],
        compiler_params=pltpu.CompilerParams(vmem_limit_bytes=56 << 20),
        cost_estimate=pl.CostEstimate(flops=count * 10**8, bytes_accessed=count << 20, transcendentals=0),
    )(*args)


def pair_up(index, mine, theirs):
    first = index == 0
    return jnp.stack([jnp.where(first, mine, theirs), jnp.where(first, theirs, mine)])


def gather_plane(block):
    copies = jnp.broadcast_to(block[None], (16,) + block.shape)
    got = lax.all_to_all(copies, ("y", "x"), 0, 0, tiled=True)
    return got.reshape(16 * block.shape[0], block.shape[1])


def on_device(right_side, diag_inverse, coupling, panel, solved):
    zh, b, core = (lax.axis_index(a) for a in ("zh", "b", "core"))
    swap = [(0, 1), (1, 0)]

    rows = lambda x: lax.dynamic_slice_in_dim(x, 16 * core, 16, 0)
    quarter = jnp.where(b == 1, rows(diag_inverse[0]), rows(coupling))
    quarter = lax.ppermute(quarter, ("zh",) + LINE, [(z, 15 - z) for z in range(16)])

    panel = panel.reshape(64, 512)
    side = right_side.reshape(64, 128)
    across = [(z, z ^ 3) for z in range(4)]
    sends = product(((1, 1), (1, 0), (0, 1)), panel, solved)
    from_both = lax.ppermute(sends[0], ("b", "core"), across)
    from_pair = lax.ppermute(sends[1], "b", swap)
    from_core = lax.ppermute(sends[2], "core", swap)
    (keep,) = product(((0, 0),), panel, solved, side)
    total = keep + from_core + from_pair + from_both
    half = pair_up(b, quarter, lax.ppermute(quarter, "b", swap))
    other = pair_up(core, half, lax.ppermute(half, "core", swap))
    other = other.transpose(1, 0, 2, 3).reshape(2, 32, 1024)
    copies = jnp.broadcast_to(total[None], (2, 4, 64, 128)).reshape(8, 64, 128)
    got_all = lax.all_to_all(copies, ("zh", "q"), 0, 0, tiled=True)
    first_half = zh == 0
    got_all, other, first_half = lax.optimization_barrier((got_all, other, first_half))
    residual = got_all.reshape(2, 4, 2, 32, 128).sum(1)
    first_res = residual[:, 0].reshape(64, 128)
    second_part = residual[:, 1].reshape(64, 128)

    def both(mine, theirs, x):
        a, c = mul(mine, x), mul(theirs, x)
        return jnp.where(first_half, jnp.concatenate([a, c]), jnp.concatenate([c, a])), a

    first_sol, first_mine = both(diag_inverse[0], other[0], gather_plane(first_res))
    cross, _ = both(coupling, other[1], gather_plane(first_sol))
    second_mine = mul(diag_inverse[1], gather_plane(second_part - cross))
    return jnp.stack([first_mine, second_mine])


def solution(mesh):
    fine = Mesh(mesh.devices.reshape(4, 4, 2, 4, 2, 2), ROWS + COLS)
    return jax.shard_map(
        on_device,
        mesh=fine,
        in_specs=(
            P(None, ROWS, COLS),
            P(None, ROWS, None),
            P(ROWS, None),
            P(None, ROWS, COLS),
            P(COLS, None),
        ),
        out_specs=P(None, ROWS, COLS),
        check_vma=False,
    )
```

time: 103 us -> 105 us (1.019)
  blocking collectives: 26.2 us -> 44.4 us
  waiting for transfers between devices: 24.3 us -> 16.3 us
  starting transfers between devices: 39.1 us -> 31.7 us
    all_to_all x2 -> x3, blocking collectives: 26.2 us -> 44.4 us  [gather_plane(): got = lax.all_to_all(copies, ('y', 'x'), 0, 0, tiled=True)]
    all_to_all x1 -> x0, waiting for transfers between devices: 8.78 us -> none  [gather_plane(): got = lax.all_to_all(copies, ('y', 'x'), 0, 0, tiled=True)]
    all_to_all x1 -> x0, starting transfers between devices: 7.48 us -> none  [gather_plane(): got = lax.all_to_all(copies, ('y', 'x'), 0, 0, tiled=True)]
    all_to_all x1, starting transfers between devices: 11.5 us -> 8.71 us  [on_device(): got_all = lax.all_to_all(copies, ('zh', 'q'), 0, 0, tiled=True)]
    ppermute x2 -> x3, starting transfers between devices: 5.74 us -> 7.8 us  [the longest x1 3.82 us: on_device(): from_pair = lax.ppermute(sends[1], 'b', swap)]
  transfers between devices with their start and end apart: 7 -> 7, of which waited for: 4 -> 3; matrix products, arithmetic and copies ran while one was open for 1% -> 2% of each run, Pallas kernels for 4% -> 2%
where the time goes in v7:
time: 105 us; the launch traced here: 104 us
  blocking collectives  44.4 us (42%)
  starting transfers between devices  31.7 us (30%)
  waiting for transfers between devices  16.3 us (16%)
  Pallas kernels  6.92 us (7%)
  matrix products  2.02 us (2%)
  other arithmetic  1.67 us (2%)
    all_to_all x3, blocking collectives, gather_plane(): got = lax.all_to_all(copies, ('y', 'x'), 0, 0, tiled=True)  44.4 us
    ppermute x1, starting transfers between devices, on_device(): lax.ppermute(quarter, ('zh',) + LINE, [(z, 15 - z) for z in range(16)])  11.2 us
    ppermute x1, waiting for transfers between devices, on_device(): half = pair_up(b, quarter, lax.ppermute(quarter, 'b', swap))  9.63 us
    all_to_all x1, starting transfers between devices, on_device(): got_all = lax.all_to_all(copies, ('zh', 'q'), 0, 0, tiled=True)  8.71 us
    pallas_call x2, Pallas kernels, product(): pl.pallas_call(functools.partial(product_kernel, flips), out_shape=[jax.S...  6.92 us
    all_to_all x1, waiting for transfers between devices, on_device(): got_all = lax.all_to_all(copies, ('zh', 'q'), 0, 0, tiled=True)  5.33 us
    ppermute x1, starting transfers between devices, on_device(): from_pair = lax.ppermute(sends[1], 'b', swap)  3.82 us
  transfers between devices with their start and end apart: 7, of which 3 were waited for; matrix products, arithmetic and copies ran while one was open for 2% of the time, Pallas kernels for 2%

profile of v7, /device:TPU:2, one launch (start us, length us, event | category | flops | bytes accessed | tf_op | source)
XLA Modules:
  0.0 104.1 jit_solution(2744292163265900602)
XLA Ops:
  0.0 0.0 slice-start
  0.0 4.4 %shard_map.56 = (f32[4,64,128]{2,1,0:T(8,128)}, f32[4,64,128]{2,1,0:T(8,128)}, f32[4,64,128]{2,1,0:T(8,128)}) custom-call(f32[64,512]{1,0:T(8,128)} %bitcast.60, f32[512,2048]{1,0:T(8,128)} %solved_ref.3), custom_call_target="tpu_custom_call" | custom-call | flops 300000000 | bytes 3145728 | tf_op jit(solution)/shard_map/pallas_call | solution.py:70
  4.4 1.9 %collective-permute-start = (f32[4,64,128]{2,1,0:T(8,128)}, f32[4,64,128]{2,1,0:T(8,128)S(1)}, u32[]{:S(2)}, u32[]{:S(2)}) collective-permute-start(f32[4,64,128]{2,1,0:T(8,128)} %get-tuple-element.11), channel_id=1, source_target_pairs={{0,1},{1,0},{2,3},{3,2},{4,5},{5,4},{6,7},{7,6},{8,9},{9,8},{10,11... | collective-permute-start | bytes 393224 | tf_op jit(solution)/shard_map/ppermute | solution.py:112
  6.3 3.8 %collective-permute-start.1 = (f32[4,64,128]{2,1,0:T(8,128)}, f32[4,64,128]{2,1,0:T(8,128)S(1)}, u32[]{:S(2)}, u32[]{:S(2)}) collective-permute-start(f32[4,64,128]{2,1,0:T(8,128)} %get-tuple-element.12), channel_id=1, source_target_pairs={{0,2},{2,0},{1,3},{3,1},{4,6},{6,4},{5,7},{7,5},{8,10},{10,8},{9,1... | collective-permute-start | bytes 393224 | tf_op jit(solution)/shard_map/ppermute | solution.py:111
  10.2 2.1 %collective-permute-start.2 = (f32[4,64,128]{2,1,0:T(8,128)}, f32[4,64,128]{2,1,0:T(8,128)S(1)}, u32[]{:S(2)}, u32[]{:S(2)}) collective-permute-start(f32[4,64,128]{2,1,0:T(8,128)} %get-tuple-element.13), channel_id=1, source_target_pairs={{0,3},{1,2},{2,1},{3,0},{4,7},{5,6},{6,5},{7,4},{8,11},{9,10},{10,... | collective-permute-start | bytes 393224 | tf_op jit(solution)/shard_map/ppermute | solution.py:110
  12.2 0.0 slice-done
  12.3 0.0 copy-done.1
  12.3 11.2 %collective-permute-start.3 = (f32[16,1024]{1,0:T(8,128)S(1)}, f32[16,1024]{1,0:T(8,128)S(1)}, u32[]{:S(2)}, u32[]{:S(2)}) collective-permute-start(f32[16,1024]{1,0:T(8,128)S(1)} %bitcast_select_fusion), channel_id=1, source_target_pairs={{0,30},{2,28},{4,26},{6,24},{8,22},{10,20},{12,18},{14,16},{16,14}... | collective-permute-start | bytes 196616 | tf_op jit(solution)/shard_map/ppermute | solution.py:104
  23.5 0.0 copy-start
  23.5 2.5 %shard_map.55 = f32[4,64,128]{2,1,0:T(8,128)} custom-call(f32[64,512]{1,0:T(8,128)} %bitcast.61, f32[512,2048]{1,0:T(8,128)} %solved_ref.3, f32[64,128]{1,0:T(8,128)} %bitcast.65), custom_call_target="tpu_custom_call" | custom-call | flops 100000000 | bytes 1048576 | tf_op jit(solution)/shard_map/pallas_call | solution.py:70
  26.0 0.0 collective-permute-done
  26.0 0.0 collective-permute-done.1
  26.0 0.0 collective-permute-done.2
  26.1 0.9 add_add_fusion
  27.0 0.7 broadcast_in_dim.10
  27.7 8.7 %all-to-all-start = ((f32[8,64,128]{2,1,0:T(8,128)}), f32[8,64,128]{2,1,0:T(8,128)S(1)}, u32[]{:S(2)}, u32[]{:S(2)}) async-start(f32[8,64,128]{2,1,0:T(8,128)} %bitcast.2), calls=%async_computation | async-start | bytes 524288 | tf_op jit(solution)/shard_map/all_to_all | solution.py:119
  36.4 0.0 collective-permute-done.3
  36.4 2.0 %collective-permute-start.4 = (f32[16,1024]{1,0:T(8,128)S(1)}, f32[16,1024]{1,0:T(8,128)S(1)}, u32[]{:S(2)}, u32[]{:S(2)}) collective-permute-start(f32[16,1024]{1,0:T(8,128)S(1)} %collective-permute-done.3), channel_id=1, source_target_pairs={{0,2},{2,0},{1,3},{3,1},{4,6},{6,4},{5,7},{7,5},{8,10},{10,8},{9,1... | collective-permute-start | bytes 196616 | tf_op jit(solution)/shard_map/ppermute | solution.py:115
  38.5 9.6 %collective-permute-done.4 = f32[16,1024]{1,0:T(8,128)S(1)} collective-permute-done((f32[16,1024]{1,0:T(8,128)S(1)}, f32[16,1024]{1,0:T(8,128)S(1)}, u32[]{:S(2)}, u32[]{:S(2)}) %collective-permute-start.4) | collective-permute-done | bytes 65568 | tf_op jit(solution)/shard_map/ppermute | solution.py:115
  48.1 1.9 %collective-permute-start.5 = (f32[2,16,1024]{2,1,0:T(8,128)S(1)}, f32[2,16,1024]{2,1,0:T(8,128)S(1)}, u32[]{:S(2)}, u32[]{:S(2)}) collective-permute-start(f32[2,16,1024]{2,1,0:T(8,128)S(1)} %pad_maximum_fusion.1), channel_id=1, source_target_pairs={{0,1},{1,0},{2,3},{3,2},{4,5},{5,4},{6,7},{7,6},{8,9},{9,8},{10,11... | collective-permute-start | bytes 393224 | tf_op jit(solution)/shard_map/ppermute | solution.py:116
  50.1 1.3 %collective-permute-done.5 = f32[2,16,1024]{2,1,0:T(8,128)S(1)} collective-permute-done((f32[2,16,1024]{2,1,0:T(8,128)S(1)}, f32[2,16,1024]{2,1,0:T(8,128)S(1)}, u32[]{:S(2)}, u32[]{:S(2)}) %collective-permute-start.5) | collective-permute-done | bytes 131104 | tf_op jit(solution)/shard_map/ppermute | solution.py:116
  51.4 5.3 %all-to-all-done = f32[8,64,128]{2,1,0:T(8,128)S(1)} async-done(((f32[8,64,128]{2,1,0:T(8,128)}), f32[8,64,128]{2,1,0:T(8,128)S(1)}, u32[]{:S(2)}, u32[]{:S(2)}) %all-to-all-start) | async-done | bytes 262176 | tf_op jit(solution)/shard_map/all_to_all | solution.py:119
  56.9 17.6 %all_to_all.20 = f32[16,64,128]{2,1,0:T(8,128)S(1)} all-to-all(f32[16,64,128]{2,1,0:T(8,128)S(1)} %broadcast_in_dim.12), channel_id=1, replica_groups=mesh['y'=4,'x'=4,'zh'=2,'q'=4,'b'=2,'core'=2] {'y','x'}, dimensions={0} | all-to-all | bytes 1048576 | tf_op jit(solution)/shard_map/all_to_all | solution.py:94
  74.4 0.0 copy-done
  74.4 0.4 fusion.5
  74.8 0.4 fusion.3
  75.3 13.9 %all_to_all.21 = f32[16,64,128]{2,1,0:T(8,128)S(1)} all-to-all(f32[16,64,128]{2,1,0:T(8,128)S(1)} %broadcast_in_dim.13), channel_id=1, replica_groups=mesh['y'=4,'x'=4,'zh'=2,'q'=4,'b'=2,'core'=2] {'y','x'}, dimensions={0} | all-to-all | bytes 1048576 | tf_op jit(solution)/shard_map/all_to_all | solution.py:94
  89.2 0.4 fusion.1
  89.6 0.4 convolution_bitcast_fusion.1
  90.1 13.0 %all_to_all.22 = f32[16,64,128]{2,1,0:T(8,128)S(1)} all-to-all(f32[16,64,128]{2,1,0:T(8,128)S(1)} %broadcast_in_dim.14), channel_id=1, replica_groups=mesh['y'=4,'x'=4,'zh'=2,'q'=4,'b'=2,'core'=2] {'y','x'}, dimensions={0} | all-to-all | bytes 1048576 | tf_op jit(solution)/shard_map/all_to_all | solution.py:94
  103.1 0.4 convolution_bitcast_fusion
  103.5 0.6 pad_maximum_fusion.2
  (13 shorter events, 0.3 us)
Async XLA Ops:
  0.0 12.2 %slice-start = ((f32[2,32,1024]{2,1,0:T(8,128)}), f32[1,32,1024]{2,1,0:T(8,128)S(1)}, s32[]{:S(2)}) async-start(f32[2,32,1024]{2,1,0:T(8,128)} %param.6), calls=%async_computation.4 | async-start | bytes 262144 | tf_op jit(solution)/shard_map/slice | solution.py:130
  0.0 12.3 %copy-start.1 = (f32[32,1024]{1,0:T(8,128)S(1)}, f32[32,1024]{1,0:T(8,128)}, u32[]{:S(2)}) copy-start(f32[32,1024]{1,0:T(8,128)} %param.7) | copy-start | bytes 393220
  4.4 21.6 %collective-permute-start = (f32[4,64,128]{2,1,0:T(8,128)}, f32[4,64,128]{2,1,0:T(8,128)S(1)}, u32[]{:S(2)}, u32[]{:S(2)}) collective-permute-start(f32[4,64,128]{2,1,0:T(8,128)} %get-tuple-element.11), channel_id=1, source_target_pairs={{0,1},{1,0},{2,3},{3,2},{4,5},{5,4},{6,7},{7,6},{8,9},{9,8},{10,11... | collective-permute-start | bytes 393224 | tf_op jit(solution)/shard_map/ppermute | solution.py:112
  6.3 19.7 %collective-permute-start.1 = (f32[4,64,128]{2,1,0:T(8,128)}, f32[4,64,128]{2,1,0:T(8,128)S(1)}, u32[]{:S(2)}, u32[]{:S(2)}) collective-permute-start(f32[4,64,128]{2,1,0:T(8,128)} %get-tuple-element.12), channel_id=1, source_target_pairs={{0,2},{2,0},{1,3},{3,1},{4,6},{6,4},{5,7},{7,5},{8,10},{10,8},{9,1... | collective-permute-start | bytes 393224 | tf_op jit(solution)/shard_map/ppermute | solution.py:111
  10.2 15.9 %collective-permute-start.2 = (f32[4,64,128]{2,1,0:T(8,128)}, f32[4,64,128]{2,1,0:T(8,128)S(1)}, u32[]{:S(2)}, u32[]{:S(2)}) collective-permute-start(f32[4,64,128]{2,1,0:T(8,128)} %get-tuple-element.13), channel_id=1, source_target_pairs={{0,3},{1,2},{2,1},{3,0},{4,7},{5,6},{6,5},{7,4},{8,11},{9,10},{10,... | collective-permute-start | bytes 393224 | tf_op jit(solution)/shard_map/ppermute | solution.py:110
  12.3 24.1 %collective-permute-start.3 = (f32[16,1024]{1,0:T(8,128)S(1)}, f32[16,1024]{1,0:T(8,128)S(1)}, u32[]{:S(2)}, u32[]{:S(2)}) collective-permute-start(f32[16,1024]{1,0:T(8,128)S(1)} %bitcast_select_fusion), channel_id=1, source_target_pairs={{0,30},{2,28},{4,26},{6,24},{8,22},{10,20},{12,18},{14,16},{16,14}... | collective-permute-start | bytes 196616 | tf_op jit(solution)/shard_map/ppermute | solution.py:104
  23.5 50.9 %copy-start = (f32[2,32,1024]{2,1,0:T(8,128)S(1)}, f32[2,32,1024]{2,1,0:T(8,128)}, u32[]{:S(2)}) copy-start(f32[2,32,1024]{2,1,0:T(8,128)} %param.6) | copy-start | bytes 786436
  27.7 29.1 %all-to-all-start = ((f32[8,64,128]{2,1,0:T(8,128)}), f32[8,64,128]{2,1,0:T(8,128)S(1)}, u32[]{:S(2)}, u32[]{:S(2)}) async-start(f32[8,64,128]{2,1,0:T(8,128)} %bitcast.2), calls=%async_computation | async-start | bytes 524288 | tf_op jit(solution)/shard_map/all_to_all | solution.py:119
  36.4 11.7 %collective-permute-start.4 = (f32[16,1024]{1,0:T(8,128)S(1)}, f32[16,1024]{1,0:T(8,128)S(1)}, u32[]{:S(2)}, u32[]{:S(2)}) collective-permute-start(f32[16,1024]{1,0:T(8,128)S(1)} %collective-permute-done.3), channel_id=1, source_target_pairs={{0,2},{2,0},{1,3},{3,1},{4,6},{6,4},{5,7},{7,5},{8,10},{10,8},{9,1... | collective-permute-start | bytes 196616 | tf_op jit(solution)/shard_map/ppermute | solution.py:115
  48.1 3.2 %collective-permute-start.5 = (f32[2,16,1024]{2,1,0:T(8,128)S(1)}, f32[2,16,1024]{2,1,0:T(8,128)S(1)}, u32[]{:S(2)}, u32[]{:S(2)}) collective-permute-start(f32[2,16,1024]{2,1,0:T(8,128)S(1)} %pad_maximum_fusion.1), channel_id=1, source_target_pairs={{0,1},{1,0},{2,3},{3,2},{4,5},{5,4},{6,7},{7,6},{8,9},{9,8},{10,11... | collective-permute-start | bytes 393224 | tf_op jit(solution)/shard_map/ppermute | solution.py:116

commit v8 on v7

v8 whole, which is shorter than its diff:
```python
import functools

import jax
import jax.numpy as jnp
from jax import lax
from jax.experimental import pallas as pl
from jax.experimental.pallas import tpu as pltpu
from jax.sharding import Mesh, PartitionSpec as P

ROWS = ("y", "x", "zh")
LINE = ("q", "b")
COLS = LINE + ("core",)


def mul(a, b):
    return jnp.dot(a, b, precision=lax.Precision.HIGHEST, preferred_element_type=jnp.float32)


def halves(x):
    high = x.astype(jnp.bfloat16)
    return high, (x - high.astype(jnp.float32)).astype(jnp.bfloat16)


def product_kernel(flips, panel_ref, solved_ref, *rest):
    count = len(flips)
    extra = rest[: -count - 5 - (count > 1)]
    outs = rest[len(extra) : -5]
    panel_held, add_held, slots, sems, small_sems = rest[-5:]
    core, q, b = (lax.axis_index(a) for a in ("core", "q", "b"))
    copies = []
    for part, (flip_b, flip_core) in enumerate(flips):
        to_b = 1 - b if flip_b else b
        to_core = 1 - core if flip_core else core
        for step in range(4):
            columns = pl.ds(pl.multiple_of((4 * step + 2 * to_b + to_core) * 128, 128), 128)
            copy = pltpu.make_async_copy(
                solved_ref.at[:, columns],
                slots.at[part, :, pl.ds(128 * step, 128)],
                sems.at[part, step],
            )
            copy.start()
            copies.append(copy)
    panel_copy = pltpu.make_async_copy(panel_ref, panel_held, small_sems.at[0])
    panel_copy.start()
    hand_copies = []
    if count > 1:
        for i, source in enumerate((extra[0].at[0], extra[1])):
            copy = pltpu.make_async_copy(source, outs[count].at[i], small_sems.at[1 + i])
            copy.start()
            hand_copies.append(copy)
    else:
        add_copy = pltpu.make_async_copy(extra[0], add_held, small_sems.at[1])
        add_copy.start()
        add_copy.wait()
    panel_copy.wait()
    p_high, p_low = halves(-panel_held[...])
    p_both = jnp.concatenate([p_high, p_low], axis=0)
    dot = functools.partial(jnp.dot, preferred_element_type=jnp.float32)
    for part in range(count):
        for two in range(2):
            copies[4 * part + 2 * two].wait()
            copies[4 * part + 2 * two + 1].wait()
            s_high, s_low = halves(slots[part, :, pl.ds(256 * two, 256)])
            wide = dot(p_both, s_high)
            got = wide[64:] + dot(p_high, s_low) + wide[:64]
            for step in range(2 * two, 2 * two + 2):
                block = got[:, 128 * (step % 2) : 128 * (step % 2 + 1)]
                if count == 1:
                    block = block + jnp.where(q == step, add_held[...], 0.0)
                outs[part][step] = block
    for copy in hand_copies:
        copy.wait()


def product(flips, panel, solved, *extra):
    args = (panel, solved) + extra
    count = len(flips)
    shapes = [(4, 64, 128)] * count + ([(2,) + extra[1].shape] if count > 1 else [])
    return pl.pallas_call(
        functools.partial(product_kernel, flips),
        out_shape=[jax.ShapeDtypeStruct(shape, jnp.float32) for shape in shapes],
        in_specs=[pl.BlockSpec(memory_space=pl.ANY)] * len(args),
        out_specs=[pl.BlockSpec(memory_space=pltpu.VMEM)] * len(shapes),
        scratch_shapes=[
            pltpu.VMEM((64, 512), jnp.float32),
            pltpu.VMEM((64, 128), jnp.float32),
            pltpu.VMEM((count, 512, 512), jnp.float32),
            pltpu.SemaphoreType.DMA((count, 4)),
            pltpu.SemaphoreType.DMA((3,)),
        ],
        compiler_params=pltpu.CompilerParams(vmem_limit_bytes=56 << 20),
        cost_estimate=pl.CostEstimate(flops=count * 10**8, bytes_accessed=count << 20, transcendentals=0),
    )(*args)


def gather_plane(block):
    copies = jnp.broadcast_to(block[None], (16,) + block.shape)
    got = lax.all_to_all(copies, ("y", "x"), 0, 0, tiled=True)
    return got.reshape(16 * block.shape[0], block.shape[1])


def on_device(right_side, diag_inverse, coupling, panel, solved):
    zh, q = lax.axis_index("zh"), lax.axis_index("q")
    swap = [(0, 1), (1, 0)]
    flip = lambda m: [(z, z ^ m) for z in range(4)]
    other_half = lambda x: lax.ppermute(x, ("zh",) + LINE, [(z, 15 - z) for z in range(16)])
    take = lambda x, index: lax.dynamic_index_in_dim(x, index, 0, keepdims=False)

    panel = panel.reshape(64, 512)
    *sends, factors = product(((1, 1), (1, 0), (0, 1)), panel, solved, diag_inverse, coupling)
    from_both = lax.ppermute(sends[0], ("b", "core"), flip(3))
    from_pair = lax.ppermute(sends[1], "b", swap)
    from_core = lax.ppermute(sends[2], "core", swap)
    factors = other_half(factors)
    (keep,) = product(((0, 0),), panel, solved, right_side.reshape(64, 128))
    total = keep + from_core + from_pair + from_both
    got = [lax.ppermute(take(total, q ^ m), "q", flip(m)) for m in (1, 2, 3)]
    residual = take(total, q) + got[0] + got[1] + got[2]
    first_half = zh == 0
    residual, factors, first_half = lax.optimization_barrier((residual, factors, first_half))

    def ordered(mine, theirs):
        return jnp.concatenate([jnp.where(first_half, mine, theirs), jnp.where(first_half, theirs, mine)])

    known = gather_plane(residual[:32]).reshape(16, 1, 32, 128)
    known = jnp.concatenate([jnp.where(first_half, known, 0.0), jnp.where(first_half, 0.0, known)], axis=1)
    known = known.reshape(1024, 128)
    parts = jnp.concatenate([mul(diag_inverse[0], known), mul(factors[0], known), residual[32:]])
    across = lax.ppermute(parts, "zh", swap)
    first_mine = parts[:32] + across[32:64]
    first_sol = gather_plane(ordered(first_mine, parts[32:64] + across[:32]))
    mine = residual[32:] - mul(coupling, first_sol)
    theirs = across[64:] - mul(factors[1], first_sol)
    second_mine = mul(diag_inverse[1], gather_plane(ordered(mine, theirs)))
    return jnp.stack([first_mine, second_mine])


def solution(mesh):
    fine = Mesh(mesh.devices.reshape(4, 4, 2, 4, 2, 2), ROWS + COLS)
    return jax.shard_map(
        on_device,
        mesh=fine,
        in_specs=(
            P(None, ROWS, COLS),
            P(None, ROWS, None),
            P(ROWS, None),
            P(None, ROWS, COLS),
            P(COLS, None),
        ),
        out_specs=P(None, ROWS, COLS),
        check_vma=False,
    )
```

time: 105 us -> 109 us (1.038)
  starting transfers between devices: 31.7 us -> 42.5 us
  blocking collectives: 44.4 us -> 40.7 us
  waiting for transfers between devices: 16.3 us -> 14.2 us
    ppermute x4 -> x6, starting transfers between devices: 17.2 us -> 36.6 us  [the longest x3 14.3 us: on_device(): got = [lax.ppermute(take(total, q ^ m), 'q', flip(m)) for m in (1, 2, 3)]]
    all_to_all x1 -> x0, starting transfers between devices: 8.71 us -> none  [on_device(): got_all = lax.all_to_all(copies, ('zh', 'q'), 0, 0, tiled=True)]
    all_to_all x1 -> x0, waiting for transfers between devices: 5.33 us -> none  [on_device(): got_all = lax.all_to_all(copies, ('zh', 'q'), 0, 0, tiled=True)]
    all_to_all x3, blocking collectives: 44.4 us -> 40.7 us  [gather_plane(): got = lax.all_to_all(copies, ('y', 'x'), 0, 0, tiled=True)]
    ppermute x4 -> x6, waiting for transfers between devices: 10.9 us -> 14.2 us  [the longest x3 8.5 us: on_device(): got = [lax.ppermute(take(total, q ^ m), 'q', flip(m)) for m in (1, 2, 3)]]
  transfers between devices with their start and end apart: 7 -> 8, of which waited for: 3 -> 4; matrix products, arithmetic and copies ran while one was open for 2% -> 1% of each run, Pallas kernels for 2% -> 2%
where the time goes in v8:
time: 109 us; the launch traced here: 108 us
  starting transfers between devices  42.5 us (39%)
  blocking collectives  40.7 us (37%)
  waiting for transfers between devices  14.2 us (13%)
  Pallas kernels  6.93 us (6%)
  matrix products  2.03 us (2%)
  other arithmetic  1.71 us (2%)
    all_to_all x3, blocking collectives, gather_plane(): got = lax.all_to_all(copies, ('y', 'x'), 0, 0, tiled=True)  40.7 us
    ppermute x3, starting transfers between devices, on_device(): got = [lax.ppermute(take(total, q ^ m), 'q', flip(m)) for m in (1, 2, 3)]  14.3 us
    ppermute x1, starting transfers between devices, on_device(): lax.ppermute(x, ('zh',) + LINE, [(z, 15 - z) for z in range(16)])  11.2 us
    ppermute x1, starting transfers between devices, on_device(): across = lax.ppermute(parts, 'zh', swap)  8.98 us
    ppermute x3, waiting for transfers between devices, on_device(): got = [lax.ppermute(take(total, q ^ m), 'q', flip(m)) for m in (1, 2, 3)]  8.5 us
    pallas_call x2, Pallas kernels, product(): pl.pallas_call(functools.partial(product_kernel, flips), out_shape=[jax.S...  6.93 us
    ppermute x1, waiting for transfers between devices, on_device(): across = lax.ppermute(parts, 'zh', swap)  5.71 us
    ppermute x1, starting transfers between devices, on_device(): from_pair = lax.ppermute(sends[1], 'b', swap)  3.86 us
  transfers between devices with their start and end apart: 8, of which 4 were waited for; matrix products, arithmetic and copies ran while one was open for 1% of the time, Pallas kernels for 2%

profile of v8, /device:TPU:2, one launch (start us, length us, event | category | flops | bytes accessed | tf_op | source)
XLA Modules:
  0.0 108.5 jit_solution(5707519074982769725)
XLA Ops:
  0.0 4.4 %shard_map.56 = (f32[4,64,128]{2,1,0:T(8,128)}, f32[4,64,128]{2,1,0:T(8,128)}, f32[4,64,128]{2,1,0:T(8,128)}, f32[2,32,1024]{2,1,0:T(8,128)}) custom-call(f32[64,512]{1,0:T(8,128)} %bitcast.58, f32[512,2048]{1,0:T(8,128)} %solved_ref.3, f32[2,32,1024]{2,1,0:T(8,128)} %rest_0_.1, f32[32,1024]{1,0:T(8,128)} %rest_1_.1), custom_call_target="tpu_custom_call" | custom-call | flops 300000000 | bytes 3145728 | tf_op jit(solution)/shard_map/pallas_call | solution.py:79
  4.4 0.0 copy-start
  4.4 2.1 %collective-permute-start = (f32[4,64,128]{2,1,0:T(8,128)}, f32[4,64,128]{2,1,0:T(8,128)S(1)}, u32[]{:S(2)}, u32[]{:S(2)}) collective-permute-start(f32[4,64,128]{2,1,0:T(8,128)} %get-tuple-element.12), channel_id=1, source_target_pairs={{0,1},{1,0},{2,3},{3,2},{4,5},{5,4},{6,7},{7,6},{8,9},{9,8},{10,11... | collective-permute-start | bytes 393224 | tf_op jit(solution)/shard_map/ppermute | solution.py:113
  6.5 3.9 %collective-permute-start.1 = (f32[4,64,128]{2,1,0:T(8,128)}, f32[4,64,128]{2,1,0:T(8,128)S(1)}, u32[]{:S(2)}, u32[]{:S(2)}) collective-permute-start(f32[4,64,128]{2,1,0:T(8,128)} %get-tuple-element.13), channel_id=1, source_target_pairs={{0,2},{2,0},{1,3},{3,1},{4,6},{6,4},{5,7},{7,5},{8,10},{10,8},{9,1... | collective-permute-start | bytes 393224 | tf_op jit(solution)/shard_map/ppermute | solution.py:112
  10.3 2.0 %collective-permute-start.2 = (f32[4,64,128]{2,1,0:T(8,128)}, f32[4,64,128]{2,1,0:T(8,128)S(1)}, u32[]{:S(2)}, u32[]{:S(2)}) collective-permute-start(f32[4,64,128]{2,1,0:T(8,128)} %get-tuple-element.14), channel_id=1, source_target_pairs={{0,3},{1,2},{2,1},{3,0},{4,7},{5,6},{6,5},{7,4},{8,11},{9,10},{10,... | collective-permute-start | bytes 393224 | tf_op jit(solution)/shard_map/ppermute | solution.py:111
  12.4 11.2 %collective-permute-start.6 = (f32[2,32,1024]{2,1,0:T(8,128)}, f32[2,32,1024]{2,1,0:T(8,128)S(1)}, u32[]{:S(2)}, u32[]{:S(2)}) collective-permute-start(f32[2,32,1024]{2,1,0:T(8,128)} %get-tuple-element.15), channel_id=1, source_target_pairs={{0,30},{2,28},{4,26},{6,24},{8,22},{10,20},{12,18},{14,16},{16,14}... | collective-permute-start | bytes 786440 | tf_op jit(solution)/shard_map/ppermute | solution.py:106
  23.6 2.5 %shard_map.55 = f32[4,64,128]{2,1,0:T(8,128)} custom-call(f32[64,512]{1,0:T(8,128)} %bitcast.59, f32[512,2048]{1,0:T(8,128)} %solved_ref.3, f32[64,128]{1,0:T(8,128)} %bitcast.60), custom_call_target="tpu_custom_call" | custom-call | flops 100000000 | bytes 1048576 | tf_op jit(solution)/shard_map/pallas_call | solution.py:79
  26.2 0.0 copy-start.1
  26.2 0.0 collective-permute-done
  26.2 0.0 collective-permute-done.1
  26.2 0.0 collective-permute-done.2
  26.2 1.0 add_add_fusion
  27.2 5.2 %collective-permute-start.3 = (f32[64,128]{1,0:T(8,128)S(1)}, f32[64,128]{1,0:T(8,128)S(1)}, u32[]{:S(2)}, u32[]{:S(2)}) collective-permute-start(f32[64,128]{1,0:T(8,128)S(1)} %get-tuple-element.21), channel_id=1, source_target_pairs={{0,4},{4,0},{8,12},{12,8},{1,5},{5,1},{9,13},{13,9},{2,6},{6,2},{1... | collective-permute-start | bytes 98312 | tf_op jit(solution)/shard_map/ppermute | solution.py:117
  32.4 7.3 %collective-permute-start.5 = (f32[64,128]{1,0:T(8,128)S(1)}, f32[64,128]{1,0:T(8,128)S(1)}, u32[]{:S(2)}, u32[]{:S(2)}) collective-permute-start(f32[64,128]{1,0:T(8,128)S(1)} %get-tuple-element.22), channel_id=1, source_target_pairs={{0,12},{4,8},{8,4},{12,0},{1,13},{5,9},{9,5},{13,1},{2,14},{6,10},... | collective-permute-start | bytes 98312 | tf_op jit(solution)/shard_map/ppermute | solution.py:117
  39.6 1.9 %collective-permute-start.4 = (f32[64,128]{1,0:T(8,128)S(1)}, f32[64,128]{1,0:T(8,128)S(1)}, u32[]{:S(2)}, u32[]{:S(2)}) collective-permute-start(f32[64,128]{1,0:T(8,128)S(1)} %get-tuple-element.23), channel_id=1, source_target_pairs={{0,8},{4,12},{8,0},{12,4},{1,9},{5,13},{9,1},{13,5},{2,10},{6,14},... | collective-permute-start | bytes 98312 | tf_op jit(solution)/shard_map/ppermute | solution.py:117
  41.6 1.1 %collective-permute-done.3 = f32[64,128]{1,0:T(8,128)S(1)} collective-permute-done((f32[64,128]{1,0:T(8,128)S(1)}, f32[64,128]{1,0:T(8,128)S(1)}, u32[]{:S(2)}, u32[]{:S(2)}) %collective-permute-start.3) | collective-permute-done | bytes 32800 | tf_op jit(solution)/shard_map/ppermute | solution.py:117
  42.7 1.2 %collective-permute-done.5 = f32[64,128]{1,0:T(8,128)S(1)} collective-permute-done((f32[64,128]{1,0:T(8,128)S(1)}, f32[64,128]{1,0:T(8,128)S(1)}, u32[]{:S(2)}, u32[]{:S(2)}) %collective-permute-start.5) | collective-permute-done | bytes 32800 | tf_op jit(solution)/shard_map/ppermute | solution.py:117
  43.9 6.2 %collective-permute-done.4 = f32[64,128]{1,0:T(8,128)S(1)} collective-permute-done((f32[64,128]{1,0:T(8,128)S(1)}, f32[64,128]{1,0:T(8,128)S(1)}, u32[]{:S(2)}, u32[]{:S(2)}) %collective-permute-start.4) | collective-permute-done | bytes 32800 | tf_op jit(solution)/shard_map/ppermute | solution.py:117
  50.1 0.0 collective-permute-done.6
  50.1 14.6 %all_to_all.15 = f32[16,32,128]{2,1,0:T(8,128)S(1)} all-to-all(f32[16,32,128]{2,1,0:T(8,128)S(1)} %broadcast_in_dim.12), channel_id=1, replica_groups=mesh['y'=4,'x'=4,'zh'=2,'q'=4,'b'=2,'core'=2] {'y','x'}, dimensions={0} | all-to-all | bytes 524288 | tf_op jit(solution)/shard_map/all_to_all | solution.py:98
  64.7 0.1 select_bitcast_fusion.1
  64.8 0.0 copy-done
  64.9 0.4 convolution_bitcast_fusion.2
  65.3 0.4 fusion.4
  65.7 9.0 %collective-permute-start.7 = (f32[96,128]{1,0:T(8,128)S(1)}, f32[96,128]{1,0:T(8,128)S(1)}, u32[]{:S(2)}, u32[]{:S(2)}) collective-permute-start(f32[96,128]{1,0:T(8,128)S(1)} %pad_maximum_fusion.1), channel_id=1, source_target_pairs={{0,16},{16,0},{1,17},{17,1},{2,18},{18,2},{3,19},{19,3},{4,20},{20... | collective-permute-start | bytes 147464 | tf_op jit(solution)/shard_map/ppermute | solution.py:129
  74.7 5.7 %collective-permute-done.7 = f32[96,128]{1,0:T(8,128)S(1)} collective-permute-done((f32[96,128]{1,0:T(8,128)S(1)}, f32[96,128]{1,0:T(8,128)S(1)}, u32[]{:S(2)}, u32[]{:S(2)}) %collective-permute-start.7) | collective-permute-done | bytes 49184 | tf_op jit(solution)/shard_map/ppermute | solution.py:129
  80.4 13.0 %all_to_all.16 = f32[16,64,128]{2,1,0:T(8,128)S(1)} all-to-all(f32[16,64,128]{2,1,0:T(8,128)S(1)} %broadcast_in_dim.14), channel_id=1, replica_groups=mesh['y'=4,'x'=4,'zh'=2,'q'=4,'b'=2,'core'=2] {'y','x'}, dimensions={0} | all-to-all | bytes 1048576 | tf_op jit(solution)/shard_map/all_to_all | solution.py:98
  93.5 0.4 fusion.2
  93.9 0.4 broadcast_select_fusion.1
  94.4 13.1 %all_to_all.17 = f32[16,64,128]{2,1,0:T(8,128)S(1)} all-to-all(f32[16,64,128]{2,1,0:T(8,128)S(1)} %broadcast_in_dim.15), channel_id=1, replica_groups=mesh['y'=4,'x'=4,'zh'=2,'q'=4,'b'=2,'core'=2] {'y','x'}, dimensions={0} | all-to-all | bytes 1048576 | tf_op jit(solution)/shard_map/all_to_all | solution.py:98
  107.5 0.4 convolution_bitcast_fusion
  107.9 0.6 pad_maximum_fusion.4
  (12 shorter events, 0.2 us)
Async XLA Ops:
  4.4 60.4 %copy-start = (f32[2,32,1024]{2,1,0:T(8,128)S(1)}, f32[2,32,1024]{2,1,0:T(8,128)}, u32[]{:S(2)}) copy-start(f32[2,32,1024]{2,1,0:T(8,128)} %rest_0_.1) | copy-start | bytes 786436
  4.4 21.8 %collective-permute-start = (f32[4,64,128]{2,1,0:T(8,128)}, f32[4,64,128]{2,1,0:T(8,128)S(1)}, u32[]{:S(2)}, u32[]{:S(2)}) collective-permute-start(f32[4,64,128]{2,1,0:T(8,128)} %get-tuple-element.12), channel_id=1, source_target_pairs={{0,1},{1,0},{2,3},{3,2},{4,5},{5,4},{6,7},{7,6},{8,9},{9,8},{10,11... | collective-permute-start | bytes 393224 | tf_op jit(solution)/shard_map/ppermute | solution.py:113
  6.5 19.7 %collective-permute-start.1 = (f32[4,64,128]{2,1,0:T(8,128)}, f32[4,64,128]{2,1,0:T(8,128)S(1)}, u32[]{:S(2)}, u32[]{:S(2)}) collective-permute-start(f32[4,64,128]{2,1,0:T(8,128)} %get-tuple-element.13), channel_id=1, source_target_pairs={{0,2},{2,0},{1,3},{3,1},{4,6},{6,4},{5,7},{7,5},{8,10},{10,8},{9,1... | collective-permute-start | bytes 393224 | tf_op jit(solution)/shard_map/ppermute | solution.py:112
  10.3 15.9 %collective-permute-start.2 = (f32[4,64,128]{2,1,0:T(8,128)}, f32[4,64,128]{2,1,0:T(8,128)S(1)}, u32[]{:S(2)}, u32[]{:S(2)}) collective-permute-start(f32[4,64,128]{2,1,0:T(8,128)} %get-tuple-element.14), channel_id=1, source_target_pairs={{0,3},{1,2},{2,1},{3,0},{4,7},{5,6},{6,5},{7,4},{8,11},{9,10},{10,... | collective-permute-start | bytes 393224 | tf_op jit(solution)/shard_map/ppermute | solution.py:111
  12.4 37.7 %collective-permute-start.6 = (f32[2,32,1024]{2,1,0:T(8,128)}, f32[2,32,1024]{2,1,0:T(8,128)S(1)}, u32[]{:S(2)}, u32[]{:S(2)}) collective-permute-start(f32[2,32,1024]{2,1,0:T(8,128)} %get-tuple-element.15), channel_id=1, source_target_pairs={{0,30},{2,28},{4,26},{6,24},{8,22},{10,20},{12,18},{14,16},{16,14}... | collective-permute-start | bytes 786440 | tf_op jit(solution)/shard_map/ppermute | solution.py:106
  26.2 67.7 %copy-start.1 = (f32[32,1024]{1,0:T(8,128)S(1)}, f32[32,1024]{1,0:T(8,128)}, u32[]{:S(2)}) copy-start(f32[32,1024]{1,0:T(8,128)} %rest_1_.1) | copy-start | bytes 393220
  27.2 15.5 %collective-permute-start.3 = (f32[64,128]{1,0:T(8,128)S(1)}, f32[64,128]{1,0:T(8,128)S(1)}, u32[]{:S(2)}, u32[]{:S(2)}) collective-permute-start(f32[64,128]{1,0:T(8,128)S(1)} %get-tuple-element.21), channel_id=1, source_target_pairs={{0,4},{4,0},{8,12},{12,8},{1,5},{5,1},{9,13},{13,9},{2,6},{6,2},{1... | collective-permute-start | bytes 98312 | tf_op jit(solution)/shard_map/ppermute | solution.py:117
  32.4 11.5 %collective-permute-start.5 = (f32[64,128]{1,0:T(8,128)S(1)}, f32[64,128]{1,0:T(8,128)S(1)}, u32[]{:S(2)}, u32[]{:S(2)}) collective-permute-start(f32[64,128]{1,0:T(8,128)S(1)} %get-tuple-element.22), channel_id=1, source_target_pairs={{0,12},{4,8},{8,4},{12,0},{1,13},{5,9},{9,5},{13,1},{2,14},{6,10},... | collective-permute-start | bytes 98312 | tf_op jit(solution)/shard_map/ppermute | solution.py:117
  39.6 10.4 %collective-permute-start.4 = (f32[64,128]{1,0:T(8,128)S(1)}, f32[64,128]{1,0:T(8,128)S(1)}, u32[]{:S(2)}, u32[]{:S(2)}) collective-permute-start(f32[64,128]{1,0:T(8,128)S(1)} %get-tuple-element.23), channel_id=1, source_target_pairs={{0,8},{4,12},{8,0},{12,4},{1,9},{5,13},{9,1},{13,5},{2,10},{6,14},... | collective-permute-start | bytes 98312 | tf_op jit(solution)/shard_map/ppermute | solution.py:117
  65.7 14.7 %collective-permute-start.7 = (f32[96,128]{1,0:T(8,128)S(1)}, f32[96,128]{1,0:T(8,128)S(1)}, u32[]{:S(2)}, u32[]{:S(2)}) collective-permute-start(f32[96,128]{1,0:T(8,128)S(1)} %pad_maximum_fusion.1), channel_id=1, source_target_pairs={{0,16},{16,0},{1,17},{17,1},{2,18},{18,2},{3,19},{19,3},{4,20},{20... | collective-permute-start | bytes 147464 | tf_op jit(solution)/shard_map/ppermute | solution.py:129

commit v9 on v7

--- a/solution.py
+++ b/solution.py
@@ -23,8 +23,8 @@
 
 def product_kernel(flips, panel_ref, solved_ref, *rest):
     count = len(flips)
-    add_ref = rest[0] if len(rest) > count + 5 else None
-    outs = rest[-count - 5 : -5]
+    add_ref = rest[0] if len(rest) > 6 else None
+    out_ref = rest[-6]
     panel_held, add_held, slots, sems, small_sems = rest[-5:]
     core, q, b = (lax.axis_index(a) for a in ("core", "q", "b"))
     copies = []
@@ -59,9 +59,9 @@
             got = wide[64:] + dot(p_high, s_low) + wide[:64]
             for step in range(2 * two, 2 * two + 2):
                 block = got[:, 128 * (step % 2) : 128 * (step % 2 + 1)]
-                if add_ref is not None:
+                if add_ref is not None and flips[part] == (0, 0):
                     block = block + jnp.where(q == step, add_held[...], 0.0)
-                outs[part][step] = block
+                out_ref[part, step] = block
 
 
 def product(flips, panel, solved, add=None):
@@ -69,9 +69,9 @@
     count = len(flips)
     return pl.pallas_call(
         functools.partial(product_kernel, flips),
-        out_shape=[jax.ShapeDtypeStruct((4, 64, 128), jnp.float32)] * count,
+        out_shape=jax.ShapeDtypeStruct((count, 4, 64, 128), jnp.float32),
         in_specs=[pl.BlockSpec(memory_space=pl.ANY)] * len(args),
-        out_specs=[pl.BlockSpec(memory_space=pltpu.VMEM)] * count,
+        out_specs=pl.BlockSpec(memory_space=pltpu.VMEM),
         scratch_shapes=[
             pltpu.VMEM((64, 512), jnp.float32),
             pltpu.VMEM((64, 128), jnp.float32),
@@ -104,14 +104,10 @@
     quarter = lax.ppermute(quarter, ("zh",) + LINE, [(z, 15 - z) for z in range(16)])
 
     panel = panel.reshape(64, 512)
-    side = right_side.reshape(64, 128)
-    across = [(z, z ^ 3) for z in range(4)]
-    sends = product(((1, 1), (1, 0), (0, 1)), panel, solved)
-    from_both = lax.ppermute(sends[0], ("b", "core"), across)
-    from_pair = lax.ppermute(sends[1], "b", swap)
-    from_core = lax.ppermute(sends[2], "core", swap)
-    (keep,) = product(((0, 0),), panel, solved, side)
-    total = keep + from_core + from_pair + from_both
+    moved = lax.ppermute(product(((1, 1), (0, 1)), panel, solved), "core", swap)
+    keep = product(((1, 0), (0, 0)), panel, solved, right_side.reshape(64, 128))
+    passed = lax.ppermute(keep[0] + moved[0], "b", swap)
+    total = keep[1] + moved[1] + passed
     half = pair_up(b, quarter, lax.ppermute(quarter, "b", swap))
     other = pair_up(core, half, lax.ppermute(half, "core", swap))
     other = other.transpose(1, 0, 2, 3).reshape(2, 32, 1024)

time: 105 us -> 103 us (0.981)
  blocking collectives: 44.4 us -> 42.2 us
    all_to_all x1, starting transfers between devices: 8.71 us -> 11.5 us  [on_device(): got_all = lax.all_to_all(copies, ('zh', 'q'), 0, 0, tiled=True)]
    all_to_all x3, blocking collectives: 44.4 us -> 42.2 us  [gather_plane(): got = lax.all_to_all(copies, ('y', 'x'), 0, 0, tiled=True)]
    ppermute x3 -> x2, starting transfers between devices: 7.8 us -> 5.74 us  [the longest x1 3.82 us: on_device(): passed = lax.ppermute(keep[0] + moved[0], 'b', swap)]
  transfers between devices with their start and end apart: 7 -> 6, of which waited for: 3 -> 3; matrix products, arithmetic and copies ran while one was open for 2% -> 2% of each run, Pallas kernels for 2% -> 3%
where the time goes in v9:
time: 103 us; the launch traced here: 102 us
  blocking collectives  42.2 us (41%)
  starting transfers between devices  31.6 us (31%)
  waiting for transfers between devices  15.5 us (15%)
  Pallas kernels  6.99 us (7%)
  other arithmetic  2.59 us (3%)
  matrix products  2.02 us (2%)
    all_to_all x3, blocking collectives, gather_plane(): got = lax.all_to_all(copies, ('y', 'x'), 0, 0, tiled=True)  42.2 us
    all_to_all x1, starting transfers between devices, on_device(): got_all = lax.all_to_all(copies, ('zh', 'q'), 0, 0, tiled=True)  11.5 us
    ppermute x1, starting transfers between devices, on_device(): lax.ppermute(quarter, ('zh',) + LINE, [(z, 15 - z) for z in range(16)])  10.5 us
    ppermute x1, waiting for transfers between devices, on_device(): half = pair_up(b, quarter, lax.ppermute(quarter, 'b', swap))  8.96 us
    pallas_call x2, Pallas kernels, product(): pl.pallas_call(functools.partial(product_kernel, flips), out_shape=jax.Sh...  6.99 us
    all_to_all x1, waiting for transfers between devices, on_device(): got_all = lax.all_to_all(copies, ('zh', 'q'), 0, 0, tiled=True)  5.2 us
    ppermute x1, starting transfers between devices, on_device(): passed = lax.ppermute(keep[0] + moved[0], 'b', swap)  3.82 us
  transfers between devices with their start and end apart: 6, of which 3 were waited for; matrix products, arithmetic and copies ran while one was open for 2% of the time, Pallas kernels for 3%

profile of v9, /device:TPU:2, one launch (start us, length us, event | category | flops | bytes accessed | tf_op | source)
XLA Modules:
  0.0 102.0 jit_solution(18052786874255318775)
XLA Ops:
  0.0 0.0 slice-start
  0.0 0.0 copy-start.1
  0.0 3.5 %shard_map.56 = f32[2,4,64,128]{3,2,1,0:T(8,128)} custom-call(f32[64,512]{1,0:T(8,128)} %bitcast.66, f32[512,2048]{1,0:T(8,128)} %solved_ref.3), custom_call_target="tpu_custom_call" | custom-call | flops 200000000 | bytes 2097152 | tf_op jit(solution)/shard_map/pallas_call | solution.py:70
  3.5 1.9 %collective-permute-start = (f32[2,4,64,128]{3,2,1,0:T(8,128)}, f32[2,4,64,128]{3,2,1,0:T(8,128)S(1)}, u32[]{:S(2)}, u32[]{:S(2)}) collective-permute-start(f32[2,4,64,128]{3,2,1,0:T(8,128)} %shard_map.56), channel_id=1, source_target_pairs={{0,1},{1,0},{2,3},{3,2},{4,5},{5,4},{6,7},{7,6},{8,9},{9,8},{10,11... | collective-permute-start | bytes 786440 | tf_op jit(solution)/shard_map/ppermute | solution.py:107
  5.5 0.0 copy-start
  5.5 3.5 %shard_map.55 = f32[2,4,64,128]{3,2,1,0:T(8,128)} custom-call(f32[64,512]{1,0:T(8,128)} %bitcast.67, f32[512,2048]{1,0:T(8,128)} %solved_ref.3, f32[64,128]{1,0:T(8,128)} %bitcast.71), custom_call_target="tpu_custom_call" | custom-call | flops 200000000 | bytes 2097152 | tf_op jit(solution)/shard_map/pallas_call | solution.py:70
  8.9 0.0 collective-permute-done
  9.0 0.9 fusion
  9.9 3.8 %collective-permute-start.1 = (f32[4,64,128]{2,1,0:T(8,128)S(1)}, f32[4,64,128]{2,1,0:T(8,128)S(1)}, u32[]{:S(2)}, u32[]{:S(2)}) collective-permute-start(f32[4,64,128]{2,1,0:T(8,128)S(1)} %fusion), channel_id=1, source_target_pairs={{0,2},{2,0},{1,3},{3,1},{4,6},{6,4},{5,7},{7,5},{8,10},{10,8},{9,1... | collective-permute-start | bytes 393224 | tf_op jit(solution)/shard_map/ppermute | solution.py:109
  13.7 0.0 slice-done
  13.7 0.0 copy-done.1
  13.8 10.5 %collective-permute-start.2 = (f32[16,1024]{1,0:T(8,128)S(1)}, f32[16,1024]{1,0:T(8,128)S(1)}, u32[]{:S(2)}, u32[]{:S(2)}) collective-permute-start(f32[16,1024]{1,0:T(8,128)S(1)} %bitcast_select_fusion), channel_id=1, source_target_pairs={{0,30},{2,28},{4,26},{6,24},{8,22},{10,20},{12,18},{14,16},{16,14}... | collective-permute-start | bytes 196616 | tf_op jit(solution)/shard_map/ppermute | solution.py:104
  24.3 0.0 collective-permute-done.1
  24.3 0.9 fusion.2
  25.2 0.7 broadcast_in_dim.10
  25.9 11.5 %all-to-all-start = ((f32[8,64,128]{2,1,0:T(8,128)}), f32[8,64,128]{2,1,0:T(8,128)S(1)}, u32[]{:S(2)}, u32[]{:S(2)}) async-start(f32[8,64,128]{2,1,0:T(8,128)} %bitcast.4), calls=%async_computation | async-start | bytes 524288 | tf_op jit(solution)/shard_map/all_to_all | solution.py:115
  37.4 0.0 collective-permute-done.2
  37.4 1.9 %collective-permute-start.3 = (f32[16,1024]{1,0:T(8,128)S(1)}, f32[16,1024]{1,0:T(8,128)S(1)}, u32[]{:S(2)}, u32[]{:S(2)}) collective-permute-start(f32[16,1024]{1,0:T(8,128)S(1)} %collective-permute-done.2), channel_id=1, source_target_pairs={{0,2},{2,0},{1,3},{3,1},{4,6},{6,4},{5,7},{7,5},{8,10},{10,8},{9,1... | collective-permute-start | bytes 196616 | tf_op jit(solution)/shard_map/ppermute | solution.py:111
  39.4 9.0 %collective-permute-done.3 = f32[16,1024]{1,0:T(8,128)S(1)} collective-permute-done((f32[16,1024]{1,0:T(8,128)S(1)}, f32[16,1024]{1,0:T(8,128)S(1)}, u32[]{:S(2)}, u32[]{:S(2)}) %collective-permute-start.3) | collective-permute-done | bytes 65568 | tf_op jit(solution)/shard_map/ppermute | solution.py:111
  48.4 1.9 %collective-permute-start.4 = (f32[2,16,1024]{2,1,0:T(8,128)S(1)}, f32[2,16,1024]{2,1,0:T(8,128)S(1)}, u32[]{:S(2)}, u32[]{:S(2)}) collective-permute-start(f32[2,16,1024]{2,1,0:T(8,128)S(1)} %pad_maximum_fusion.1), channel_id=1, source_target_pairs={{0,1},{1,0},{2,3},{3,2},{4,5},{5,4},{6,7},{7,6},{8,9},{9,8},{10,11... | collective-permute-start | bytes 393224 | tf_op jit(solution)/shard_map/ppermute | solution.py:112
  50.3 1.3 %collective-permute-done.4 = f32[2,16,1024]{2,1,0:T(8,128)S(1)} collective-permute-done((f32[2,16,1024]{2,1,0:T(8,128)S(1)}, f32[2,16,1024]{2,1,0:T(8,128)S(1)}, u32[]{:S(2)}, u32[]{:S(2)}) %collective-permute-start.4) | collective-permute-done | bytes 131104 | tf_op jit(solution)/shard_map/ppermute | solution.py:112
  51.7 5.2 %all-to-all-done = f32[8,64,128]{2,1,0:T(8,128)S(1)} async-done(((f32[8,64,128]{2,1,0:T(8,128)}), f32[8,64,128]{2,1,0:T(8,128)S(1)}, u32[]{:S(2)}, u32[]{:S(2)}) %all-to-all-start) | async-done | bytes 262176 | tf_op jit(solution)/shard_map/all_to_all | solution.py:115
  57.0 16.0 %all_to_all.20 = f32[16,64,128]{2,1,0:T(8,128)S(1)} all-to-all(f32[16,64,128]{2,1,0:T(8,128)S(1)} %broadcast_in_dim.12), channel_id=1, replica_groups=mesh['y'=4,'x'=4,'zh'=2,'q'=4,'b'=2,'core'=2] {'y','x'}, dimensions={0} | all-to-all | bytes 1048576 | tf_op jit(solution)/shard_map/all_to_all | solution.py:94
  73.0 0.0 copy-done
  73.0 0.4 fusion.8
  73.4 0.4 fusion.6
  73.9 13.1 %all_to_all.21 = f32[16,64,128]{2,1,0:T(8,128)S(1)} all-to-all(f32[16,64,128]{2,1,0:T(8,128)S(1)} %broadcast_in_dim.13), channel_id=1, replica_groups=mesh['y'=4,'x'=4,'zh'=2,'q'=4,'b'=2,'core'=2] {'y','x'}, dimensions={0} | all-to-all | bytes 1048576 | tf_op jit(solution)/shard_map/all_to_all | solution.py:94
  87.0 0.4 fusion.4
  87.4 0.4 convolution_bitcast_fusion.1
  87.9 13.1 %all_to_all.22 = f32[16,64,128]{2,1,0:T(8,128)S(1)} all-to-all(f32[16,64,128]{2,1,0:T(8,128)S(1)} %broadcast_in_dim.14), channel_id=1, replica_groups=mesh['y'=4,'x'=4,'zh'=2,'q'=4,'b'=2,'core'=2] {'y','x'}, dimensions={0} | all-to-all | bytes 1048576 | tf_op jit(solution)/shard_map/all_to_all | solution.py:94
  100.9 0.4 convolution_bitcast_fusion
  101.4 0.6 pad_maximum_fusion.2
  (12 shorter events, 0.3 us)
Async XLA Ops:
  0.0 13.7 %slice-start = ((f32[2,32,1024]{2,1,0:T(8,128)}), f32[1,32,1024]{2,1,0:T(8,128)S(1)}, s32[]{:S(2)}) async-start(f32[2,32,1024]{2,1,0:T(8,128)} %param.6), calls=%async_computation.4 | async-start | bytes 262144 | tf_op jit(solution)/shard_map/slice | solution.py:126
  0.0 13.7 %copy-start.1 = (f32[32,1024]{1,0:T(8,128)S(1)}, f32[32,1024]{1,0:T(8,128)}, u32[]{:S(2)}) copy-start(f32[32,1024]{1,0:T(8,128)} %param.7) | copy-start | bytes 393220
  3.5 5.4 %collective-permute-start = (f32[2,4,64,128]{3,2,1,0:T(8,128)}, f32[2,4,64,128]{3,2,1,0:T(8,128)S(1)}, u32[]{:S(2)}, u32[]{:S(2)}) collective-permute-start(f32[2,4,64,128]{3,2,1,0:T(8,128)} %shard_map.56), channel_id=1, source_target_pairs={{0,1},{1,0},{2,3},{3,2},{4,5},{5,4},{6,7},{7,6},{8,9},{9,8},{10,11... | collective-permute-start | bytes 786440 | tf_op jit(solution)/shard_map/ppermute | solution.py:107
  5.5 67.5 %copy-start = (f32[2,32,1024]{2,1,0:T(8,128)S(1)}, f32[2,32,1024]{2,1,0:T(8,128)}, u32[]{:S(2)}) copy-start(f32[2,32,1024]{2,1,0:T(8,128)} %param.6) | copy-start | bytes 786436
  9.9 14.4 %collective-permute-start.1 = (f32[4,64,128]{2,1,0:T(8,128)S(1)}, f32[4,64,128]{2,1,0:T(8,128)S(1)}, u32[]{:S(2)}, u32[]{:S(2)}) collective-permute-start(f32[4,64,128]{2,1,0:T(8,128)S(1)} %fusion), channel_id=1, source_target_pairs={{0,2},{2,0},{1,3},{3,1},{4,6},{6,4},{5,7},{7,5},{8,10},{10,8},{9,1... | collective-permute-start | bytes 393224 | tf_op jit(solution)/shard_map/ppermute | solution.py:109
  13.8 23.7 %collective-permute-start.2 = (f32[16,1024]{1,0:T(8,128)S(1)}, f32[16,1024]{1,0:T(8,128)S(1)}, u32[]{:S(2)}, u32[]{:S(2)}) collective-permute-start(f32[16,1024]{1,0:T(8,128)S(1)} %bitcast_select_fusion), channel_id=1, source_target_pairs={{0,30},{2,28},{4,26},{6,24},{8,22},{10,20},{12,18},{14,16},{16,14}... | collective-permute-start | bytes 196616 | tf_op jit(solution)/shard_map/ppermute | solution.py:104
  25.9 30.9 %all-to-all-start = ((f32[8,64,128]{2,1,0:T(8,128)}), f32[8,64,128]{2,1,0:T(8,128)S(1)}, u32[]{:S(2)}, u32[]{:S(2)}) async-start(f32[8,64,128]{2,1,0:T(8,128)} %bitcast.4), calls=%async_computation | async-start | bytes 524288 | tf_op jit(solution)/shard_map/all_to_all | solution.py:115
  37.4 10.9 %collective-permute-start.3 = (f32[16,1024]{1,0:T(8,128)S(1)}, f32[16,1024]{1,0:T(8,128)S(1)}, u32[]{:S(2)}, u32[]{:S(2)}) collective-permute-start(f32[16,1024]{1,0:T(8,128)S(1)} %collective-permute-done.2), channel_id=1, source_target_pairs={{0,2},{2,0},{1,3},{3,1},{4,6},{6,4},{5,7},{7,5},{8,10},{10,8},{9,1... | collective-permute-start | bytes 196616 | tf_op jit(solution)/shard_map/ppermute | solution.py:111
  48.4 3.2 %collective-permute-start.4 = (f32[2,16,1024]{2,1,0:T(8,128)S(1)}, f32[2,16,1024]{2,1,0:T(8,128)S(1)}, u32[]{:S(2)}, u32[]{:S(2)}) collective-permute-start(f32[2,16,1024]{2,1,0:T(8,128)S(1)} %pad_maximum_fusion.1), channel_id=1, source_target_pairs={{0,1},{1,0},{2,3},{3,2},{4,5},{5,4},{6,7},{7,6},{8,9},{9,8},{10,11... | collective-permute-start | bytes 393224 | tf_op jit(solution)/shard_map/ppermute | solution.py:112

commit v10 on v9

--- a/solution.py
+++ b/solution.py
@@ -79,8 +79,30 @@
             pltpu.SemaphoreType.DMA((count, 4)),
             pltpu.SemaphoreType.DMA((2,)),
         ],
-        compiler_params=pltpu.CompilerParams(vmem_limit_bytes=56 << 20),
+        compiler_params=pltpu.CompilerParams(vmem_limit_bytes=52 << 20),
         cost_estimate=pl.CostEstimate(flops=count * 10**8, bytes_accessed=count << 20, transcendentals=0),
+    )(*args)
+
+
+def pass_kernel(keep_ref, moved_ref, out_ref):
+    out_ref[...] = keep_ref[0] + moved_ref[0]
+
+
+def spread_kernel(keep_ref, moved_ref, passed_ref, out_ref):
+    total = keep_ref[1] + moved_ref[1] + passed_ref[...]
+    out_ref[0] = total
+    out_ref[1] = total
+
+
+def in_vmem(kernel, shape, *args):
+    vmem = pl.BlockSpec(memory_space=pltpu.VMEM)
+    return pl.pallas_call(
+        kernel,
+        out_shape=jax.ShapeDtypeStruct(shape, jnp.float32),
+        in_specs=[vmem] * len(args),
+        out_specs=vmem,
+        compiler_params=pltpu.CompilerParams(vmem_limit_bytes=4 << 20),
+        cost_estimate=pl.CostEstimate(flops=10**6, bytes_accessed=10**6, transcendentals=0),
     )(*args)
 
 
@@ -106,12 +128,10 @@
     panel = panel.reshape(64, 512)
     moved = lax.ppermute(product(((1, 1), (0, 1)), panel, solved), "core", swap)
     keep = product(((1, 0), (0, 0)), panel, solved, right_side.reshape(64, 128))
-    passed = lax.ppermute(keep[0] + moved[0], "b", swap)
-    total = keep[1] + moved[1] + passed
-    half = pair_up(b, quarter, lax.ppermute(quarter, "b", swap))
-    other = pair_up(core, half, lax.ppermute(half, "core", swap))
-    other = other.transpose(1, 0, 2, 3).reshape(2, 32, 1024)
-    copies = jnp.broadcast_to(total[None], (2, 4, 64, 128)).reshape(8, 64, 128)
+    passed = lax.ppermute(in_vmem(pass_kernel, (4, 64, 128), keep, moved), "b", swap)
+    copies = in_vmem(spread_kernel, (2, 4, 64, 128), keep, moved, passed).reshape(8, 64, 128)
+    half = pair_up(core, quarter, lax.ppermute(quarter, "core", swap))
+    other = pair_up(b, half, lax.ppermute(half, "b", swap)).reshape(2, 32, 1024)
     got_all = lax.all_to_all(copies, ("zh", "q"), 0, 0, tiled=True)
     first_half = zh == 0
     got_all, other, first_half = lax.optimization_barrier((got_all, other, first_half))

time: 103 us -> 99 us (0.961)
  other arithmetic: 2.59 us -> 0.73 us
  Pallas kernels: 6.99 us -> 5.32 us
    pallas_call x2, Pallas kernels: 6.99 us -> 4.58 us  [product(): pl.pallas_call(functools.partial(product_kernel, flips), out_shape=jax.Sh...]
    add x2 -> x0, other arithmetic: 1.85 us -> none  [the longest x1 0.93 us: on_device(): total = keep[1] + moved[1] + passed]
  transfers between devices with their start and end apart: 6 -> 6, of which waited for: 3 -> 3; matrix products, arithmetic and copies ran while one was open for 2% -> 0% of each run, Pallas kernels for 3% -> 3%
where the time goes in v10:
time: 99 us; the launch traced here: 98.6 us
  blocking collectives  42.2 us (43%)
  starting transfers between devices  31.6 us (32%)
  waiting for transfers between devices  15.3 us (15%)
  Pallas kernels  5.32 us (5%)
  matrix products  2.02 us (2%)
  local copies, waits for them, and re-layouts  1.06 us (1%)
    all_to_all x3, blocking collectives, gather_plane(): got = lax.all_to_all(copies, ('y', 'x'), 0, 0, tiled=True)  42.2 us
    all_to_all x1, starting transfers between devices, on_device(): got_all = lax.all_to_all(copies, ('zh', 'q'), 0, 0, tiled=True)  11.5 us
    ppermute x1, starting transfers between devices, on_device(): lax.ppermute(quarter, ('zh',) + LINE, [(z, 15 - z) for z in range(16)])  10.5 us
    ppermute x1, waiting for transfers between devices, on_device(): other = pair_up(b, half, lax.ppermute(half, 'b', swap)).reshape(2, 32, 1024)  8.5 us
    all_to_all x1, waiting for transfers between devices, on_device(): got_all = lax.all_to_all(copies, ('zh', 'q'), 0, 0, tiled=True)  5.61 us
    pallas_call x2, Pallas kernels, product(): pl.pallas_call(functools.partial(product_kernel, flips), out_shape=jax.Sh...  4.58 us
    ppermute x1, starting transfers between devices, on_device(): lax.ppermute(in_vmem(pass_kernel, (4, 64, 128), keep, moved), 'b', swap)  3.83 us
    dot_general x5, matrix products, mul(): jnp.dot(a, b, precision=lax.Precision.HIGHEST, preferred_element_type=jnp...  2.02 us
  transfers between devices with their start and end apart: 6, of which 3 were waited for; matrix products, arithmetic and copies ran while one was open for 0% of the time, Pallas kernels for 3%

profile of v10, /device:TPU:2, one launch (start us, length us, event | category | flops | bytes accessed | tf_op | source)
XLA Modules:
  0.0 98.6 jit_solution(5927726745439908825)
XLA Ops:
  0.0 0.0 copy-start
  0.0 0.9 copy-done
  0.9 2.3 %shard_map.56 = f32[2,4,64,128]{3,2,1,0:T(8,128)S(1)} custom-call(f32[64,512]{1,0:T(8,128)S(1)} %bitcast.45, f32[512,2048]{1,0:T(8,128)} %solved_ref.3), custom_call_target="tpu_custom_call" | custom-call | flops 200000000 | bytes 2097152 | tf_op jit(solution)/shard_map/pallas_call | solution.py:70
  3.2 1.9 %collective-permute-start = (f32[2,4,64,128]{3,2,1,0:T(8,128)S(1)}, f32[2,4,64,128]{3,2,1,0:T(8,128)S(1)}, u32[]{:S(2)}, u32[]{:S(2)}) collective-permute-start(f32[2,4,64,128]{3,2,1,0:T(8,128)S(1)} %shard_map.56), channel_id=1, source_target_pairs={{0,1},{1,0},{2,3},{3,2},{4,5},{5,4},{6,7},{7,6},{8,9},{9,8},{10,11... | collective-permute-start | bytes 786440 | tf_op jit(solution)/shard_map/ppermute | solution.py:129
  5.2 0.0 copy-done.1
  5.2 0.0 copy-done.2
  5.2 0.0 copy-start.3
  5.2 2.3 %shard_map.55.keep_ref = f32[2,4,64,128]{3,2,1,0:T(8,128)S(1)} custom-call(f32[64,512]{1,0:T(8,128)S(1)} %bitcast.46, f32[512,2048]{1,0:T(8,128)} %solved_ref.3, f32[64,128]{1,0:T(8,128)S(1)} %bitcast.47), custom_call_target="tpu_custom_call" | custom-call | flops 200000000 | bytes 2097152 | tf_op jit(solution)/shard_map/pallas_call | solution.py:70
  7.5 0.0 collective-permute-done.moved_ref
  7.5 3.8 %collective-permute-start.1 = (f32[4,64,128]{2,1,0:T(8,128)S(1)}, f32[4,64,128]{2,1,0:T(8,128)S(1)}, u32[]{:S(2)}, u32[]{:S(2)}) collective-permute-start(f32[4,64,128]{2,1,0:T(8,128)S(1)} %shard_map.57), channel_id=1, source_target_pairs={{0,2},{2,0},{1,3},{3,1},{4,6},{6,4},{5,7},{7,5},{8,10},{10,8},{9,1... | collective-permute-start | bytes 393224 | tf_op jit(solution)/shard_map/ppermute | solution.py:131
  11.3 0.0 slice-done
  11.4 0.0 copy-done.4
  11.4 10.5 %collective-permute-start.2 = (f32[16,1024]{1,0:T(8,128)S(1)}, f32[16,1024]{1,0:T(8,128)S(1)}, u32[]{:S(2)}, u32[]{:S(2)}) collective-permute-start(f32[16,1024]{1,0:T(8,128)S(1)} %bitcast_select_fusion), channel_id=1, source_target_pairs={{0,30},{2,28},{4,26},{6,24},{8,22},{10,20},{12,18},{14,16},{16,14}... | collective-permute-start | bytes 196616 | tf_op jit(solution)/shard_map/ppermute | solution.py:126
  21.9 0.0 collective-permute-done.1.passed_ref
  21.9 0.7 shard_map.58
  22.6 11.5 %all-to-all-start = ((f32[8,64,128]{2,1,0:T(8,128)}), f32[8,64,128]{2,1,0:T(8,128)S(1)}, u32[]{:S(2)}, u32[]{:S(2)}) async-start(f32[8,64,128]{2,1,0:T(8,128)} %bitcast.2), calls=%async_computation | async-start | bytes 524288 | tf_op jit(solution)/shard_map/all_to_all | solution.py:135
  34.1 0.0 collective-permute-done.2
  34.1 1.9 %collective-permute-start.3 = (f32[16,1024]{1,0:T(8,128)S(1)}, f32[16,1024]{1,0:T(8,128)S(1)}, u32[]{:S(2)}, u32[]{:S(2)}) collective-permute-start(f32[16,1024]{1,0:T(8,128)S(1)} %collective-permute-done.2), channel_id=1, source_target_pairs={{0,1},{1,0},{2,3},{3,2},{4,5},{5,4},{6,7},{7,6},{8,9},{9,8},{10,11... | collective-permute-start | bytes 196616 | tf_op jit(solution)/shard_map/ppermute | solution.py:133
  36.1 1.2 %collective-permute-done.3 = f32[16,1024]{1,0:T(8,128)S(1)} collective-permute-done((f32[16,1024]{1,0:T(8,128)S(1)}, f32[16,1024]{1,0:T(8,128)S(1)}, u32[]{:S(2)}, u32[]{:S(2)}) %collective-permute-start.3) | collective-permute-done | bytes 65568 | tf_op jit(solution)/shard_map/ppermute | solution.py:133
  37.3 1.9 %collective-permute-start.4 = (f32[2,16,1024]{2,1,0:T(8,128)S(1)}, f32[2,16,1024]{2,1,0:T(8,128)S(1)}, u32[]{:S(2)}, u32[]{:S(2)}) collective-permute-start(f32[2,16,1024]{2,1,0:T(8,128)S(1)} %pad_maximum_fusion.1), channel_id=1, source_target_pairs={{0,2},{2,0},{1,3},{3,1},{4,6},{6,4},{5,7},{7,5},{8,10},{10,8},{9,1... | collective-permute-start | bytes 393224 | tf_op jit(solution)/shard_map/ppermute | solution.py:134
  39.3 8.5 %collective-permute-done.4 = f32[2,16,1024]{2,1,0:T(8,128)S(1)} collective-permute-done((f32[2,16,1024]{2,1,0:T(8,128)S(1)}, f32[2,16,1024]{2,1,0:T(8,128)S(1)}, u32[]{:S(2)}, u32[]{:S(2)}) %collective-permute-start.4) | collective-permute-done | bytes 131104 | tf_op jit(solution)/shard_map/ppermute | solution.py:134
  47.8 5.6 %all-to-all-done = f32[8,64,128]{2,1,0:T(8,128)S(1)} async-done(((f32[8,64,128]{2,1,0:T(8,128)}), f32[8,64,128]{2,1,0:T(8,128)S(1)}, u32[]{:S(2)}, u32[]{:S(2)}) %all-to-all-start) | async-done | bytes 262176 | tf_op jit(solution)/shard_map/all_to_all | solution.py:135
  53.5 16.0 %all_to_all.20 = f32[16,64,128]{2,1,0:T(8,128)S(1)} all-to-all(f32[16,64,128]{2,1,0:T(8,128)S(1)} %broadcast_in_dim.9), channel_id=1, replica_groups=mesh['y'=4,'x'=4,'zh'=2,'q'=4,'b'=2,'core'=2] {'y','x'}, dimensions={0} | all-to-all | bytes 1048576 | tf_op jit(solution)/shard_map/all_to_all | solution.py:116
  69.6 0.0 copy-done.3
  69.6 0.4 fusion.5
  70.0 0.4 fusion.3
  70.5 13.2 %all_to_all.21 = f32[16,64,128]{2,1,0:T(8,128)S(1)} all-to-all(f32[16,64,128]{2,1,0:T(8,128)S(1)} %broadcast_in_dim.10), channel_id=1, replica_groups=mesh['y'=4,'x'=4,'zh'=2,'q'=4,'b'=2,'core'=2] {'y','x'}, dimensions={0} | all-to-all | bytes 1048576 | tf_op jit(solution)/shard_map/all_to_all | solution.py:116
  83.7 0.4 fusion.1
  84.0 0.4 convolution_bitcast_fusion.1
  84.5 13.0 %all_to_all.22 = f32[16,64,128]{2,1,0:T(8,128)S(1)} all-to-all(f32[16,64,128]{2,1,0:T(8,128)S(1)} %broadcast_in_dim.22), channel_id=1, replica_groups=mesh['y'=4,'x'=4,'zh'=2,'q'=4,'b'=2,'core'=2] {'y','x'}, dimensions={0} | all-to-all | bytes 1048576 | tf_op jit(solution)/shard_map/all_to_all | solution.py:116
  97.5 0.4 convolution_bitcast_fusion
  97.9 0.6 pad_maximum_fusion.2
  (17 shorter events, 0.3 us)
Async XLA Ops:
  0.0 0.9 copy-start
  0.9 4.2 %copy-start.1 = (f32[2,32,512]{2,1,0:T(8,128)S(1)}, f32[2,32,512]{2,1,0:T(8,128)}, u32[]{:S(2)}) copy-start(f32[2,32,512]{2,1,0:T(8,128)} %param.8) | copy-start | bytes 393220
  0.9 4.3 %copy-start.2 = (f32[2,32,128]{2,1,0:T(8,128)S(1)}, f32[2,32,128]{2,1,0:T(8,128)}, u32[]{:S(2)}) copy-start(f32[2,32,128]{2,1,0:T(8,128)} %param.5) | copy-start | bytes 98308
  0.9 10.4 %slice-start = ((f32[2,32,1024]{2,1,0:T(8,128)}), f32[1,32,1024]{2,1,0:T(8,128)S(1)}, s32[]{:S(2)}) async-start(f32[2,32,1024]{2,1,0:T(8,128)} %param.6), calls=%async_computation.4 | async-start | bytes 262144 | tf_op jit(solution)/shard_map/slice | solution.py:146
  0.9 10.4 %copy-start.4 = (f32[32,1024]{1,0:T(8,128)S(1)}, f32[32,1024]{1,0:T(8,128)}, u32[]{:S(2)}) copy-start(f32[32,1024]{1,0:T(8,128)} %param.7) | copy-start | bytes 393220
  3.2 4.3 %collective-permute-start = (f32[2,4,64,128]{3,2,1,0:T(8,128)S(1)}, f32[2,4,64,128]{3,2,1,0:T(8,128)S(1)}, u32[]{:S(2)}, u32[]{:S(2)}) collective-permute-start(f32[2,4,64,128]{3,2,1,0:T(8,128)S(1)} %shard_map.56), channel_id=1, source_target_pairs={{0,1},{1,0},{2,3},{3,2},{4,5},{5,4},{6,7},{7,6},{8,9},{9,8},{10,11... | collective-permute-start | bytes 786440 | tf_op jit(solution)/shard_map/ppermute | solution.py:129
  5.2 64.4 %copy-start.3 = (f32[2,32,1024]{2,1,0:T(8,128)S(1)}, f32[2,32,1024]{2,1,0:T(8,128)}, u32[]{:S(2)}) copy-start(f32[2,32,1024]{2,1,0:T(8,128)} %param.6) | copy-start | bytes 786436
  7.5 14.4 %collective-permute-start.1 = (f32[4,64,128]{2,1,0:T(8,128)S(1)}, f32[4,64,128]{2,1,0:T(8,128)S(1)}, u32[]{:S(2)}, u32[]{:S(2)}) collective-permute-start(f32[4,64,128]{2,1,0:T(8,128)S(1)} %shard_map.57), channel_id=1, source_target_pairs={{0,2},{2,0},{1,3},{3,1},{4,6},{6,4},{5,7},{7,5},{8,10},{10,8},{9,1... | collective-permute-start | bytes 393224 | tf_op jit(solution)/shard_map/ppermute | solution.py:131
  11.4 22.7 %collective-permute-start.2 = (f32[16,1024]{1,0:T(8,128)S(1)}, f32[16,1024]{1,0:T(8,128)S(1)}, u32[]{:S(2)}, u32[]{:S(2)}) collective-permute-start(f32[16,1024]{1,0:T(8,128)S(1)} %bitcast_select_fusion), channel_id=1, source_target_pairs={{0,30},{2,28},{4,26},{6,24},{8,22},{10,20},{12,18},{14,16},{16,14}... | collective-permute-start | bytes 196616 | tf_op jit(solution)/shard_map/ppermute | solution.py:126
  22.6 30.8 %all-to-all-start = ((f32[8,64,128]{2,1,0:T(8,128)}), f32[8,64,128]{2,1,0:T(8,128)S(1)}, u32[]{:S(2)}, u32[]{:S(2)}) async-start(f32[8,64,128]{2,1,0:T(8,128)} %bitcast.2), calls=%async_computation | async-start | bytes 524288 | tf_op jit(solution)/shard_map/all_to_all | solution.py:135
  34.1 3.1 %collective-permute-start.3 = (f32[16,1024]{1,0:T(8,128)S(1)}, f32[16,1024]{1,0:T(8,128)S(1)}, u32[]{:S(2)}, u32[]{:S(2)}) collective-permute-start(f32[16,1024]{1,0:T(8,128)S(1)} %collective-permute-done.2), channel_id=1, source_target_pairs={{0,1},{1,0},{2,3},{3,2},{4,5},{5,4},{6,7},{7,6},{8,9},{9,8},{10,11... | collective-permute-start | bytes 196616 | tf_op jit(solution)/shard_map/ppermute | solution.py:133
  37.3 10.4 %collective-permute-start.4 = (f32[2,16,1024]{2,1,0:T(8,128)S(1)}, f32[2,16,1024]{2,1,0:T(8,128)S(1)}, u32[]{:S(2)}, u32[]{:S(2)}) collective-permute-start(f32[2,16,1024]{2,1,0:T(8,128)S(1)} %pad_maximum_fusion.1), channel_id=1, source_target_pairs={{0,2},{2,0},{1,3},{3,1},{4,6},{6,4},{5,7},{7,5},{8,10},{10,8},{9,1... | collective-permute-start | bytes 393224 | tf_op jit(solution)/shard_map/ppermute | solution.py:134

commit v11 on v10

--- a/solution.py
+++ b/solution.py
@@ -10,10 +10,6 @@
 ROWS = ("y", "x", "zh")
 LINE = ("q", "b")
 COLS = LINE + ("core",)
-
-
-def mul(a, b):
-    return jnp.dot(a, b, precision=lax.Precision.HIGHEST, preferred_element_type=jnp.float32)
 
 
 def halves(x):
@@ -94,6 +90,29 @@
     out_ref[1] = total
 
 
+def times(factor, x):
+    f_high, f_low = halves(factor)
+    x_high, x_low = halves(x)
+    dot = functools.partial(jnp.dot, preferred_element_type=jnp.float32)
+    wide = dot(jnp.concatenate([f_high, f_low], axis=0), x_high)
+    rows = factor.shape[0]
+    return wide[rows:] + dot(f_high, x_low) + wide[:rows]
+
+
+def rows_kernel(step, mine_ref, theirs_ref, x_ref, *rest):
+    out_ref = rest[-1]
+    zh = lax.axis_index("zh")
+    got = times(jnp.concatenate([mine_ref[0], theirs_ref[step]], axis=0), x_ref[...])
+    got = jnp.where(zh == 0, got, jnp.concatenate([got[32:], got[:32]], axis=0))
+    out_ref[...] = rest[0][...] - got if len(rest) == 2 else got
+
+
+def last_kernel(factor_ref, x_ref, first_ref, out_ref):
+    zh = lax.axis_index("zh")
+    out_ref[0] = jnp.where(zh == 0, first_ref[:32], first_ref[32:])
+    out_ref[1] = times(factor_ref[1], x_ref[...])
+
+
 def in_vmem(kernel, shape, *args):
     vmem = pl.BlockSpec(memory_space=pltpu.VMEM)
     return pl.pallas_call(
@@ -101,7 +120,7 @@
         out_shape=jax.ShapeDtypeStruct(shape, jnp.float32),
         in_specs=[vmem] * len(args),
         out_specs=vmem,
-        compiler_params=pltpu.CompilerParams(vmem_limit_bytes=4 << 20),
+        compiler_params=pltpu.CompilerParams(vmem_limit_bytes=8 << 20),
         cost_estimate=pl.CostEstimate(flops=10**6, bytes_accessed=10**6, transcendentals=0),
     )(*args)
 
@@ -118,7 +137,7 @@
 
 
 def on_device(right_side, diag_inverse, coupling, panel, solved):
-    zh, b, core = (lax.axis_index(a) for a in ("zh", "b", "core"))
+    b, core = (lax.axis_index(a) for a in ("b", "core"))
     swap = [(0, 1), (1, 0)]
 
     rows = lambda x: lax.dynamic_slice_in_dim(x, 16 * core, 16, 0)
@@ -133,20 +152,17 @@
     half = pair_up(core, quarter, lax.ppermute(quarter, "core", swap))
     other = pair_up(b, half, lax.ppermute(half, "b", swap)).reshape(2, 32, 1024)
     got_all = lax.all_to_all(copies, ("zh", "q"), 0, 0, tiled=True)
-    first_half = zh == 0
-    got_all, other, first_half = lax.optimization_barrier((got_all, other, first_half))
+    got_all, other = lax.optimization_barrier((got_all, other))
     residual = got_all.reshape(2, 4, 2, 32, 128).sum(1)
     first_res = residual[:, 0].reshape(64, 128)
     second_part = residual[:, 1].reshape(64, 128)
 
-    def both(mine, theirs, x):
-        a, c = mul(mine, x), mul(theirs, x)
-        return jnp.where(first_half, jnp.concatenate([a, c]), jnp.concatenate([c, a])), a
-
-    first_sol, first_mine = both(diag_inverse[0], other[0], gather_plane(first_res))
-    cross, _ = both(coupling, other[1], gather_plane(first_sol))
-    second_mine = mul(diag_inverse[1], gather_plane(second_part - cross))
-    return jnp.stack([first_mine, second_mine])
+    first_rows, second_rows = (functools.partial(rows_kernel, step) for step in range(2))
+    first_sol = in_vmem(first_rows, (64, 128), diag_inverse, other, gather_plane(first_res))
+    second_res = in_vmem(
+        second_rows, (64, 128), coupling[None], other, gather_plane(first_sol), second_part
+    )
+    return in_vmem(last_kernel, (2, 32, 128), diag_inverse, gather_plane(second_res), first_sol)
 
 
 def solution(mesh):

time: 99 us -> 97.8 us (0.988)
  matrix products: 2.02 us -> 0 us
  Pallas kernels: 5.32 us -> 6.71 us
    dot_general x5 -> x0, matrix products: 2.02 us -> none  [mul(): jnp.dot(a, b, precision=lax.Precision.HIGHEST, preferred_element_type=jnp...]
    pallas_call x2 -> x5, Pallas kernels: 0.75 us -> 2.13 us  [in_vmem(): pl.pallas_call(kernel, out_shape=jax.ShapeDtypeStruct(shape, jnp.float32)...]
where the time goes in v11:
time: 97.8 us; the launch traced here: 97.3 us
  blocking collectives  42.2 us (43%)
  starting transfers between devices  31.6 us (32%)
  waiting for transfers between devices  15.4 us (16%)
  Pallas kernels  6.71 us (7%)
  local copies, waits for them, and re-layouts  1.06 us (1%)
    all_to_all x3, blocking collectives, gather_plane(): got = lax.all_to_all(copies, ('y', 'x'), 0, 0, tiled=True)  42.2 us
    all_to_all x1, starting transfers between devices, on_device(): got_all = lax.all_to_all(copies, ('zh', 'q'), 0, 0, tiled=True)  11.5 us
    ppermute x1, starting transfers between devices, on_device(): lax.ppermute(quarter, ('zh',) + LINE, [(z, 15 - z) for z in range(16)])  10.5 us
    ppermute x1, waiting for transfers between devices, on_device(): other = pair_up(b, half, lax.ppermute(half, 'b', swap)).reshape(2, 32, 1024)  8.52 us
    all_to_all x1, waiting for transfers between devices, on_device(): got_all = lax.all_to_all(copies, ('zh', 'q'), 0, 0, tiled=True)  5.69 us
    pallas_call x2, Pallas kernels, product(): pl.pallas_call(functools.partial(product_kernel, flips), out_shape=jax.Sh...  4.58 us
    ppermute x1, starting transfers between devices, on_device(): lax.ppermute(in_vmem(pass_kernel, (4, 64, 128), keep, moved), 'b', swap)  3.83 us
    pallas_call x5, Pallas kernels, in_vmem(): pl.pallas_call(kernel, out_shape=jax.ShapeDtypeStruct(shape, jnp.float32)...  2.13 us
  transfers between devices with their start and end apart: 6, of which 3 were waited for; matrix products, arithmetic and copies ran while one was open for 0% of the time, Pallas kernels for 3%

profile of v11, /device:TPU:2, one launch (start us, length us, event | category | flops | bytes accessed | tf_op | source)
XLA Modules:
  0.0 97.3 jit_solution(5364121127295853318)
XLA Ops:
  0.0 0.0 copy-start.1
  0.0 0.9 copy-done.1
  0.9 0.0 copy-start.2
  0.9 0.0 copy-start.4
  0.9 0.0 slice-start
  0.9 2.3 %shard_map.56 = f32[2,4,64,128]{3,2,1,0:T(8,128)S(1)} custom-call(f32[64,512]{1,0:T(8,128)S(1)} %bitcast.21, f32[512,2048]{1,0:T(8,128)} %solved_ref.3), custom_call_target="tpu_custom_call" | custom-call | flops 200000000 | bytes 2097152 | tf_op jit(solution)/shard_map/pallas_call | solution.py:66
  3.2 1.9 %collective-permute-start = (f32[2,4,64,128]{3,2,1,0:T(8,128)S(1)}, f32[2,4,64,128]{3,2,1,0:T(8,128)S(1)}, u32[]{:S(2)}, u32[]{:S(2)}) collective-permute-start(f32[2,4,64,128]{3,2,1,0:T(8,128)S(1)} %shard_map.56), channel_id=1, source_target_pairs={{0,1},{1,0},{2,3},{3,2},{4,5},{5,4},{6,7},{7,6},{8,9},{9,8},{10,11... | collective-permute-start | bytes 786440 | tf_op jit(solution)/shard_map/ppermute | solution.py:148
  5.1 0.0 copy-done.2
  5.2 0.0 copy-done.4
  5.2 0.0 copy-start
  5.2 2.3 %shard_map.55.keep_ref = f32[2,4,64,128]{3,2,1,0:T(8,128)S(1)} custom-call(f32[64,512]{1,0:T(8,128)S(1)} %bitcast.22, f32[512,2048]{1,0:T(8,128)} %solved_ref.3, f32[64,128]{1,0:T(8,128)S(1)} %bitcast.25), custom_call_target="tpu_custom_call" | custom-call | flops 200000000 | bytes 2097152 | tf_op jit(solution)/shard_map/pallas_call | solution.py:66
  7.5 0.0 collective-permute-done.moved_ref
  7.5 3.8 %collective-permute-start.1 = (f32[4,64,128]{2,1,0:T(8,128)S(1)}, f32[4,64,128]{2,1,0:T(8,128)S(1)}, u32[]{:S(2)}, u32[]{:S(2)}) collective-permute-start(f32[4,64,128]{2,1,0:T(8,128)S(1)} %shard_map.57), channel_id=1, source_target_pairs={{0,2},{2,0},{1,3},{3,1},{4,6},{6,4},{5,7},{7,5},{8,10},{10,8},{9,1... | collective-permute-start | bytes 393224 | tf_op jit(solution)/shard_map/ppermute | solution.py:150
  11.3 0.0 slice-done
  11.4 0.0 copy-done.3
  11.4 10.5 %collective-permute-start.2 = (f32[16,1024]{1,0:T(8,128)S(1)}, f32[16,1024]{1,0:T(8,128)S(1)}, u32[]{:S(2)}, u32[]{:S(2)}) collective-permute-start(f32[16,1024]{1,0:T(8,128)S(1)} %bitcast_select_fusion), channel_id=1, source_target_pairs={{0,30},{2,28},{4,26},{6,24},{8,22},{10,20},{12,18},{14,16},{16,14}... | collective-permute-start | bytes 196616 | tf_op jit(solution)/shard_map/ppermute | solution.py:145
  21.9 0.0 collective-permute-done.1.passed_ref
  21.9 0.7 shard_map.58
  22.6 11.5 %all-to-all-start = ((f32[8,64,128]{2,1,0:T(8,128)}), f32[8,64,128]{2,1,0:T(8,128)S(1)}, u32[]{:S(2)}, u32[]{:S(2)}) async-start(f32[8,64,128]{2,1,0:T(8,128)} %bitcast.3), calls=%async_computation | async-start | bytes 524288 | tf_op jit(solution)/shard_map/all_to_all | solution.py:154
  34.1 0.0 collective-permute-done.2
  34.1 1.9 %collective-permute-start.3 = (f32[16,1024]{1,0:T(8,128)S(1)}, f32[16,1024]{1,0:T(8,128)S(1)}, u32[]{:S(2)}, u32[]{:S(2)}) collective-permute-start(f32[16,1024]{1,0:T(8,128)S(1)} %collective-permute-done.2), channel_id=1, source_target_pairs={{0,1},{1,0},{2,3},{3,2},{4,5},{5,4},{6,7},{7,6},{8,9},{9,8},{10,11... | collective-permute-start | bytes 196616 | tf_op jit(solution)/shard_map/ppermute | solution.py:152
  36.1 1.2 %collective-permute-done.3 = f32[16,1024]{1,0:T(8,128)S(1)} collective-permute-done((f32[16,1024]{1,0:T(8,128)S(1)}, f32[16,1024]{1,0:T(8,128)S(1)}, u32[]{:S(2)}, u32[]{:S(2)}) %collective-permute-start.3) | collective-permute-done | bytes 65568 | tf_op jit(solution)/shard_map/ppermute | solution.py:152
  37.3 1.9 %collective-permute-start.4 = (f32[2,16,1024]{2,1,0:T(8,128)S(1)}, f32[2,16,1024]{2,1,0:T(8,128)S(1)}, u32[]{:S(2)}, u32[]{:S(2)}) collective-permute-start(f32[2,16,1024]{2,1,0:T(8,128)S(1)} %pad_maximum_fusion.1), channel_id=1, source_target_pairs={{0,2},{2,0},{1,3},{3,1},{4,6},{6,4},{5,7},{7,5},{8,10},{10,8},{9,1... | collective-permute-start | bytes 393224 | tf_op jit(solution)/shard_map/ppermute | solution.py:153
  39.3 8.5 %collective-permute-done.4 = f32[2,16,1024]{2,1,0:T(8,128)S(1)} collective-permute-done((f32[2,16,1024]{2,1,0:T(8,128)S(1)}, f32[2,16,1024]{2,1,0:T(8,128)S(1)}, u32[]{:S(2)}, u32[]{:S(2)}) %collective-permute-start.4) | collective-permute-done | bytes 131104 | tf_op jit(solution)/shard_map/ppermute | solution.py:153
  47.8 5.7 %all-to-all-done = f32[8,64,128]{2,1,0:T(8,128)S(1)} async-done(((f32[8,64,128]{2,1,0:T(8,128)}), f32[8,64,128]{2,1,0:T(8,128)S(1)}, u32[]{:S(2)}, u32[]{:S(2)}) %all-to-all-start) | async-done | bytes 262176 | tf_op jit(solution)/shard_map/all_to_all | solution.py:154
  53.6 16.0 %all_to_all.20 = f32[16,64,128]{2,1,0:T(8,128)S(1)} all-to-all(f32[16,64,128]{2,1,0:T(8,128)S(1)} %broadcast_in_dim.24), channel_id=1, replica_groups=mesh['y'=4,'x'=4,'zh'=2,'q'=4,'b'=2,'core'=2] {'y','x'}, dimensions={0} | all-to-all | bytes 1048576 | tf_op jit(solution)/shard_map/all_to_all | solution.py:135
  69.6 0.0 copy-done
  69.6 0.3 shard_map.59.first_ref
  70.0 13.4 %all_to_all.21 = f32[16,64,128]{2,1,0:T(8,128)S(1)} all-to-all(f32[16,64,128]{2,1,0:T(8,128)S(1)} %broadcast_in_dim.25), channel_id=1, replica_groups=mesh['y'=4,'x'=4,'zh'=2,'q'=4,'b'=2,'core'=2] {'y','x'}, dimensions={0} | all-to-all | bytes 1048576 | tf_op jit(solution)/shard_map/all_to_all | solution.py:135
  83.4 0.3 shard_map.60
  83.7 12.7 %all_to_all.22 = f32[16,64,128]{2,1,0:T(8,128)S(1)} all-to-all(f32[16,64,128]{2,1,0:T(8,128)S(1)} %broadcast_in_dim.26), channel_id=1, replica_groups=mesh['y'=4,'x'=4,'zh'=2,'q'=4,'b'=2,'core'=2] {'y','x'}, dimensions={0} | all-to-all | bytes 1048576 | tf_op jit(solution)/shard_map/all_to_all | solution.py:135
  96.5 0.9 shard_map.61
  (12 shorter events, 0.3 us)
Async XLA Ops:
  0.0 0.9 copy-start.1
  0.9 4.2 %copy-start.2 = (f32[2,32,512]{2,1,0:T(8,128)S(1)}, f32[2,32,512]{2,1,0:T(8,128)}, u32[]{:S(2)}) copy-start(f32[2,32,512]{2,1,0:T(8,128)} %param.8) | copy-start | bytes 393220
  0.9 4.3 %copy-start.4 = (f32[2,32,128]{2,1,0:T(8,128)S(1)}, f32[2,32,128]{2,1,0:T(8,128)}, u32[]{:S(2)}) copy-start(f32[2,32,128]{2,1,0:T(8,128)} %param.5) | copy-start | bytes 98308
  0.9 10.4 %slice-start = ((f32[2,32,1024]{2,1,0:T(8,128)}), f32[1,32,1024]{2,1,0:T(8,128)S(1)}, s32[]{:S(2)}) async-start(f32[2,32,1024]{2,1,0:T(8,128)} %factor_ref.1), calls=%async_computation.4 | async-start | bytes 262144 | tf_op jit(solution)/shard_map/slice | solution.py:144
  0.9 10.4 %copy-start.3 = (f32[32,1024]{1,0:T(8,128)S(1)}, f32[32,1024]{1,0:T(8,128)}, u32[]{:S(2)}) copy-start(f32[32,1024]{1,0:T(8,128)} %param.7) | copy-start | bytes 393220
  3.2 4.3 %collective-permute-start = (f32[2,4,64,128]{3,2,1,0:T(8,128)S(1)}, f32[2,4,64,128]{3,2,1,0:T(8,128)S(1)}, u32[]{:S(2)}, u32[]{:S(2)}) collective-permute-start(f32[2,4,64,128]{3,2,1,0:T(8,128)S(1)} %shard_map.56), channel_id=1, source_target_pairs={{0,1},{1,0},{2,3},{3,2},{4,5},{5,4},{6,7},{7,6},{8,9},{9,8},{10,11... | collective-permute-start | bytes 786440 | tf_op jit(solution)/shard_map/ppermute | solution.py:148
  5.2 64.5 %copy-start = (f32[2,32,1024]{2,1,0:T(8,128)S(1)}, f32[2,32,1024]{2,1,0:T(8,128)}, u32[]{:S(2)}) copy-start(f32[2,32,1024]{2,1,0:T(8,128)} %factor_ref.1) | copy-start | bytes 786436
  7.5 14.4 %collective-permute-start.1 = (f32[4,64,128]{2,1,0:T(8,128)S(1)}, f32[4,64,128]{2,1,0:T(8,128)S(1)}, u32[]{:S(2)}, u32[]{:S(2)}) collective-permute-start(f32[4,64,128]{2,1,0:T(8,128)S(1)} %shard_map.57), channel_id=1, source_target_pairs={{0,2},{2,0},{1,3},{3,1},{4,6},{6,4},{5,7},{7,5},{8,10},{10,8},{9,1... | collective-permute-start | bytes 393224 | tf_op jit(solution)/shard_map/ppermute | solution.py:150
  11.4 22.7 %collective-permute-start.2 = (f32[16,1024]{1,0:T(8,128)S(1)}, f32[16,1024]{1,0:T(8,128)S(1)}, u32[]{:S(2)}, u32[]{:S(2)}) collective-permute-start(f32[16,1024]{1,0:T(8,128)S(1)} %bitcast_select_fusion), channel_id=1, source_target_pairs={{0,30},{2,28},{4,26},{6,24},{8,22},{10,20},{12,18},{14,16},{16,14}... | collective-permute-start | bytes 196616 | tf_op jit(solution)/shard_map/ppermute | solution.py:145
  22.6 30.9 %all-to-all-start = ((f32[8,64,128]{2,1,0:T(8,128)}), f32[8,64,128]{2,1,0:T(8,128)S(1)}, u32[]{:S(2)}, u32[]{:S(2)}) async-start(f32[8,64,128]{2,1,0:T(8,128)} %bitcast.3), calls=%async_computation | async-start | bytes 524288 | tf_op jit(solution)/shard_map/all_to_all | solution.py:154
  34.1 3.1 %collective-permute-start.3 = (f32[16,1024]{1,0:T(8,128)S(1)}, f32[16,1024]{1,0:T(8,128)S(1)}, u32[]{:S(2)}, u32[]{:S(2)}) collective-permute-start(f32[16,1024]{1,0:T(8,128)S(1)} %collective-permute-done.2), channel_id=1, source_target_pairs={{0,1},{1,0},{2,3},{3,2},{4,5},{5,4},{6,7},{7,6},{8,9},{9,8},{10,11... | collective-permute-start | bytes 196616 | tf_op jit(solution)/shard_map/ppermute | solution.py:152
  37.3 10.4 %collective-permute-start.4 = (f32[2,16,1024]{2,1,0:T(8,128)S(1)}, f32[2,16,1024]{2,1,0:T(8,128)S(1)}, u32[]{:S(2)}, u32[]{:S(2)}) collective-permute-start(f32[2,16,1024]{2,1,0:T(8,128)S(1)} %pad_maximum_fusion.1), channel_id=1, source_target_pairs={{0,2},{2,0},{1,3},{3,1},{4,6},{6,4},{5,7},{7,5},{8,10},{10,8},{9,1... | collective-permute-start | bytes 393224 | tf_op jit(solution)/shard_map/ppermute | solution.py:153

commit v12 on v11

--- a/solution.py
+++ b/solution.py
@@ -86,11 +86,12 @@
 
 def spread_kernel(keep_ref, moved_ref, passed_ref, out_ref):
     total = keep_ref[1] + moved_ref[1] + passed_ref[...]
-    out_ref[0] = total
-    out_ref[1] = total
+    out_ref[:, 0] = total
+    out_ref[:, 1] = total
 
 
-def times(factor, x):
+def times(factor, blocks_ref):
+    x = jnp.concatenate([blocks_ref[4 * x + y] for y in range(4) for x in range(4)], axis=0)
     f_high, f_low = halves(factor)
     x_high, x_low = halves(x)
     dot = functools.partial(jnp.dot, preferred_element_type=jnp.float32)
@@ -102,7 +103,7 @@
 def rows_kernel(step, mine_ref, theirs_ref, x_ref, *rest):
     out_ref = rest[-1]
     zh = lax.axis_index("zh")
-    got = times(jnp.concatenate([mine_ref[0], theirs_ref[step]], axis=0), x_ref[...])
+    got = times(jnp.concatenate([mine_ref[0], theirs_ref[step]], axis=0), x_ref)
     got = jnp.where(zh == 0, got, jnp.concatenate([got[32:], got[:32]], axis=0))
     out_ref[...] = rest[0][...] - got if len(rest) == 2 else got
 
@@ -110,7 +111,7 @@
 def last_kernel(factor_ref, x_ref, first_ref, out_ref):
     zh = lax.axis_index("zh")
     out_ref[0] = jnp.where(zh == 0, first_ref[:32], first_ref[32:])
-    out_ref[1] = times(factor_ref[1], x_ref[...])
+    out_ref[1] = times(factor_ref[1], x_ref)
 
 
 def in_vmem(kernel, shape, *args):
@@ -132,8 +133,7 @@
 
 def gather_plane(block):
     copies = jnp.broadcast_to(block[None], (16,) + block.shape)
-    got = lax.all_to_all(copies, ("y", "x"), 0, 0, tiled=True)
-    return got.reshape(16 * block.shape[0], block.shape[1])
+    return lax.all_to_all(copies, ("x", "y"), 0, 0, tiled=True)
 
 
 def on_device(right_side, diag_inverse, coupling, panel, solved):
@@ -148,12 +148,12 @@
     moved = lax.ppermute(product(((1, 1), (0, 1)), panel, solved), "core", swap)
     keep = product(((1, 0), (0, 0)), panel, solved, right_side.reshape(64, 128))
     passed = lax.ppermute(in_vmem(pass_kernel, (4, 64, 128), keep, moved), "b", swap)
-    copies = in_vmem(spread_kernel, (2, 4, 64, 128), keep, moved, passed).reshape(8, 64, 128)
+    copies = in_vmem(spread_kernel, (4, 2, 64, 128), keep, moved, passed).reshape(8, 64, 128)
     half = pair_up(core, quarter, lax.ppermute(quarter, "core", swap))
     other = pair_up(b, half, lax.ppermute(half, "b", swap)).reshape(2, 32, 1024)
-    got_all = lax.all_to_all(copies, ("zh", "q"), 0, 0, tiled=True)
+    got_all = lax.all_to_all(copies, ("q", "zh"), 0, 0, tiled=True)
     got_all, other = lax.optimization_barrier((got_all, other))
-    residual = got_all.reshape(2, 4, 2, 32, 128).sum(1)
+    residual = got_all.reshape(4, 2, 2, 32, 128).sum(0)
     first_res = residual[:, 0].reshape(64, 128)
     second_part = residual[:, 1].reshape(64, 128)
 

time: 97.8 us -> 95.8 us (0.980)
  the two profiles are of different devices: /device:TPU:2 before, /device:TPU:64 now
where the time goes in v12:
time: 95.8 us; the launch traced here: 95.4 us
  blocking collectives  43.6 us (46%)
  starting transfers between devices  31.2 us (33%)
  waiting for transfers between devices  12.5 us (13%)
  Pallas kernels  6.72 us (7%)
  local copies, waits for them, and re-layouts  1.06 us (1%)
    all_to_all x3, blocking collectives, gather_plane(): return lax.all_to_all(copies, ('x', 'y'), 0, 0, tiled=True)  43.6 us
    all_to_all x1, starting transfers between devices, on_device(): got_all = lax.all_to_all(copies, ('q', 'zh'), 0, 0, tiled=True)  11.2 us
    ppermute x1, starting transfers between devices, on_device(): lax.ppermute(quarter, ('zh',) + LINE, [(z, 15 - z) for z in range(16)])  10.5 us
    ppermute x1, waiting for transfers between devices, on_device(): other = pair_up(b, half, lax.ppermute(half, 'b', swap)).reshape(2, 32, 1024)  8 us
    pallas_call x2, Pallas kernels, product(): pl.pallas_call(functools.partial(product_kernel, flips), out_shape=jax.Sh...  4.58 us
    ppermute x1, starting transfers between devices, on_device(): lax.ppermute(in_vmem(pass_kernel, (4, 64, 128), keep, moved), 'b', swap)  3.82 us
    all_to_all x1, waiting for transfers between devices, on_device(): got_all = lax.all_to_all(copies, ('q', 'zh'), 0, 0, tiled=True)  3.23 us
    pallas_call x5, Pallas kernels, in_vmem(): pl.pallas_call(kernel, out_shape=jax.ShapeDtypeStruct(shape, jnp.float32)...  2.14 us
  transfers between devices with their start and end apart: 6, of which 3 were waited for; matrix products, arithmetic and copies ran while one was open for 0% of the time, Pallas kernels for 3%

profile of v12, /device:TPU:64, one launch (start us, length us, event | category | flops | bytes accessed | tf_op | source)
XLA Modules:
  0.0 95.4 jit_solution(2974529140493057696)
XLA Ops:
  0.0 0.0 copy-start.1
  0.0 0.9 copy-done.1
  0.9 0.0 copy-start.2
  0.9 0.0 copy-start.4
  0.9 0.0 slice-start
  0.9 2.3 %shard_map.56 = f32[2,4,64,128]{3,2,1,0:T(8,128)S(1)} custom-call(f32[64,512]{1,0:T(8,128)S(1)} %bitcast.15, f32[512,2048]{1,0:T(8,128)} %solved_ref.3), custom_call_target="tpu_custom_call" | custom-call | flops 200000000 | bytes 2097152 | tf_op jit(solution)/shard_map/pallas_call | solution.py:66
  3.2 1.9 %collective-permute-start = (f32[2,4,64,128]{3,2,1,0:T(8,128)S(1)}, f32[2,4,64,128]{3,2,1,0:T(8,128)S(1)}, u32[]{:S(2)}, u32[]{:S(2)}) collective-permute-start(f32[2,4,64,128]{3,2,1,0:T(8,128)S(1)} %shard_map.56), channel_id=1, source_target_pairs={{0,1},{1,0},{2,3},{3,2},{4,5},{5,4},{6,7},{7,6},{8,9},{9,8},{10,11... | collective-permute-start | bytes 786440 | tf_op jit(solution)/shard_map/ppermute | solution.py:148
  5.2 0.0 copy-done.2
  5.2 0.0 copy-done.4
  5.2 0.0 copy-start
  5.2 2.3 %shard_map.55.keep_ref = f32[2,4,64,128]{3,2,1,0:T(8,128)S(1)} custom-call(f32[64,512]{1,0:T(8,128)S(1)} %bitcast.16, f32[512,2048]{1,0:T(8,128)} %solved_ref.3, f32[64,128]{1,0:T(8,128)S(1)} %bitcast.19), custom_call_target="tpu_custom_call" | custom-call | flops 200000000 | bytes 2097152 | tf_op jit(solution)/shard_map/pallas_call | solution.py:66
  7.5 0.0 collective-permute-done.moved_ref
  7.5 3.8 %collective-permute-start.1 = (f32[4,64,128]{2,1,0:T(8,128)S(1)}, f32[4,64,128]{2,1,0:T(8,128)S(1)}, u32[]{:S(2)}, u32[]{:S(2)}) collective-permute-start(f32[4,64,128]{2,1,0:T(8,128)S(1)} %shard_map.57), channel_id=1, source_target_pairs={{0,2},{2,0},{1,3},{3,1},{4,6},{6,4},{5,7},{7,5},{8,10},{10,8},{9,1... | collective-permute-start | bytes 393224 | tf_op jit(solution)/shard_map/ppermute | solution.py:150
  11.3 0.0 slice-done
  11.4 0.0 copy-done.3
  11.4 10.5 %collective-permute-start.2 = (f32[16,1024]{1,0:T(8,128)S(1)}, f32[16,1024]{1,0:T(8,128)S(1)}, u32[]{:S(2)}, u32[]{:S(2)}) collective-permute-start(f32[16,1024]{1,0:T(8,128)S(1)} %bitcast_select_fusion), channel_id=1, source_target_pairs={{0,30},{2,28},{4,26},{6,24},{8,22},{10,20},{12,18},{14,16},{16,14}... | collective-permute-start | bytes 196616 | tf_op jit(solution)/shard_map/ppermute | solution.py:145
  21.9 0.0 collective-permute-done.1.passed_ref
  21.9 0.7 shard_map.58
  22.6 11.2 %all-to-all-start = ((f32[8,64,128]{2,1,0:T(8,128)}), f32[8,64,128]{2,1,0:T(8,128)S(1)}, u32[]{:S(2)}, u32[]{:S(2)}) async-start(f32[8,64,128]{2,1,0:T(8,128)} %bitcast.3), calls=%async_computation | async-start | bytes 524288 | tf_op jit(solution)/shard_map/all_to_all | solution.py:154
  33.8 0.0 collective-permute-done.2
  33.8 1.9 %collective-permute-start.3 = (f32[16,1024]{1,0:T(8,128)S(1)}, f32[16,1024]{1,0:T(8,128)S(1)}, u32[]{:S(2)}, u32[]{:S(2)}) collective-permute-start(f32[16,1024]{1,0:T(8,128)S(1)} %collective-permute-done.2), channel_id=1, source_target_pairs={{0,1},{1,0},{2,3},{3,2},{4,5},{5,4},{6,7},{7,6},{8,9},{9,8},{10,11... | collective-permute-start | bytes 196616 | tf_op jit(solution)/shard_map/ppermute | solution.py:152
  35.7 1.2 %collective-permute-done.3 = f32[16,1024]{1,0:T(8,128)S(1)} collective-permute-done((f32[16,1024]{1,0:T(8,128)S(1)}, f32[16,1024]{1,0:T(8,128)S(1)}, u32[]{:S(2)}, u32[]{:S(2)}) %collective-permute-start.3) | collective-permute-done | bytes 65568 | tf_op jit(solution)/shard_map/ppermute | solution.py:152
  37.0 1.9 %collective-permute-start.4 = (f32[2,16,1024]{2,1,0:T(8,128)S(1)}, f32[2,16,1024]{2,1,0:T(8,128)S(1)}, u32[]{:S(2)}, u32[]{:S(2)}) collective-permute-start(f32[2,16,1024]{2,1,0:T(8,128)S(1)} %pad_maximum_fusion.1), channel_id=1, source_target_pairs={{0,2},{2,0},{1,3},{3,1},{4,6},{6,4},{5,7},{7,5},{8,10},{10,8},{9,1... | collective-permute-start | bytes 393224 | tf_op jit(solution)/shard_map/ppermute | solution.py:153
  38.9 8.0 %collective-permute-done.4 = f32[2,16,1024]{2,1,0:T(8,128)S(1)} collective-permute-done((f32[2,16,1024]{2,1,0:T(8,128)S(1)}, f32[2,16,1024]{2,1,0:T(8,128)S(1)}, u32[]{:S(2)}, u32[]{:S(2)}) %collective-permute-start.4) | collective-permute-done | bytes 131104 | tf_op jit(solution)/shard_map/ppermute | solution.py:153
  46.9 3.2 %all-to-all-done = f32[8,64,128]{2,1,0:T(8,128)S(1)} async-done(((f32[8,64,128]{2,1,0:T(8,128)}), f32[8,64,128]{2,1,0:T(8,128)S(1)}, u32[]{:S(2)}, u32[]{:S(2)}) %all-to-all-start) | async-done | bytes 262176 | tf_op jit(solution)/shard_map/all_to_all | solution.py:154
  50.3 16.9 %all_to_all.20.x_ref = f32[16,64,128]{2,1,0:T(8,128)S(1)} all-to-all(f32[16,64,128]{2,1,0:T(8,128)S(1)} %broadcast_in_dim.24), channel_id=1, replica_groups=mesh['y'=4,'x'=4,'zh'=2,'q'=4,'b'=2,'core'=2] {'x','y'}, dimensions={0} | all-to-all | bytes 1048576 | tf_op jit(solution)/shard_map/all_to_all | solution.py:136
  67.2 0.0 copy-done
  67.2 0.3 shard_map.59.first_ref
  67.5 13.3 %all_to_all.21.x_ref = f32[16,64,128]{2,1,0:T(8,128)S(1)} all-to-all(f32[16,64,128]{2,1,0:T(8,128)S(1)} %broadcast_in_dim.25), channel_id=1, replica_groups=mesh['y'=4,'x'=4,'zh'=2,'q'=4,'b'=2,'core'=2] {'x','y'}, dimensions={0} | all-to-all | bytes 1048576 | tf_op jit(solution)/shard_map/all_to_all | solution.py:136
  80.8 0.3 shard_map.60
  81.1 13.3 %all_to_all.22.x_ref = f32[16,64,128]{2,1,0:T(8,128)S(1)} all-to-all(f32[16,64,128]{2,1,0:T(8,128)S(1)} %broadcast_in_dim.26), channel_id=1, replica_groups=mesh['y'=4,'x'=4,'zh'=2,'q'=4,'b'=2,'core'=2] {'x','y'}, dimensions={0} | all-to-all | bytes 1048576 | tf_op jit(solution)/shard_map/all_to_all | solution.py:136
  94.5 0.9 shard_map.61
  (12 shorter events, 0.3 us)
Async XLA Ops:
  0.0 0.9 copy-start.1
  0.9 4.2 %copy-start.2 = (f32[2,32,512]{2,1,0:T(8,128)S(1)}, f32[2,32,512]{2,1,0:T(8,128)}, u32[]{:S(2)}) copy-start(f32[2,32,512]{2,1,0:T(8,128)} %param.8) | copy-start | bytes 393220
  0.9 4.3 %copy-start.4 = (f32[2,32,128]{2,1,0:T(8,128)S(1)}, f32[2,32,128]{2,1,0:T(8,128)}, u32[]{:S(2)}) copy-start(f32[2,32,128]{2,1,0:T(8,128)} %param.5) | copy-start | bytes 98308
  0.9 10.4 %slice-start = ((f32[2,32,1024]{2,1,0:T(8,128)}), f32[1,32,1024]{2,1,0:T(8,128)S(1)}, s32[]{:S(2)}) async-start(f32[2,32,1024]{2,1,0:T(8,128)} %factor_ref.1), calls=%async_computation.4 | async-start | bytes 262144 | tf_op jit(solution)/shard_map/slice | solution.py:144
  0.9 10.4 %copy-start.3 = (f32[32,1024]{1,0:T(8,128)S(1)}, f32[32,1024]{1,0:T(8,128)}, u32[]{:S(2)}) copy-start(f32[32,1024]{1,0:T(8,128)} %param.7) | copy-start | bytes 393220
  3.2 4.3 %collective-permute-start = (f32[2,4,64,128]{3,2,1,0:T(8,128)S(1)}, f32[2,4,64,128]{3,2,1,0:T(8,128)S(1)}, u32[]{:S(2)}, u32[]{:S(2)}) collective-permute-start(f32[2,4,64,128]{3,2,1,0:T(8,128)S(1)} %shard_map.56), channel_id=1, source_target_pairs={{0,1},{1,0},{2,3},{3,2},{4,5},{5,4},{6,7},{7,6},{8,9},{9,8},{10,11... | collective-permute-start | bytes 786440 | tf_op jit(solution)/shard_map/ppermute | solution.py:148
  5.2 62.0 %copy-start = (f32[2,32,1024]{2,1,0:T(8,128)S(1)}, f32[2,32,1024]{2,1,0:T(8,128)}, u32[]{:S(2)}) copy-start(f32[2,32,1024]{2,1,0:T(8,128)} %factor_ref.1) | copy-start | bytes 786436
  7.5 14.4 %collective-permute-start.1 = (f32[4,64,128]{2,1,0:T(8,128)S(1)}, f32[4,64,128]{2,1,0:T(8,128)S(1)}, u32[]{:S(2)}, u32[]{:S(2)}) collective-permute-start(f32[4,64,128]{2,1,0:T(8,128)S(1)} %shard_map.57), channel_id=1, source_target_pairs={{0,2},{2,0},{1,3},{3,1},{4,6},{6,4},{5,7},{7,5},{8,10},{10,8},{9,1... | collective-permute-start | bytes 393224 | tf_op jit(solution)/shard_map/ppermute | solution.py:150
  11.4 22.4 %collective-permute-start.2 = (f32[16,1024]{1,0:T(8,128)S(1)}, f32[16,1024]{1,0:T(8,128)S(1)}, u32[]{:S(2)}, u32[]{:S(2)}) collective-permute-start(f32[16,1024]{1,0:T(8,128)S(1)} %bitcast_select_fusion), channel_id=1, source_target_pairs={{0,30},{2,28},{4,26},{6,24},{8,22},{10,20},{12,18},{14,16},{16,14}... | collective-permute-start | bytes 196616 | tf_op jit(solution)/shard_map/ppermute | solution.py:145
  22.6 27.6 %all-to-all-start = ((f32[8,64,128]{2,1,0:T(8,128)}), f32[8,64,128]{2,1,0:T(8,128)S(1)}, u32[]{:S(2)}, u32[]{:S(2)}) async-start(f32[8,64,128]{2,1,0:T(8,128)} %bitcast.3), calls=%async_computation | async-start | bytes 524288 | tf_op jit(solution)/shard_map/all_to_all | solution.py:154
  33.8 3.1 %collective-permute-start.3 = (f32[16,1024]{1,0:T(8,128)S(1)}, f32[16,1024]{1,0:T(8,128)S(1)}, u32[]{:S(2)}, u32[]{:S(2)}) collective-permute-start(f32[16,1024]{1,0:T(8,128)S(1)} %collective-permute-done.2), channel_id=1, source_target_pairs={{0,1},{1,0},{2,3},{3,2},{4,5},{5,4},{6,7},{7,6},{8,9},{9,8},{10,11... | collective-permute-start | bytes 196616 | tf_op jit(solution)/shard_map/ppermute | solution.py:152
  37.0 9.9 %collective-permute-start.4 = (f32[2,16,1024]{2,1,0:T(8,128)S(1)}, f32[2,16,1024]{2,1,0:T(8,128)S(1)}, u32[]{:S(2)}, u32[]{:S(2)}) collective-permute-start(f32[2,16,1024]{2,1,0:T(8,128)S(1)} %pad_maximum_fusion.1), channel_id=1, source_target_pairs={{0,2},{2,0},{1,3},{3,1},{4,6},{6,4},{5,7},{7,5},{8,10},{10,8},{9,1... | collective-permute-start | bytes 393224 | tf_op jit(solution)/shard_map/ppermute | solution.py:153

commit v13 on v12

--- a/solution.py
+++ b/solution.py
@@ -91,7 +91,7 @@
 
 
 def times(factor, blocks_ref):
-    x = jnp.concatenate([blocks_ref[4 * x + y] for y in range(4) for x in range(4)], axis=0)
+    x = blocks_ref[...].reshape(1024, 128)
     f_high, f_low = halves(factor)
     x_high, x_low = halves(x)
     dot = functools.partial(jnp.dot, preferred_element_type=jnp.float32)
@@ -133,7 +133,7 @@
 
 def gather_plane(block):
     copies = jnp.broadcast_to(block[None], (16,) + block.shape)
-    return lax.all_to_all(copies, ("x", "y"), 0, 0, tiled=True)
+    return lax.all_to_all(copies, ("y", "x"), 0, 0, tiled=True)
 
 
 def on_device(right_side, diag_inverse, coupling, panel, solved):

time: 95.8 us -> 95.4 us (level)
  no operation moved by 1% of the time
where the time goes in v13:
time: 95.4 us; the launch traced here: 94.9 us
  blocking collectives  43.1 us (45%)
  starting transfers between devices  31.2 us (33%)
  waiting for transfers between devices  12.5 us (13%)
  Pallas kernels  6.71 us (7%)
  local copies, waits for them, and re-layouts  1.06 us (1%)
    all_to_all x3, blocking collectives, gather_plane(): return lax.all_to_all(copies, ('y', 'x'), 0, 0, tiled=True)  43.1 us
    all_to_all x1, starting transfers between devices, on_device(): got_all = lax.all_to_all(copies, ('q', 'zh'), 0, 0, tiled=True)  11.2 us
    ppermute x1, starting transfers between devices, on_device(): lax.ppermute(quarter, ('zh',) + LINE, [(z, 15 - z) for z in range(16)])  10.5 us
    ppermute x1, waiting for transfers between devices, on_device(): other = pair_up(b, half, lax.ppermute(half, 'b', swap)).reshape(2, 32, 1024)  8 us
    pallas_call x2, Pallas kernels, product(): pl.pallas_call(functools.partial(product_kernel, flips), out_shape=jax.Sh...  4.58 us
    ppermute x1, starting transfers between devices, on_device(): lax.ppermute(in_vmem(pass_kernel, (4, 64, 128), keep, moved), 'b', swap)  3.82 us
    all_to_all x1, waiting for transfers between devices, on_device(): got_all = lax.all_to_all(copies, ('q', 'zh'), 0, 0, tiled=True)  3.23 us
    pallas_call x5, Pallas kernels, in_vmem(): pl.pallas_call(kernel, out_shape=jax.ShapeDtypeStruct(shape, jnp.float32)...  2.13 us
  transfers between devices with their start and end apart: 6, of which 3 were waited for; matrix products, arithmetic and copies ran while one was open for 0% of the time, Pallas kernels for 3%

profile of v13, /device:TPU:64, one launch (start us, length us, event | category | flops | bytes accessed | tf_op | source)
XLA Modules:
  0.0 94.9 jit_solution(6355238457400181397)
XLA Ops:
  0.0 0.0 copy-start.1
  0.0 0.9 copy-done.1
  0.9 0.0 copy-start.2
  0.9 0.0 copy-start.4
  0.9 0.0 slice-start
  0.9 2.3 %shard_map.56 = f32[2,4,64,128]{3,2,1,0:T(8,128)S(1)} custom-call(f32[64,512]{1,0:T(8,128)S(1)} %bitcast.15, f32[512,2048]{1,0:T(8,128)} %solved_ref.3), custom_call_target="tpu_custom_call" | custom-call | flops 200000000 | bytes 2097152 | tf_op jit(solution)/shard_map/pallas_call | solution.py:66
  3.2 1.9 %collective-permute-start = (f32[2,4,64,128]{3,2,1,0:T(8,128)S(1)}, f32[2,4,64,128]{3,2,1,0:T(8,128)S(1)}, u32[]{:S(2)}, u32[]{:S(2)}) collective-permute-start(f32[2,4,64,128]{3,2,1,0:T(8,128)S(1)} %shard_map.56), channel_id=1, source_target_pairs={{0,1},{1,0},{2,3},{3,2},{4,5},{5,4},{6,7},{7,6},{8,9},{9,8},{10,11... | collective-permute-start | bytes 786440 | tf_op jit(solution)/shard_map/ppermute | solution.py:148
  5.2 0.0 copy-done.2
  5.2 0.0 copy-done.4
  5.2 0.0 copy-start
  5.2 2.3 %shard_map.55.keep_ref = f32[2,4,64,128]{3,2,1,0:T(8,128)S(1)} custom-call(f32[64,512]{1,0:T(8,128)S(1)} %bitcast.16, f32[512,2048]{1,0:T(8,128)} %solved_ref.3, f32[64,128]{1,0:T(8,128)S(1)} %bitcast.19), custom_call_target="tpu_custom_call" | custom-call | flops 200000000 | bytes 2097152 | tf_op jit(solution)/shard_map/pallas_call | solution.py:66
  7.5 0.0 collective-permute-done.moved_ref
  7.5 3.8 %collective-permute-start.1 = (f32[4,64,128]{2,1,0:T(8,128)S(1)}, f32[4,64,128]{2,1,0:T(8,128)S(1)}, u32[]{:S(2)}, u32[]{:S(2)}) collective-permute-start(f32[4,64,128]{2,1,0:T(8,128)S(1)} %shard_map.57), channel_id=1, source_target_pairs={{0,2},{2,0},{1,3},{3,1},{4,6},{6,4},{5,7},{7,5},{8,10},{10,8},{9,1... | collective-permute-start | bytes 393224 | tf_op jit(solution)/shard_map/ppermute | solution.py:150
  11.3 0.0 slice-done
  11.4 0.0 copy-done.3
  11.4 10.5 %collective-permute-start.2 = (f32[16,1024]{1,0:T(8,128)S(1)}, f32[16,1024]{1,0:T(8,128)S(1)}, u32[]{:S(2)}, u32[]{:S(2)}) collective-permute-start(f32[16,1024]{1,0:T(8,128)S(1)} %bitcast_select_fusion), channel_id=1, source_target_pairs={{0,30},{2,28},{4,26},{6,24},{8,22},{10,20},{12,18},{14,16},{16,14}... | collective-permute-start | bytes 196616 | tf_op jit(solution)/shard_map/ppermute | solution.py:145
  21.9 0.0 collective-permute-done.1.passed_ref
  21.9 0.7 shard_map.58
  22.6 11.2 %all-to-all-start = ((f32[8,64,128]{2,1,0:T(8,128)}), f32[8,64,128]{2,1,0:T(8,128)S(1)}, u32[]{:S(2)}, u32[]{:S(2)}) async-start(f32[8,64,128]{2,1,0:T(8,128)} %bitcast.3), calls=%async_computation | async-start | bytes 524288 | tf_op jit(solution)/shard_map/all_to_all | solution.py:154
  33.8 0.0 collective-permute-done.2
  33.8 1.9 %collective-permute-start.3 = (f32[16,1024]{1,0:T(8,128)S(1)}, f32[16,1024]{1,0:T(8,128)S(1)}, u32[]{:S(2)}, u32[]{:S(2)}) collective-permute-start(f32[16,1024]{1,0:T(8,128)S(1)} %collective-permute-done.2), channel_id=1, source_target_pairs={{0,1},{1,0},{2,3},{3,2},{4,5},{5,4},{6,7},{7,6},{8,9},{9,8},{10,11... | collective-permute-start | bytes 196616 | tf_op jit(solution)/shard_map/ppermute | solution.py:152
  35.7 1.2 %collective-permute-done.3 = f32[16,1024]{1,0:T(8,128)S(1)} collective-permute-done((f32[16,1024]{1,0:T(8,128)S(1)}, f32[16,1024]{1,0:T(8,128)S(1)}, u32[]{:S(2)}, u32[]{:S(2)}) %collective-permute-start.3) | collective-permute-done | bytes 65568 | tf_op jit(solution)/shard_map/ppermute | solution.py:152
  37.0 1.9 %collective-permute-start.4 = (f32[2,16,1024]{2,1,0:T(8,128)S(1)}, f32[2,16,1024]{2,1,0:T(8,128)S(1)}, u32[]{:S(2)}, u32[]{:S(2)}) collective-permute-start(f32[2,16,1024]{2,1,0:T(8,128)S(1)} %pad_maximum_fusion.1), channel_id=1, source_target_pairs={{0,2},{2,0},{1,3},{3,1},{4,6},{6,4},{5,7},{7,5},{8,10},{10,8},{9,1... | collective-permute-start | bytes 393224 | tf_op jit(solution)/shard_map/ppermute | solution.py:153
  38.9 8.0 %collective-permute-done.4 = f32[2,16,1024]{2,1,0:T(8,128)S(1)} collective-permute-done((f32[2,16,1024]{2,1,0:T(8,128)S(1)}, f32[2,16,1024]{2,1,0:T(8,128)S(1)}, u32[]{:S(2)}, u32[]{:S(2)}) %collective-permute-start.4) | collective-permute-done | bytes 131104 | tf_op jit(solution)/shard_map/ppermute | solution.py:153
  46.9 3.2 %all-to-all-done = f32[8,64,128]{2,1,0:T(8,128)S(1)} async-done(((f32[8,64,128]{2,1,0:T(8,128)}), f32[8,64,128]{2,1,0:T(8,128)S(1)}, u32[]{:S(2)}, u32[]{:S(2)}) %all-to-all-start) | async-done | bytes 262176 | tf_op jit(solution)/shard_map/all_to_all | solution.py:154
  50.3 16.9 %all_to_all.20.x_ref = f32[16,64,128]{2,1,0:T(8,128)S(1)} all-to-all(f32[16,64,128]{2,1,0:T(8,128)S(1)} %broadcast_in_dim.24), channel_id=1, replica_groups=mesh['y'=4,'x'=4,'zh'=2,'q'=4,'b'=2,'core'=2] {'y','x'}, dimensions={0} | all-to-all | bytes 1048576 | tf_op jit(solution)/shard_map/all_to_all | solution.py:136
  67.2 0.0 copy-done
  67.2 0.3 shard_map.59.first_ref
  67.5 13.1 %all_to_all.21.x_ref = f32[16,64,128]{2,1,0:T(8,128)S(1)} all-to-all(f32[16,64,128]{2,1,0:T(8,128)S(1)} %broadcast_in_dim.25), channel_id=1, replica_groups=mesh['y'=4,'x'=4,'zh'=2,'q'=4,'b'=2,'core'=2] {'y','x'}, dimensions={0} | all-to-all | bytes 1048576 | tf_op jit(solution)/shard_map/all_to_all | solution.py:136
  80.6 0.3 shard_map.60
  80.9 13.1 %all_to_all.22.x_ref = f32[16,64,128]{2,1,0:T(8,128)S(1)} all-to-all(f32[16,64,128]{2,1,0:T(8,128)S(1)} %broadcast_in_dim.26), channel_id=1, replica_groups=mesh['y'=4,'x'=4,'zh'=2,'q'=4,'b'=2,'core'=2] {'y','x'}, dimensions={0} | all-to-all | bytes 1048576 | tf_op jit(solution)/shard_map/all_to_all | solution.py:136
  94.0 0.9 shard_map.61
  (12 shorter events, 0.3 us)
Async XLA Ops:
  0.0 0.9 copy-start.1
  0.9 4.2 %copy-start.2 = (f32[2,32,512]{2,1,0:T(8,128)S(1)}, f32[2,32,512]{2,1,0:T(8,128)}, u32[]{:S(2)}) copy-start(f32[2,32,512]{2,1,0:T(8,128)} %param.8) | copy-start | bytes 393220
  0.9 4.3 %copy-start.4 = (f32[2,32,128]{2,1,0:T(8,128)S(1)}, f32[2,32,128]{2,1,0:T(8,128)}, u32[]{:S(2)}) copy-start(f32[2,32,128]{2,1,0:T(8,128)} %param.5) | copy-start | bytes 98308
  0.9 10.4 %slice-start = ((f32[2,32,1024]{2,1,0:T(8,128)}), f32[1,32,1024]{2,1,0:T(8,128)S(1)}, s32[]{:S(2)}) async-start(f32[2,32,1024]{2,1,0:T(8,128)} %factor_ref.1), calls=%async_computation.4 | async-start | bytes 262144 | tf_op jit(solution)/shard_map/slice | solution.py:144
  0.9 10.4 %copy-start.3 = (f32[32,1024]{1,0:T(8,128)S(1)}, f32[32,1024]{1,0:T(8,128)}, u32[]{:S(2)}) copy-start(f32[32,1024]{1,0:T(8,128)} %param.7) | copy-start | bytes 393220
  3.2 4.3 %collective-permute-start = (f32[2,4,64,128]{3,2,1,0:T(8,128)S(1)}, f32[2,4,64,128]{3,2,1,0:T(8,128)S(1)}, u32[]{:S(2)}, u32[]{:S(2)}) collective-permute-start(f32[2,4,64,128]{3,2,1,0:T(8,128)S(1)} %shard_map.56), channel_id=1, source_target_pairs={{0,1},{1,0},{2,3},{3,2},{4,5},{5,4},{6,7},{7,6},{8,9},{9,8},{10,11... | collective-permute-start | bytes 786440 | tf_op jit(solution)/shard_map/ppermute | solution.py:148
  5.2 62.0 %copy-start = (f32[2,32,1024]{2,1,0:T(8,128)S(1)}, f32[2,32,1024]{2,1,0:T(8,128)}, u32[]{:S(2)}) copy-start(f32[2,32,1024]{2,1,0:T(8,128)} %factor_ref.1) | copy-start | bytes 786436
  7.5 14.4 %collective-permute-start.1 = (f32[4,64,128]{2,1,0:T(8,128)S(1)}, f32[4,64,128]{2,1,0:T(8,128)S(1)}, u32[]{:S(2)}, u32[]{:S(2)}) collective-permute-start(f32[4,64,128]{2,1,0:T(8,128)S(1)} %shard_map.57), channel_id=1, source_target_pairs={{0,2},{2,0},{1,3},{3,1},{4,6},{6,4},{5,7},{7,5},{8,10},{10,8},{9,1... | collective-permute-start | bytes 393224 | tf_op jit(solution)/shard_map/ppermute | solution.py:150
  11.4 22.4 %collective-permute-start.2 = (f32[16,1024]{1,0:T(8,128)S(1)}, f32[16,1024]{1,0:T(8,128)S(1)}, u32[]{:S(2)}, u32[]{:S(2)}) collective-permute-start(f32[16,1024]{1,0:T(8,128)S(1)} %bitcast_select_fusion), channel_id=1, source_target_pairs={{0,30},{2,28},{4,26},{6,24},{8,22},{10,20},{12,18},{14,16},{16,14}... | collective-permute-start | bytes 196616 | tf_op jit(solution)/shard_map/ppermute | solution.py:145
  22.6 27.6 %all-to-all-start = ((f32[8,64,128]{2,1,0:T(8,128)}), f32[8,64,128]{2,1,0:T(8,128)S(1)}, u32[]{:S(2)}, u32[]{:S(2)}) async-start(f32[8,64,128]{2,1,0:T(8,128)} %bitcast.3), calls=%async_computation | async-start | bytes 524288 | tf_op jit(solution)/shard_map/all_to_all | solution.py:154
  33.8 3.1 %collective-permute-start.3 = (f32[16,1024]{1,0:T(8,128)S(1)}, f32[16,1024]{1,0:T(8,128)S(1)}, u32[]{:S(2)}, u32[]{:S(2)}) collective-permute-start(f32[16,1024]{1,0:T(8,128)S(1)} %collective-permute-done.2), channel_id=1, source_target_pairs={{0,1},{1,0},{2,3},{3,2},{4,5},{5,4},{6,7},{7,6},{8,9},{9,8},{10,11... | collective-permute-start | bytes 196616 | tf_op jit(solution)/shard_map/ppermute | solution.py:152
  37.0 9.9 %collective-permute-start.4 = (f32[2,16,1024]{2,1,0:T(8,128)S(1)}, f32[2,16,1024]{2,1,0:T(8,128)S(1)}, u32[]{:S(2)}, u32[]{:S(2)}) collective-permute-start(f32[2,16,1024]{2,1,0:T(8,128)S(1)} %pad_maximum_fusion.1), channel_id=1, source_target_pairs={{0,2},{2,0},{1,3},{3,1},{4,6},{6,4},{5,7},{7,5},{8,10},{10,8},{9,1... | collective-permute-start | bytes 393224 | tf_op jit(solution)/shard_map/ppermute | solution.py:153

commit v14 on v13

--- a/solution.py
+++ b/solution.py
@@ -149,8 +149,9 @@
     keep = product(((1, 0), (0, 0)), panel, solved, right_side.reshape(64, 128))
     passed = lax.ppermute(in_vmem(pass_kernel, (4, 64, 128), keep, moved), "b", swap)
     copies = in_vmem(spread_kernel, (4, 2, 64, 128), keep, moved, passed).reshape(8, 64, 128)
-    half = pair_up(core, quarter, lax.ppermute(quarter, "core", swap))
-    other = pair_up(b, half, lax.ppermute(half, "b", swap)).reshape(2, 32, 1024)
+    half = pair_up(b, quarter, lax.ppermute(quarter, "b", swap))
+    other = pair_up(core, half, lax.ppermute(half, "core", swap))
+    other = other.transpose(1, 0, 2, 3).reshape(2, 32, 1024)
     got_all = lax.all_to_all(copies, ("q", "zh"), 0, 0, tiled=True)
     got_all, other = lax.optimization_barrier((got_all, other))
     residual = got_all.reshape(4, 2, 2, 32, 128).sum(0)

time: 95.4 us -> 95.9 us (level)
  the two profiles are of different devices: /device:TPU:64 before, /device:TPU:32 now
where the time goes in v14:
time: 95.9 us; the launch traced here: 95.4 us
  blocking collectives  45.9 us (48%)
  starting transfers between devices  31.8 us (33%)
  waiting for transfers between devices  9.63 us (10%)
  Pallas kernels  6.67 us (7%)
  local copies, waits for them, and re-layouts  1.08 us (1%)
    all_to_all x3, blocking collectives, gather_plane(): return lax.all_to_all(copies, ('y', 'x'), 0, 0, tiled=True)  45.9 us
    all_to_all x1, starting transfers between devices, on_device(): got_all = lax.all_to_all(copies, ('q', 'zh'), 0, 0, tiled=True)  8.98 us
    ppermute x1, waiting for transfers between devices, on_device(): half = pair_up(b, quarter, lax.ppermute(quarter, 'b', swap))  8.31 us
    ppermute x1, starting transfers between devices, on_device(): lax.ppermute(in_vmem(pass_kernel, (4, 64, 128), keep, moved), 'b', swap)  7.52 us
    ppermute x1, starting transfers between devices, on_device(): lax.ppermute(quarter, ('zh',) + LINE, [(z, 15 - z) for z in range(16)])  6.93 us
    pallas_call x2, Pallas kernels, product(): pl.pallas_call(functools.partial(product_kernel, flips), out_shape=jax.Sh...  4.54 us
    ppermute x1, starting transfers between devices, on_device(): half = pair_up(b, quarter, lax.ppermute(quarter, 'b', swap))  4.53 us
    pallas_call x5, Pallas kernels, in_vmem(): pl.pallas_call(kernel, out_shape=jax.ShapeDtypeStruct(shape, jnp.float32)...  2.13 us
  transfers between devices with their start and end apart: 6, of which 2 were waited for; matrix products, arithmetic and copies ran while one was open for 0% of the time, Pallas kernels for 3%

profile of v14, /device:TPU:32, one launch (start us, length us, event | category | flops | bytes accessed | tf_op | source)
XLA Modules:
  0.0 95.4 jit_solution(2366961014616898994)
XLA Ops:
  0.0 0.9 copy-done.1
  0.9 0.0 copy-start.2
  0.9 0.0 copy-start.4
  0.9 0.0 slice-start
  0.9 0.0 copy-start.3
  0.9 2.3 %shard_map.56 = f32[2,4,64,128]{3,2,1,0:T(8,128)S(1)} custom-call(f32[64,512]{1,0:T(8,128)S(1)} %bitcast.22, f32[512,2048]{1,0:T(8,128)} %solved_ref.3), custom_call_target="tpu_custom_call" | custom-call | flops 200000000 | bytes 2097152 | tf_op jit(solution)/shard_map/pallas_call | solution.py:66
  3.2 1.9 %collective-permute-start = (f32[2,4,64,128]{3,2,1,0:T(8,128)S(1)}, f32[2,4,64,128]{3,2,1,0:T(8,128)S(1)}, u32[]{:S(2)}, u32[]{:S(2)}) collective-permute-start(f32[2,4,64,128]{3,2,1,0:T(8,128)S(1)} %shard_map.56), channel_id=1, source_target_pairs={{0,1},{1,0},{2,3},{3,2},{4,5},{5,4},{6,7},{7,6},{8,9},{9,8},{10,11... | collective-permute-start | bytes 786440 | tf_op jit(solution)/shard_map/ppermute | solution.py:148
  5.1 0.0 copy-done.2
  5.2 0.0 copy-done.4
  5.2 2.2 %shard_map.55.keep_ref = f32[2,4,64,128]{3,2,1,0:T(8,128)S(1)} custom-call(f32[64,512]{1,0:T(8,128)S(1)} %bitcast.23, f32[512,2048]{1,0:T(8,128)} %solved_ref.3, f32[64,128]{1,0:T(8,128)S(1)} %bitcast.26), custom_call_target="tpu_custom_call" | custom-call | flops 200000000 | bytes 2097152 | tf_op jit(solution)/shard_map/pallas_call | solution.py:66
  7.4 0.0 copy-start
  7.4 0.0 collective-permute-done.moved_ref
  7.5 7.5 %collective-permute-start.1 = (f32[4,64,128]{2,1,0:T(8,128)S(1)}, f32[4,64,128]{2,1,0:T(8,128)S(1)}, u32[]{:S(2)}, u32[]{:S(2)}) collective-permute-start(f32[4,64,128]{2,1,0:T(8,128)S(1)} %shard_map.57), channel_id=1, source_target_pairs={{0,2},{2,0},{1,3},{3,1},{4,6},{6,4},{5,7},{7,5},{8,10},{10,8},{9,1... | collective-permute-start | bytes 393224 | tf_op jit(solution)/shard_map/ppermute | solution.py:150
  15.0 0.0 slice-done
  15.0 0.0 copy-done.3
  15.0 6.9 %collective-permute-start.2 = (f32[16,1024]{1,0:T(8,128)S(1)}, f32[16,1024]{1,0:T(8,128)S(1)}, u32[]{:S(2)}, u32[]{:S(2)}) collective-permute-start(f32[16,1024]{1,0:T(8,128)S(1)} %bitcast_select_fusion), channel_id=1, source_target_pairs={{0,30},{2,28},{4,26},{6,24},{8,22},{10,20},{12,18},{14,16},{16,14}... | collective-permute-start | bytes 196616 | tf_op jit(solution)/shard_map/ppermute | solution.py:145
  22.0 0.0 collective-permute-done.1.passed_ref
  22.0 0.7 shard_map.58
  22.7 9.0 %all-to-all-start = ((f32[8,64,128]{2,1,0:T(8,128)}), f32[8,64,128]{2,1,0:T(8,128)S(1)}, u32[]{:S(2)}, u32[]{:S(2)}) async-start(f32[8,64,128]{2,1,0:T(8,128)} %bitcast.3), calls=%async_computation | async-start | bytes 524288 | tf_op jit(solution)/shard_map/all_to_all | solution.py:155
  31.7 0.0 collective-permute-done.2
  31.7 4.5 %collective-permute-start.3 = (f32[16,1024]{1,0:T(8,128)S(1)}, f32[16,1024]{1,0:T(8,128)S(1)}, u32[]{:S(2)}, u32[]{:S(2)}) collective-permute-start(f32[16,1024]{1,0:T(8,128)S(1)} %collective-permute-done.2), channel_id=1, source_target_pairs={{0,2},{2,0},{1,3},{3,1},{4,6},{6,4},{5,7},{7,5},{8,10},{10,8},{9,1... | collective-permute-start | bytes 196616 | tf_op jit(solution)/shard_map/ppermute | solution.py:152
  36.3 8.3 %collective-permute-done.3 = f32[16,1024]{1,0:T(8,128)S(1)} collective-permute-done((f32[16,1024]{1,0:T(8,128)S(1)}, f32[16,1024]{1,0:T(8,128)S(1)}, u32[]{:S(2)}, u32[]{:S(2)}) %collective-permute-start.3) | collective-permute-done | bytes 65568 | tf_op jit(solution)/shard_map/ppermute | solution.py:152
  44.6 1.9 %collective-permute-start.4 = (f32[2,16,1024]{2,1,0:T(8,128)S(1)}, f32[2,16,1024]{2,1,0:T(8,128)S(1)}, u32[]{:S(2)}, u32[]{:S(2)}) collective-permute-start(f32[2,16,1024]{2,1,0:T(8,128)S(1)} %pad_maximum_fusion), channel_id=1, source_target_pairs={{0,1},{1,0},{2,3},{3,2},{4,5},{5,4},{6,7},{7,6},{8,9},{9,8},{10,11... | collective-permute-start | bytes 393224 | tf_op jit(solution)/shard_map/ppermute | solution.py:153
  46.5 1.3 %collective-permute-done.4 = f32[2,16,1024]{2,1,0:T(8,128)S(1)} collective-permute-done((f32[2,16,1024]{2,1,0:T(8,128)S(1)}, f32[2,16,1024]{2,1,0:T(8,128)S(1)}, u32[]{:S(2)}, u32[]{:S(2)}) %collective-permute-start.4) | collective-permute-done | bytes 131104 | tf_op jit(solution)/shard_map/ppermute | solution.py:153
  47.9 0.0 all-to-all-done
  48.0 18.7 %all_to_all.20.x_ref = f32[16,64,128]{2,1,0:T(8,128)S(1)} all-to-all(f32[16,64,128]{2,1,0:T(8,128)S(1)} %broadcast_in_dim.24), channel_id=1, replica_groups=mesh['y'=4,'x'=4,'zh'=2,'q'=4,'b'=2,'core'=2] {'y','x'}, dimensions={0} | all-to-all | bytes 1048576 | tf_op jit(solution)/shard_map/all_to_all | solution.py:136
  66.7 0.0 copy-done
  66.7 0.3 shard_map.59.first_ref
  67.1 14.0 %all_to_all.21.x_ref = f32[16,64,128]{2,1,0:T(8,128)S(1)} all-to-all(f32[16,64,128]{2,1,0:T(8,128)S(1)} %broadcast_in_dim.25), channel_id=1, replica_groups=mesh['y'=4,'x'=4,'zh'=2,'q'=4,'b'=2,'core'=2] {'y','x'}, dimensions={0} | all-to-all | bytes 1048576 | tf_op jit(solution)/shard_map/all_to_all | solution.py:136
  81.0 0.3 shard_map.60
  81.4 13.2 %all_to_all.22.x_ref = f32[16,64,128]{2,1,0:T(8,128)S(1)} all-to-all(f32[16,64,128]{2,1,0:T(8,128)S(1)} %broadcast_in_dim.26), channel_id=1, replica_groups=mesh['y'=4,'x'=4,'zh'=2,'q'=4,'b'=2,'core'=2] {'y','x'}, dimensions={0} | all-to-all | bytes 1048576 | tf_op jit(solution)/shard_map/all_to_all | solution.py:136
  94.5 0.9 shard_map.61
  (13 shorter events, 0.3 us)
Async XLA Ops:
  0.0 0.9 copy-start.1
  0.9 4.2 %copy-start.2 = (f32[2,32,512]{2,1,0:T(8,128)S(1)}, f32[2,32,512]{2,1,0:T(8,128)}, u32[]{:S(2)}) copy-start(f32[2,32,512]{2,1,0:T(8,128)} %param.8) | copy-start | bytes 393220
  0.9 4.3 %copy-start.4 = (f32[2,32,128]{2,1,0:T(8,128)S(1)}, f32[2,32,128]{2,1,0:T(8,128)}, u32[]{:S(2)}) copy-start(f32[2,32,128]{2,1,0:T(8,128)} %param.5) | copy-start | bytes 98308
  0.9 14.1 %slice-start = ((f32[2,32,1024]{2,1,0:T(8,128)}), f32[1,32,1024]{2,1,0:T(8,128)S(1)}, s32[]{:S(2)}) async-start(f32[2,32,1024]{2,1,0:T(8,128)} %factor_ref.1), calls=%async_computation.4 | async-start | bytes 262144 | tf_op jit(solution)/shard_map/slice | solution.py:144
  0.9 14.1 %copy-start.3 = (f32[32,1024]{1,0:T(8,128)S(1)}, f32[32,1024]{1,0:T(8,128)}, u32[]{:S(2)}) copy-start(f32[32,1024]{1,0:T(8,128)} %param.7) | copy-start | bytes 393220
  3.2 4.2 %collective-permute-start = (f32[2,4,64,128]{3,2,1,0:T(8,128)S(1)}, f32[2,4,64,128]{3,2,1,0:T(8,128)S(1)}, u32[]{:S(2)}, u32[]{:S(2)}) collective-permute-start(f32[2,4,64,128]{3,2,1,0:T(8,128)S(1)} %shard_map.56), channel_id=1, source_target_pairs={{0,1},{1,0},{2,3},{3,2},{4,5},{5,4},{6,7},{7,6},{8,9},{9,8},{10,11... | collective-permute-start | bytes 786440 | tf_op jit(solution)/shard_map/ppermute | solution.py:148
  7.4 59.3 %copy-start = (f32[2,32,1024]{2,1,0:T(8,128)S(1)}, f32[2,32,1024]{2,1,0:T(8,128)}, u32[]{:S(2)}) copy-start(f32[2,32,1024]{2,1,0:T(8,128)} %factor_ref.1) | copy-start | bytes 786436
  7.5 14.5 %collective-permute-start.1 = (f32[4,64,128]{2,1,0:T(8,128)S(1)}, f32[4,64,128]{2,1,0:T(8,128)S(1)}, u32[]{:S(2)}, u32[]{:S(2)}) collective-permute-start(f32[4,64,128]{2,1,0:T(8,128)S(1)} %shard_map.57), channel_id=1, source_target_pairs={{0,2},{2,0},{1,3},{3,1},{4,6},{6,4},{5,7},{7,5},{8,10},{10,8},{9,1... | collective-permute-start | bytes 393224 | tf_op jit(solution)/shard_map/ppermute | solution.py:150
  15.0 16.7 %collective-permute-start.2 = (f32[16,1024]{1,0:T(8,128)S(1)}, f32[16,1024]{1,0:T(8,128)S(1)}, u32[]{:S(2)}, u32[]{:S(2)}) collective-permute-start(f32[16,1024]{1,0:T(8,128)S(1)} %bitcast_select_fusion), channel_id=1, source_target_pairs={{0,30},{2,28},{4,26},{6,24},{8,22},{10,20},{12,18},{14,16},{16,14}... | collective-permute-start | bytes 196616 | tf_op jit(solution)/shard_map/ppermute | solution.py:145
  22.7 25.2 %all-to-all-start = ((f32[8,64,128]{2,1,0:T(8,128)}), f32[8,64,128]{2,1,0:T(8,128)S(1)}, u32[]{:S(2)}, u32[]{:S(2)}) async-start(f32[8,64,128]{2,1,0:T(8,128)} %bitcast.3), calls=%async_computation | async-start | bytes 524288 | tf_op jit(solution)/shard_map/all_to_all | solution.py:155
  31.7 12.9 %collective-permute-start.3 = (f32[16,1024]{1,0:T(8,128)S(1)}, f32[16,1024]{1,0:T(8,128)S(1)}, u32[]{:S(2)}, u32[]{:S(2)}) collective-permute-start(f32[16,1024]{1,0:T(8,128)S(1)} %collective-permute-done.2), channel_id=1, source_target_pairs={{0,2},{2,0},{1,3},{3,1},{4,6},{6,4},{5,7},{7,5},{8,10},{10,8},{9,1... | collective-permute-start | bytes 196616 | tf_op jit(solution)/shard_map/ppermute | solution.py:152
  44.6 3.2 %collective-permute-start.4 = (f32[2,16,1024]{2,1,0:T(8,128)S(1)}, f32[2,16,1024]{2,1,0:T(8,128)S(1)}, u32[]{:S(2)}, u32[]{:S(2)}) collective-permute-start(f32[2,16,1024]{2,1,0:T(8,128)S(1)} %pad_maximum_fusion), channel_id=1, source_target_pairs={{0,1},{1,0},{2,3},{3,2},{4,5},{5,4},{6,7},{7,6},{8,9},{9,8},{10,11... | collective-permute-start | bytes 393224 | tf_op jit(solution)/shard_map/ppermute | solution.py:153

commit v15 on v13

--- a/solution.py
+++ b/solution.py
@@ -80,6 +80,14 @@
     )(*args)
 
 
+def sum_kernel(got_ref, first_ref, second_ref):
+    total = got_ref[0]
+    for q in range(1, 4):
+        total = total + got_ref[q]
+    first_ref[...] = jnp.concatenate([total[0, 0], total[1, 0]], axis=0)
+    second_ref[...] = jnp.concatenate([total[0, 1], total[1, 1]], axis=0)
+
+
 def pass_kernel(keep_ref, moved_ref, out_ref):
     out_ref[...] = keep_ref[0] + moved_ref[0]
 
@@ -153,10 +161,14 @@
     other = pair_up(b, half, lax.ppermute(half, "b", swap)).reshape(2, 32, 1024)
     got_all = lax.all_to_all(copies, ("q", "zh"), 0, 0, tiled=True)
     got_all, other = lax.optimization_barrier((got_all, other))
-    residual = got_all.reshape(4, 2, 2, 32, 128).sum(0)
-    first_res = residual[:, 0].reshape(64, 128)
-    second_part = residual[:, 1].reshape(64, 128)
-
+    vmem = pl.BlockSpec(memory_space=pltpu.VMEM)
+    first_res, second_part = pl.pallas_call(
+        sum_kernel,
+        out_shape=(jax.ShapeDtypeStruct((64, 128), jnp.float32),) * 2,
+        in_specs=[vmem],
+        out_specs=(vmem, vmem),
+        compiler_params=pltpu.CompilerParams(vmem_limit_bytes=8 << 20),
+    )(got_all.reshape(4, 2, 2, 32, 128))
     first_rows, second_rows = (functools.partial(rows_kernel, step) for step in range(2))
     first_sol = in_vmem(first_rows, (64, 128), diag_inverse, other, gather_plane(first_res))
     second_res = in_vmem(

time: 95.4 us -> 95.4 us (level)
  no operation moved by 1% of the time
where the time goes in v15:
time: 95.4 us; the launch traced here: 94.9 us
  blocking collectives  43.1 us (45%)
  starting transfers between devices  31.2 us (33%)
  waiting for transfers between devices  12.5 us (13%)
  Pallas kernels  6.72 us (7%)
  local copies, waits for them, and re-layouts  1.06 us (1%)
    all_to_all x3, blocking collectives, gather_plane(): return lax.all_to_all(copies, ('y', 'x'), 0, 0, tiled=True)  43.1 us
    all_to_all x1, starting transfers between devices, on_device(): got_all = lax.all_to_all(copies, ('q', 'zh'), 0, 0, tiled=True)  11.2 us
    ppermute x1, starting transfers between devices, on_device(): lax.ppermute(quarter, ('zh',) + LINE, [(z, 15 - z) for z in range(16)])  10.5 us
    ppermute x1, waiting for transfers between devices, on_device(): other = pair_up(b, half, lax.ppermute(half, 'b', swap)).reshape(2, 32, 1024)  8 us
    pallas_call x2, Pallas kernels, product(): pl.pallas_call(functools.partial(product_kernel, flips), out_shape=jax.Sh...  4.58 us
    ppermute x1, starting transfers between devices, on_device(): lax.ppermute(in_vmem(pass_kernel, (4, 64, 128), keep, moved), 'b', swap)  3.82 us
    all_to_all x1, waiting for transfers between devices, on_device(): got_all = lax.all_to_all(copies, ('q', 'zh'), 0, 0, tiled=True)  3.23 us
    pallas_call x5, Pallas kernels, in_vmem(): pl.pallas_call(kernel, out_shape=jax.ShapeDtypeStruct(shape, jnp.float32)...  2.12 us
  transfers between devices with their start and end apart: 6, of which 3 were waited for; matrix products, arithmetic and copies ran while one was open for 0% of the time, Pallas kernels for 3%

profile of v15, /device:TPU:64, one launch (start us, length us, event | category | flops | bytes accessed | tf_op | source)
XLA Modules:
  0.0 94.9 jit_solution(3923380040937551444)
XLA Ops:
  0.0 0.0 copy-start.1
  0.0 0.9 copy-done.1
  0.9 0.0 copy-start.2
  0.9 0.0 copy-start.4
  0.9 0.0 slice-start
  0.9 2.3 %shard_map.56 = f32[2,4,64,128]{3,2,1,0:T(8,128)S(1)} custom-call(f32[64,512]{1,0:T(8,128)S(1)} %bitcast.14, f32[512,2048]{1,0:T(8,128)} %solved_ref.3), custom_call_target="tpu_custom_call" | custom-call | flops 200000000 | bytes 2097152 | tf_op jit(solution)/shard_map/pallas_call | solution.py:66
  3.2 1.9 %collective-permute-start = (f32[2,4,64,128]{3,2,1,0:T(8,128)S(1)}, f32[2,4,64,128]{3,2,1,0:T(8,128)S(1)}, u32[]{:S(2)}, u32[]{:S(2)}) collective-permute-start(f32[2,4,64,128]{3,2,1,0:T(8,128)S(1)} %shard_map.56), channel_id=1, source_target_pairs={{0,1},{1,0},{2,3},{3,2},{4,5},{5,4},{6,7},{7,6},{8,9},{9,8},{10,11... | collective-permute-start | bytes 786440 | tf_op jit(solution)/shard_map/ppermute | solution.py:156
  5.2 0.0 copy-done.2
  5.2 0.0 copy-done.4
  5.2 0.0 copy-start
  5.2 2.3 %shard_map.55.keep_ref = f32[2,4,64,128]{3,2,1,0:T(8,128)S(1)} custom-call(f32[64,512]{1,0:T(8,128)S(1)} %bitcast.15, f32[512,2048]{1,0:T(8,128)} %solved_ref.3, f32[64,128]{1,0:T(8,128)S(1)} %bitcast.17), custom_call_target="tpu_custom_call" | custom-call | flops 200000000 | bytes 2097152 | tf_op jit(solution)/shard_map/pallas_call | solution.py:66
  7.5 0.0 collective-permute-done.moved_ref
  7.5 3.8 %collective-permute-start.1 = (f32[4,64,128]{2,1,0:T(8,128)S(1)}, f32[4,64,128]{2,1,0:T(8,128)S(1)}, u32[]{:S(2)}, u32[]{:S(2)}) collective-permute-start(f32[4,64,128]{2,1,0:T(8,128)S(1)} %shard_map.57), channel_id=1, source_target_pairs={{0,2},{2,0},{1,3},{3,1},{4,6},{6,4},{5,7},{7,5},{8,10},{10,8},{9,1... | collective-permute-start | bytes 393224 | tf_op jit(solution)/shard_map/ppermute | solution.py:158
  11.3 0.0 slice-done
  11.4 0.0 copy-done.3
  11.4 10.5 %collective-permute-start.2 = (f32[16,1024]{1,0:T(8,128)S(1)}, f32[16,1024]{1,0:T(8,128)S(1)}, u32[]{:S(2)}, u32[]{:S(2)}) collective-permute-start(f32[16,1024]{1,0:T(8,128)S(1)} %bitcast_select_fusion), channel_id=1, source_target_pairs={{0,30},{2,28},{4,26},{6,24},{8,22},{10,20},{12,18},{14,16},{16,14}... | collective-permute-start | bytes 196616 | tf_op jit(solution)/shard_map/ppermute | solution.py:153
  21.9 0.0 collective-permute-done.1.passed_ref
  21.9 0.7 shard_map.58
  22.6 11.2 %all-to-all-start = ((f32[8,64,128]{2,1,0:T(8,128)}), f32[8,64,128]{2,1,0:T(8,128)S(1)}, u32[]{:S(2)}, u32[]{:S(2)}) async-start(f32[8,64,128]{2,1,0:T(8,128)} %bitcast.3), calls=%async_computation | async-start | bytes 524288 | tf_op jit(solution)/shard_map/all_to_all | solution.py:162
  33.8 0.0 collective-permute-done.2
  33.8 1.9 %collective-permute-start.3 = (f32[16,1024]{1,0:T(8,128)S(1)}, f32[16,1024]{1,0:T(8,128)S(1)}, u32[]{:S(2)}, u32[]{:S(2)}) collective-permute-start(f32[16,1024]{1,0:T(8,128)S(1)} %collective-permute-done.2), channel_id=1, source_target_pairs={{0,1},{1,0},{2,3},{3,2},{4,5},{5,4},{6,7},{7,6},{8,9},{9,8},{10,11... | collective-permute-start | bytes 196616 | tf_op jit(solution)/shard_map/ppermute | solution.py:160
  35.7 1.2 %collective-permute-done.3 = f32[16,1024]{1,0:T(8,128)S(1)} collective-permute-done((f32[16,1024]{1,0:T(8,128)S(1)}, f32[16,1024]{1,0:T(8,128)S(1)}, u32[]{:S(2)}, u32[]{:S(2)}) %collective-permute-start.3) | collective-permute-done | bytes 65568 | tf_op jit(solution)/shard_map/ppermute | solution.py:160
  36.9 1.9 %collective-permute-start.4 = (f32[2,16,1024]{2,1,0:T(8,128)S(1)}, f32[2,16,1024]{2,1,0:T(8,128)S(1)}, u32[]{:S(2)}, u32[]{:S(2)}) collective-permute-start(f32[2,16,1024]{2,1,0:T(8,128)S(1)} %pad_maximum_fusion.1), channel_id=1, source_target_pairs={{0,2},{2,0},{1,3},{3,1},{4,6},{6,4},{5,7},{7,5},{8,10},{10,8},{9,1... | collective-permute-start | bytes 393224 | tf_op jit(solution)/shard_map/ppermute | solution.py:161
  38.9 8.0 %collective-permute-done.4 = f32[2,16,1024]{2,1,0:T(8,128)S(1)} collective-permute-done((f32[2,16,1024]{2,1,0:T(8,128)S(1)}, f32[2,16,1024]{2,1,0:T(8,128)S(1)}, u32[]{:S(2)}, u32[]{:S(2)}) %collective-permute-start.4) | collective-permute-done | bytes 131104 | tf_op jit(solution)/shard_map/ppermute | solution.py:161
  46.9 3.2 %all-to-all-done = f32[8,64,128]{2,1,0:T(8,128)S(1)} async-done(((f32[8,64,128]{2,1,0:T(8,128)}), f32[8,64,128]{2,1,0:T(8,128)S(1)}, u32[]{:S(2)}, u32[]{:S(2)}) %all-to-all-start) | async-done | bytes 262176 | tf_op jit(solution)/shard_map/all_to_all | solution.py:162
  50.2 16.9 %all_to_all.20.x_ref = f32[16,64,128]{2,1,0:T(8,128)S(1)} all-to-all(f32[16,64,128]{2,1,0:T(8,128)S(1)} %broadcast_in_dim.9), channel_id=1, replica_groups=mesh['y'=4,'x'=4,'zh'=2,'q'=4,'b'=2,'core'=2] {'y','x'}, dimensions={0} | all-to-all | bytes 1048576 | tf_op jit(solution)/shard_map/all_to_all | solution.py:144
  67.2 0.0 copy-done
  67.2 0.3 shard_map.60.first_ref
  67.5 13.1 %all_to_all.21.x_ref = f32[16,64,128]{2,1,0:T(8,128)S(1)} all-to-all(f32[16,64,128]{2,1,0:T(8,128)S(1)} %broadcast_in_dim.10), channel_id=1, replica_groups=mesh['y'=4,'x'=4,'zh'=2,'q'=4,'b'=2,'core'=2] {'y','x'}, dimensions={0} | all-to-all | bytes 1048576 | tf_op jit(solution)/shard_map/all_to_all | solution.py:144
  80.6 0.3 shard_map.61
  80.9 13.1 %all_to_all.22.x_ref = f32[16,64,128]{2,1,0:T(8,128)S(1)} all-to-all(f32[16,64,128]{2,1,0:T(8,128)S(1)} %broadcast_in_dim.11), channel_id=1, replica_groups=mesh['y'=4,'x'=4,'zh'=2,'q'=4,'b'=2,'core'=2] {'y','x'}, dimensions={0} | all-to-all | bytes 1048576 | tf_op jit(solution)/shard_map/all_to_all | solution.py:144
  94.0 0.9 shard_map.62
  (11 shorter events, 0.3 us)
Async XLA Ops:
  0.0 0.9 copy-start.1
  0.9 4.2 %copy-start.2 = (f32[2,32,512]{2,1,0:T(8,128)S(1)}, f32[2,32,512]{2,1,0:T(8,128)}, u32[]{:S(2)}) copy-start(f32[2,32,512]{2,1,0:T(8,128)} %param.8) | copy-start | bytes 393220
  0.9 4.3 %copy-start.4 = (f32[2,32,128]{2,1,0:T(8,128)S(1)}, f32[2,32,128]{2,1,0:T(8,128)}, u32[]{:S(2)}) copy-start(f32[2,32,128]{2,1,0:T(8,128)} %param.5) | copy-start | bytes 98308
  0.9 10.4 %slice-start = ((f32[2,32,1024]{2,1,0:T(8,128)}), f32[1,32,1024]{2,1,0:T(8,128)S(1)}, s32[]{:S(2)}) async-start(f32[2,32,1024]{2,1,0:T(8,128)} %factor_ref.1), calls=%async_computation.4 | async-start | bytes 262144 | tf_op jit(solution)/shard_map/slice | solution.py:152
  0.9 10.4 %copy-start.3 = (f32[32,1024]{1,0:T(8,128)S(1)}, f32[32,1024]{1,0:T(8,128)}, u32[]{:S(2)}) copy-start(f32[32,1024]{1,0:T(8,128)} %param.7) | copy-start | bytes 393220
  3.2 4.3 %collective-permute-start = (f32[2,4,64,128]{3,2,1,0:T(8,128)S(1)}, f32[2,4,64,128]{3,2,1,0:T(8,128)S(1)}, u32[]{:S(2)}, u32[]{:S(2)}) collective-permute-start(f32[2,4,64,128]{3,2,1,0:T(8,128)S(1)} %shard_map.56), channel_id=1, source_target_pairs={{0,1},{1,0},{2,3},{3,2},{4,5},{5,4},{6,7},{7,6},{8,9},{9,8},{10,11... | collective-permute-start | bytes 786440 | tf_op jit(solution)/shard_map/ppermute | solution.py:156
  5.2 62.0 %copy-start = (f32[2,32,1024]{2,1,0:T(8,128)S(1)}, f32[2,32,1024]{2,1,0:T(8,128)}, u32[]{:S(2)}) copy-start(f32[2,32,1024]{2,1,0:T(8,128)} %factor_ref.1) | copy-start | bytes 786436
  7.5 14.4 %collective-permute-start.1 = (f32[4,64,128]{2,1,0:T(8,128)S(1)}, f32[4,64,128]{2,1,0:T(8,128)S(1)}, u32[]{:S(2)}, u32[]{:S(2)}) collective-permute-start(f32[4,64,128]{2,1,0:T(8,128)S(1)} %shard_map.57), channel_id=1, source_target_pairs={{0,2},{2,0},{1,3},{3,1},{4,6},{6,4},{5,7},{7,5},{8,10},{10,8},{9,1... | collective-permute-start | bytes 393224 | tf_op jit(solution)/shard_map/ppermute | solution.py:158
  11.4 22.4 %collective-permute-start.2 = (f32[16,1024]{1,0:T(8,128)S(1)}, f32[16,1024]{1,0:T(8,128)S(1)}, u32[]{:S(2)}, u32[]{:S(2)}) collective-permute-start(f32[16,1024]{1,0:T(8,128)S(1)} %bitcast_select_fusion), channel_id=1, source_target_pairs={{0,30},{2,28},{4,26},{6,24},{8,22},{10,20},{12,18},{14,16},{16,14}... | collective-permute-start | bytes 196616 | tf_op jit(solution)/shard_map/ppermute | solution.py:153
  22.6 27.6 %all-to-all-start = ((f32[8,64,128]{2,1,0:T(8,128)}), f32[8,64,128]{2,1,0:T(8,128)S(1)}, u32[]{:S(2)}, u32[]{:S(2)}) async-start(f32[8,64,128]{2,1,0:T(8,128)} %bitcast.3), calls=%async_computation | async-start | bytes 524288 | tf_op jit(solution)/shard_map/all_to_all | solution.py:162
  33.8 3.1 %collective-permute-start.3 = (f32[16,1024]{1,0:T(8,128)S(1)}, f32[16,1024]{1,0:T(8,128)S(1)}, u32[]{:S(2)}, u32[]{:S(2)}) collective-permute-start(f32[16,1024]{1,0:T(8,128)S(1)} %collective-permute-done.2), channel_id=1, source_target_pairs={{0,1},{1,0},{2,3},{3,2},{4,5},{5,4},{6,7},{7,6},{8,9},{9,8},{10,11... | collective-permute-start | bytes 196616 | tf_op jit(solution)/shard_map/ppermute | solution.py:160
  36.9 9.9 %collective-permute-start.4 = (f32[2,16,1024]{2,1,0:T(8,128)S(1)}, f32[2,16,1024]{2,1,0:T(8,128)S(1)}, u32[]{:S(2)}, u32[]{:S(2)}) collective-permute-start(f32[2,16,1024]{2,1,0:T(8,128)S(1)} %pad_maximum_fusion.1), channel_id=1, source_target_pairs={{0,2},{2,0},{1,3},{3,1},{4,6},{6,4},{5,7},{7,5},{8,10},{10,8},{9,1... | collective-permute-start | bytes 393224 | tf_op jit(solution)/shard_map/ppermute | solution.py:161
